TPU v7x, 128 devices: a whole 4x4x4 slice. The times are simulated.
128 devices in a mesh: dp: 8 (over y, z_hi), seq: 16 (over z_lo, x, core).
Axes of the slice: x: 4, y: 4, z: 4 (z_hi: 2, z_lo: 2; z = z_hi * 2 + z_lo), core: 2. Of those that a mesh axis runs over, the one named last changes fastest.
Arguments:
- frames: bfloat16 [8, 256, 256, 1280], P('dp', 'seq'), may hold values from -6 to 6
- map_weight: bfloat16 [1280, 8], replicated, may hold values from -0.15625 to 0.15625
- qkv_weight: bfloat16 [1280, 3840], replicated, may hold values from -8 to 8, as said below
- cotangent: bfloat16 [8, 2048, 1280], P('dp', 'seq'), may hold values from -6 to 6
Outputs:
- grad_qkv_weight: float32 [1280, 3840], P(None, 'seq')
Inputs may be any that keep to these rules, and one draw needn't show every extreme that they name: qkv_weight has mean zero and entries of order 1280 ** -0.5 times at most 40.
All inputs are finite; a program needn't handle non-finite values.
Results may differ from a plain program's by a relative error of at most 0.019.
Values may be sent and summed in bfloat16 or wider, within the bound.
No kernel may reach another device: no remote copies, remote signals or barrier semaphores. Data moves between devices by JAX's collectives and lax.ppermute only.
A program may use at most 128 MiB of HBM per device.

v0:
```python
import math

import jax
import jax.numpy as jnp
from jax import lax
from jax.sharding import PartitionSpec as P

HEAD_DIM = 80


def as_sent(array):
    return jax.tree.map(lambda a: a.astype(jnp.bfloat16) if a.dtype == jnp.float32 else a, array)


def learn_tokens(frames, map_weight):
    frame_count = frames.shape[0]
    width_all = frames.shape[2]
    logits = jnp.dot(frames.reshape(-1, width_all), map_weight, preferred_element_type=jnp.float32)
    token_maps = (
        jax.nn.sigmoid(logits).astype(jnp.bfloat16).reshape(frame_count, frames.shape[1], -1)
    )
    pooled = jnp.einsum("fps,fpd->fsd", token_maps, frames, preferred_element_type=jnp.float32)
    pooled = pooled.reshape(-1, width_all)
    centred = pooled - jnp.mean(pooled, axis=-1, keepdims=True)
    variance = jnp.mean(centred * centred, axis=-1, keepdims=True)
    return (centred * lax.rsqrt(variance + 1e-06)).astype(jnp.bfloat16)


def one_head(query_rows, key_rows, value_rows, upstream):
    length = query_rows.shape[0]
    block_rows = math.gcd(length, 512)
    block_count = length // block_rows
    scaling = 1.0 / math.sqrt(HEAD_DIM)

    def advance(totals, position):
        key_total, value_total = totals
        query_block = lax.dynamic_slice_in_dim(query_rows, position * block_rows, block_rows, 0)
        grad_block = lax.dynamic_slice_in_dim(upstream, position * block_rows, block_rows, 0)
        scores = (
            jnp.einsum("qd,kd->qk", query_block, key_rows, preferred_element_type=jnp.float32)
            * scaling
        )
        shifted = jnp.exp(scores - jnp.max(scores, axis=-1, keepdims=True))
        attention = shifted / jnp.sum(shifted, axis=-1, keepdims=True)
        rounded = attention.astype(jnp.bfloat16)
        attended = jnp.dot(rounded, value_rows, preferred_element_type=jnp.float32)
        row_dot = jnp.sum(grad_block.astype(jnp.float32) * attended, axis=-1, keepdims=True)
        grad_attention = jnp.einsum(
            "qd,kd->qk", grad_block, value_rows, preferred_element_type=jnp.float32
        )
        grad_scores = (attention * (grad_attention - row_dot) * scaling).astype(jnp.bfloat16)
        grad_query = jnp.dot(grad_scores, key_rows, preferred_element_type=jnp.float32).astype(
            jnp.bfloat16
        )
        key_total = key_total + jnp.einsum(
            "qk,qd->kd", grad_scores, query_block, preferred_element_type=jnp.float32
        )
        value_total = value_total + jnp.einsum(
            "qk,qd->kd", rounded, grad_block, preferred_element_type=jnp.float32
        )
        return ((key_total, value_total), grad_query)

    empty_rows = jnp.zeros((length, HEAD_DIM), jnp.float32)
    totals, grad_query = lax.scan(advance, (empty_rows, empty_rows), jnp.arange(block_count))
    grad_query = grad_query.reshape(length, HEAD_DIM)
    return jnp.concatenate(
        [grad_query, totals[0].astype(jnp.bfloat16), totals[1].astype(jnp.bfloat16)], axis=1
    )


def heads_backward(projected, upstream):
    query_rows = projected[:, 0:HEAD_DIM]
    key_rows = projected[:, HEAD_DIM : 2 * HEAD_DIM]
    value_rows = projected[:, 2 * HEAD_DIM : 3 * HEAD_DIM]
    pieces = [one_head(query_rows, key_rows, value_rows, upstream)]
    return jnp.concatenate(pieces, axis=1)


def heads_items(operands):
    return jax.vmap(heads_backward)(operands[0], operands[1])


def body(frames, map_weight, qkv_weight, cotangent):
    normed = learn_tokens(frames[0], map_weight)
    projected = jnp.dot(normed, qkv_weight, preferred_element_type=jnp.float32).astype(jnp.bfloat16)
    grads_heads = heads_items(
        (
            lax.all_to_all(projected[None], "seq", split_axis=2, concat_axis=1, tiled=True),
            lax.all_to_all(cotangent, "seq", split_axis=2, concat_axis=1, tiled=True),
        )
    )
    grads = lax.all_to_all(
        as_sent(grads_heads), "seq", split_axis=1, concat_axis=2, tiled=True
    ).astype(grads_heads.dtype)
    partial_value = jnp.einsum("td,tc->dc", normed, grads[0], preferred_element_type=jnp.float32)
    shares = lax.psum_scatter(partial_value, "seq", scatter_dimension=1, tiled=True)
    grad_weight = lax.psum(shares, "dp")
    return grad_weight


def solution(mesh):
    placed = (P("dp", "seq", None, None), P(), P(), P("dp", "seq", None))
    return jax.shard_map(
        body, mesh=mesh, in_specs=placed, out_specs=P(None, "seq"), check_vma=False
    )
```

profile of v0, /device:TPU:0, one launch (start us, length us, event | category | flops | bytes accessed | tf_op | source)
XLA Modules:
  0.0 412.4 jit_solution(12583312983164715362)
XLA Ops:
  6.5 1.4 copy.31
  8.5 7.5 %reduce.9 = bf16[1280,128]{1,0:T(8,128)(2,1)S(1)} reduce(bf16[1280,1,128]{2,1,0:T(2,128)(2,1)S(1)} %bitcast.145, bf16[]{:T(256)} %broadcast.113), dimensions={1}, to_apply=%bitcast.76.reduce_sub_computation | reduce | bytes 655362
  16.8 5.8 %all-to-all-start.1 = ((bf16[16,2,5120]{2,1,0:T(2,128)(2,1)}), bf16[16,2,5120]{2,1,0:T(2,128)(2,1)S(1)}, u32[]{:S(2)}, u32[]{:S(2)}) async-start(bf16[16,2,5120]{2,1,0:T(2,128)(2,1)} %reshape.172), calls=%async_computation.1 | async-start | bytes 655360 | tf_op jit(solution)/shard_map/all_to_all | solution.py:89
  22.7 6.9 %fusion.32 = bf16[4096,8]{0,1:T(8,128)(2,1)S(1)} fusion(bf16[4096,1280]{1,0:T(8,128)(2,1)} %bitcast.134, bf16[1280,8]{0,1:T(8,128)(2,1)S(1)} %copy-done), kind=kOutput, calls=%fused_computation.42 | convolution fusion | flops 84017152 | bytes 10571776 | tf_op jit(solution)/shard_map/dot_general | solution.py:18
  29.6 1.5 fusion.44
  31.6 6.3 %fusion.28 = bf16[1,128,3840]{2,1,0:T(8,128)(2,1)} fusion(bf16[1280,3840]{1,0:T(8,128)(2,1)} %param.8, f32[16,8,1280]{2,1,0:T(8,128)S(1)} %get-tuple-element.160, f32[128]{0:T(128)S(1)} %rsqrt.13, f32[128]{0:T(128)S(1)} %div.23), kind=kOutput, calls=%fused_computation.37 | convolution fusion | flops 1259274240 | bytes 11469824 | tf_op jit(solution)/shard_map/dot_general | solution.py:85
  37.9 3.7 copy.29
  41.5 22.0 %reduce.8 = bf16[3840,128]{1,0:T(8,128)(2,1)} reduce(bf16[3840,1,128]{2,1,0:T(2,128)(2,1)S(1)} %bitcast.137, bf16[]{:T(256)} %broadcast.113), dimensions={1}, to_apply=%bitcast.74.reduce_sub_computation | reduce | bytes 1966082
  63.5 3.1 reshape.170
  67.4 5.7 %all-to-all-start = ((bf16[16,2,15360]{2,1,0:T(2,128)(2,1)}), bf16[16,2,15360]{2,1,0:T(2,128)(2,1)S(1)}, u32[]{:S(2)}, u32[]{:S(2)}) async-start(bf16[16,2,15360]{2,1,0:T(2,128)(2,1)} %reshape.170), calls=%async_computation | async-start | bytes 1966080 | tf_op jit(solution)/shard_map/all_to_all | solution.py:88
  73.4 3.2 reshape.173
  76.7 1.1 copy.43
  77.9 11.0 %all-to-all-done = bf16[16,2,15360]{2,1,0:T(2,128)(2,1)S(1)} async-done(((bf16[16,2,15360]{2,1,0:T(2,128)(2,1)}), bf16[16,2,15360]{2,1,0:T(2,128)(2,1)S(1)}, u32[]{:S(2)}, u32[]{:S(2)}) %all-to-all-start) | async-done | bytes 983072 | tf_op jit(solution)/shard_map/all_to_all | solution.py:88
  88.9 3.2 reshape.171
  92.1 1.7 copy.42
  94.1 0.9 fusion.43
  95.3 1.2 copy.34
  96.5 42.3 %while.17 = (s32[]{:T(128)}, f32[1,2048,80]{1,2,0:T(8,128)S(1)}, f32[1,2048,80]{1,2,0:T(8,128)S(1)}, bf16[4,1,512,80]{2,3,1,0:T(8,128)(2,1)}, s32[4]{0:T(128)S(1...) while((s32[]{:T(128)}, f32[1,2048,80]{1,2,0:T(8,128)S(1)}, ...), condition=%wide.region_6.7_spmd.clone, body=%wide.region_2.6_spmd.clone.sunk | while | flops 1022130688 | bytes 40287472 | solution.py:64
  97.9 1.9 multiply_reduce_fusion.3
  100.6 0.8 fusion.79
  102.9 1.2 multiply_convert_fusion.3
  104.1 1.4 fusion.83
  105.6 1.5 fusion.81
  108.4 1.9 multiply_reduce_fusion.3
  113.4 1.3 multiply_convert_fusion.3
  114.7 1.4 fusion.83
  116.1 1.5 fusion.81
  119.0 1.9 multiply_reduce_fusion.3
  124.0 1.2 multiply_convert_fusion.3
  125.3 1.4 fusion.83
  126.7 1.5 fusion.81
  129.6 1.9 multiply_reduce_fusion.3
  134.6 1.3 multiply_convert_fusion.3
  135.8 1.4 fusion.83
  137.3 1.5 fusion.81
  138.8 1.0 copy.47
  139.9 1.0 pad_maximum_fusion
  140.9 4.6 %copy.37 = bf16[1,2048,240]{2,0,1:T(2,128)(2,1)S(1)} copy(bf16[1,2048,240]{1,2,0:T(8,128)(2,1)} %pad_maximum_fusion) | data formatting | bytes 1966080 | tf_op jit(solution)/shard_map/vmap()/concatenate | solution.py:66
  145.5 12.6 %reduce.10 = bf16[2048,240]{1,0:T(8,128)(2,1)} reduce(bf16[2048,1,240]{2,1,0:T(2,128)(2,1)S(1)} %bitcast.136, bf16[]{:T(256)} %broadcast.113), dimensions={1}, to_apply=%bitcast.78.reduce_sub_computation | reduce | bytes 1966082
  158.2 3.8 reshape.174
  161.9 19.1 %all_to_all.51 = bf16[16,2,15360]{2,1,0:T(2,128)(2,1)} all-to-all(bf16[16,2,15360]{2,1,0:T(2,128)(2,1)S(1)} %reshape.174), channel_id=1, replica_groups=mesh['dp'=8,'seq'=16] {'seq'}, dimensions={0} | all-to-all | bytes 1966080 | tf_op jit(solution)/shard_map/all_to_all | solution.py:92
  181.0 6.0 %reshape.175 = bf16[2048,1,240]{2,1,0:T(2,128)(2,1)S(1)} reshape(bf16[16,2,15360]{2,1,0:T(2,128)(2,1)} %all_to_all.51) | data formatting | bytes 1966080
  187.0 1.2 copy.44
  188.1 1.7 copy.40
  190.1 8.3 %fusion.36 = f32[1280,3840]{0,1:T(8,128)} fusion(bf16[128,3840]{0,1:T(8,128)(2,1)S(1)} %bitcast.140, f32[16,8,1280]{2,1,0:T(8,128)S(1)} %get-tuple-element.160, f32[16,8]{1,0:T(8,128)S(1)} %add_rsqrt_fusion, f32[16,8]{1,0:T(8,128)S(1)} %broadcast_multiply_fusion), kind=kOutput, calls=%fused_computation.51 | convolution fusion | flops 1258782720 | bytes 21300224 | tf_op jit(solution)/shard_map/td,tc->dc/dot_general | solution.py:95
  198.5 112.5 %reduce-scatter.2.cloned.1.call-done = f32[1280,240]{0,1:T(8,128)} async-done(((f32[1280,3840]{0,1:T(8,128)}), f32[1280,240]{0,1:T(8,128)}) %reduce-scatter.2.cloned.1.call-update) | async-done | bytes 1228816 | tf_op jit(solution)/shard_map/reduce_scatter | solution.py:96
  311.0 92.2 %all-reduce.2.cloned.1.call-done = f32[1280,240]{0,1:T(8,128)} async-done(((f32[1280,240]{0,1:T(8,128)}), f32[1280,240]{0,1:T(8,128)}) %all-reduce.2.cloned.1.call-update) | async-done | bytes 1228816 | tf_op jit(solution)/shard_map/psum | solution.py:97
  403.2 2.4 copy.66
  (53 shorter events, 18.1 us)
Async XLA Ops:
  6.5 16.1 %copy-start = (bf16[1280,8]{0,1:T(8,128)(2,1)S(1)}, bf16[1280,8]{0,1:T(8,128)(2,1)}, u32[]{:S(2)}) copy-start(bf16[1280,8]{0,1:T(8,128)(2,1)} %param.7) | copy-start | bytes 61444
  16.8 49.9 %all-to-all-start.1 = ((bf16[16,2,5120]{2,1,0:T(2,128)(2,1)}), bf16[16,2,5120]{2,1,0:T(2,128)(2,1)S(1)}, u32[]{:S(2)}, u32[]{:S(2)}) async-start(bf16[16,2,5120]{2,1,0:T(2,128)(2,1)} %reshape.172), calls=%async_computation.1 | async-start | bytes 655360 | tf_op jit(solution)/shard_map/all_to_all | solution.py:89
  22.7 7.0 %copy-start.2 = (bf16[1,16,256,1280]{3,2,1,0:T(8,128)(2,1)S(1)}, bf16[1,16,256,1280]{3,2,1,0:T(8,128)(2,1)}, u32[]{:S(2)}) copy-start(bf16[1,16,256,1280]{3,2,1,0:T(8,128)(2,1)} %param.6) | copy-start | bytes 31457284
  66.7 0.7 copy-start.3
  67.4 21.5 %all-to-all-start = ((bf16[16,2,15360]{2,1,0:T(2,128)(2,1)}), bf16[16,2,15360]{2,1,0:T(2,128)(2,1)S(1)}, u32[]{:S(2)}, u32[]{:S(2)}) async-start(bf16[16,2,15360]{2,1,0:T(2,128)(2,1)} %reshape.170), calls=%async_computation | async-start | bytes 1966080 | tf_op jit(solution)/shard_map/all_to_all | solution.py:88
  73.1 237.8 %reduce-scatter.2.cloned.1.call-start = ((), (), s32[]{:S(2)}) async-start(), calls=%async_computation.4 | async-start | bytes 20889600 | tf_op jit(solution)/shard_map/reduce_scatter | solution.py:96
  198.4 207.2 %copy-start.1 = (bf16[1280,8]{0,1:T(8,128)(2,1)S(1)}, bf16[1280,8]{0,1:T(8,128)(2,1)}, u32[]{:S(2)}) copy-start(bf16[1280,8]{0,1:T(8,128)(2,1)} %param.7) | copy-start | bytes 61444
  198.4 204.8 %all-reduce.2.cloned.1.call-start = ((), (), s32[]{:S(2)}) async-start(), calls=%async_computation.5 | async-start | bytes 2457600 | tf_op jit(solution)/shard_map/psum | solution.py:97
Sparse Core Ops, SparseCore 0:
  198.5 112.3 reduce-scatter.1
  313.6 89.5 all-reduce.1
where the time goes:
time: 414 us; the launch traced here: 412 us
  waiting for transfers between devices  216 us (52%)
  matrix products  53.1 us (13%)
  other arithmetic  50.4 us (12%)
  local copies, waits for them, and re-layouts  45.7 us (11%)
  blocking collectives  19.1 us (5%)
  between operations  13.6 us (3%)
  starting transfers between devices  11.9 us (3%)
    reduce_scatter x1, waiting for transfers between devices, body(): lax.psum_scatter(partial_value, 'seq', scatter_dimension=1, tiled=True)  112 us
    psum x1, waiting for transfers between devices, body(): grad_weight = lax.psum(shares, 'dp')  92.2 us
    unnamed x5, other arithmetic  42.1 us
    unnamed x22, local copies, waits for them, and re-layouts  30.7 us
    all_to_all x1, blocking collectives, body(): lax.all_to_all(as_sent(grads_heads), 'seq', split_axis=1, concat_axis=2,...  19.1 us
    all_to_all x1, waiting for transfers between devices, body(): lax.all_to_all(projected[None], 'seq', split_axis=2, concat_axis=1, tiled...  11 us
  transfers between devices with their start and end apart: 4, of which 3 were waited for; matrix products, arithmetic and copies ran while one was open for 12% of the time, Pallas kernels for 0%

commit v1 on v0

v1 whole, which is shorter than its diff:
```python
import functools
import math

import jax
import jax.numpy as jnp
from jax import lax
from jax.experimental import pallas as pl
from jax.experimental.pallas import tpu as pltpu
from jax.sharding import PartitionSpec as P

HEAD_DIM = 80
F32, BF16 = jnp.float32, jnp.bfloat16
LANES = 128


def matmul(a, b, dims=((1,), (0,))):
    return lax.dot_general(a, b, (dims, ((), ())), preferred_element_type=F32)


def thirds(value):
    high = value.astype(BF16)
    rest = value - high.astype(F32)
    middle = rest.astype(BF16)
    return high, middle, (rest - middle.astype(F32)).astype(BF16)


def learn_tokens(frames, map_weight):
    frame_count = frames.shape[0]
    width_all = frames.shape[2]
    logits = jnp.dot(frames.reshape(-1, width_all), map_weight, preferred_element_type=F32)
    token_maps = jax.nn.sigmoid(logits).astype(BF16).reshape(frame_count, frames.shape[1], -1)
    pooled = jnp.einsum("fps,fpd->fsd", token_maps, frames, preferred_element_type=F32)
    pooled = pooled.reshape(-1, width_all)
    centred = pooled - jnp.mean(pooled, axis=-1, keepdims=True)
    variance = jnp.mean(centred * centred, axis=-1, keepdims=True)
    return (centred * lax.rsqrt(variance + 1e-06)).astype(BF16)


def attention_kernel(step_rows, sub_rows, qkv_ref, cot_ref, out_ref, x, c, k3, v1, dk, dv):
    step = pl.program_id(0)
    hd = HEAD_DIM
    scale = 1.0 / math.sqrt(hd)
    pieces, _, width = qkv_ref.shape

    @pl.when(step == 0)
    def _():
        for piece in range(pieces):
            columns = slice(piece * width, (piece + 1) * width)
            x[:, columns] = qkv_ref[piece]
            c[:, columns] = cot_ref[piece]
        key = x[hd : 2 * hd, :]
        k3[...] = jnp.concatenate([key, key, key], axis=0)
        row = lax.broadcasted_iota(jnp.int32, (LANES - hd, pieces * width), 0)
        ones = jnp.where(row < 3, 1.0, 0.0).astype(BF16)
        v1[...] = jnp.concatenate([x[2 * hd : 3 * hd, :], ones], axis=0)
        dk[...] = jnp.zeros_like(dk)
        dv[...] = jnp.zeros_like(dv)

    lane = lax.broadcasted_iota(jnp.int32, (sub_rows, LANES - hd), 1)
    for sub in range(step_rows // sub_rows):
        rows = pl.ds(pl.multiple_of(step * step_rows + sub * sub_rows, sub_rows), sub_rows)
        query_t = x[0:hd, rows].astype(F32)
        cot_t = c[:, rows]
        cot = cot_t.T
        terms = jnp.concatenate(thirds(query_t * (scale * math.log2(math.e))), axis=0).T
        scores = matmul(terms, k3[...])
        shifted = jnp.exp2(scores - jnp.max(scores, axis=-1, keepdims=True)).astype(BF16)
        attended = matmul(shifted, v1[...], ((1,), (1,)))
        inverse = 1.0 / attended[:, hd : hd + 1]
        row_dot = jnp.sum(cot.astype(F32) * attended[:, 0:hd], axis=-1, keepdims=True) * inverse
        first, second, third = (t.astype(F32) for t in thirds(-row_dot))
        tail = jnp.where(
            lane == 0, first, jnp.where(lane == 1, second, jnp.where(lane == 2, third, 0.0))
        ).astype(BF16)
        difference = matmul(jnp.concatenate([cot, tail], axis=1), v1[...])
        grad_scores = (shifted.astype(F32) * difference).astype(BF16)
        grad_query = matmul(grad_scores, k3[0:hd, :], ((1,), (1,))) * (inverse * scale)
        out_ref[0:hd, rows] = grad_query.T.astype(BF16)
        inverse_t = jnp.broadcast_to(inverse, (sub_rows, LANES)).T[0:1, :]
        dk[...] += matmul((query_t * (inverse_t * scale)).astype(BF16), grad_scores)
        dv[...] += matmul((cot_t.astype(F32) * inverse_t).astype(BF16), shifted)

    @pl.when(step == pl.num_programs(0) - 1)
    def _():
        out_ref[hd : 2 * hd, :] = dk[...].astype(BF16)
        out_ref[2 * hd : 3 * hd, :] = dv[...].astype(BF16)


def attention_gradient(qkv, cot):
    pieces, columns, width = qkv.shape
    tokens = pieces * width
    step_rows, sub_rows = min(1024, tokens), min(256, tokens)
    whole = lambda shape: pl.BlockSpec(shape, lambda i: (0,) * len(shape))
    return pl.pallas_call(
        functools.partial(attention_kernel, step_rows, sub_rows),
        out_shape=jax.ShapeDtypeStruct((columns, tokens), BF16),
        grid=(tokens // step_rows,),
        in_specs=[whole(qkv.shape), whole(cot.shape)],
        out_specs=whole((columns, tokens)),
        scratch_shapes=[
            pltpu.VMEM((columns, tokens), BF16),
            pltpu.VMEM((HEAD_DIM, tokens), BF16),
            pltpu.VMEM((3 * HEAD_DIM, tokens), BF16),
            pltpu.VMEM((LANES, tokens), BF16),
            pltpu.VMEM((HEAD_DIM, tokens), F32),
            pltpu.VMEM((HEAD_DIM, tokens), F32),
        ],
        compiler_params=pltpu.CompilerParams(vmem_limit_bytes=48 << 20),
        cost_estimate=pl.CostEstimate(
            flops=12 * tokens * tokens * 128, bytes_accessed=4 << 20, transcendentals=tokens * tokens
        ),
        name="attention_gradient",
    )(qkv, cot)


def exchange(array, axis_name):
    return lax.all_to_all(array, axis_name, split_axis=0, concat_axis=0, tiled=True)


def body(frames, map_weight, qkv_weight, cotangent):
    seq, dp = lax.axis_size("seq"), lax.axis_size("dp")
    cot = exchange(cotangent[0].T.reshape(seq, -1, cotangent.shape[1]), "seq")
    normed = learn_tokens(frames[0], map_weight)
    projected = jnp.dot(normed, qkv_weight, preferred_element_type=F32).astype(BF16)
    qkv = exchange(projected.T.reshape(seq, -1, normed.shape[0]), "seq")
    tokens = lax.all_gather(normed, "seq", tiled=True)
    grads = attention_gradient(qkv, cot)
    term = matmul(grads, tokens).T.astype(BF16)
    pieces = exchange(term.reshape(dp, -1, term.shape[1]), "dp")
    summed = jnp.sum(pieces.astype(F32), axis=0).astype(BF16)
    whole = exchange(jnp.broadcast_to(summed[None], (dp,) + summed.shape), "dp")
    return whole.reshape(term.shape).astype(F32)


def solution(mesh):
    placed = (P("dp", "seq", None, None), P(), P(), P("dp", "seq", None))
    return jax.shard_map(
        body, mesh=mesh, in_specs=placed, out_specs=P(None, "seq"), check_vma=False
    )
```

time: 414 us -> 128 us (0.31)
  waiting for transfers between devices: 216 us -> 2.54 us
  other arithmetic: 50.4 us -> 1.34 us
  blocking collectives: 19.1 us -> 62.4 us
  local copies, waits for them, and re-layouts: 45.7 us -> 4.19 us
  matrix products: 53.1 us -> 18 us
  Pallas kernels: 0 us -> 19.6 us
  starting transfers between devices: 11.9 us -> 5.84 us
    reduce_scatter x1 -> x0, waiting for transfers between devices: 112 us -> none  [body(): lax.psum_scatter(partial_value, 'seq', scatter_dimension=1, tiled=True)]
    psum x1 -> x0, waiting for transfers between devices: 92.2 us -> none  [body(): grad_weight = lax.psum(shares, 'dp')]
    all_to_all x1 -> x3, blocking collectives: 19.1 us -> 62.4 us  [exchange(): lax.all_to_all(array, axis_name, split_axis=0, concat_axis=0, tiled=True)]
    unnamed x5 -> x0, other arithmetic: 42.1 us -> none
    dot_general x27 -> x3, matrix products: 46.2 us -> 10.9 us  [the longest x1 5.38 us: body(): jnp.dot(normed, qkv_weight, preferred_element_type=F32).astype(BF16)]
    unnamed x22 -> x6, local copies, waits for them, and re-layouts: 30.7 us -> 0.73 us
    pallas_call x0 -> x1, Pallas kernels: none -> 19.6 us  [attention_gradient(): pl.pallas_call(functools.partial(attention_kernel, step_rows, sub_rows),...]
    all_to_all x2 -> x1, waiting for transfers between devices: 11 us -> 2.5 us  [exchange(): lax.all_to_all(array, axis_name, split_axis=0, concat_axis=0, tiled=True)]
  transfers between devices with their start and end apart: 4 -> 2, of which waited for: 3 -> 1; matrix products, arithmetic and copies ran while one was open for 12% -> 5% of each run, Pallas kernels for 0% -> 15%
where the time goes in v1:
time: 128 us; the launch traced here: 127 us
  blocking collectives  62.4 us (49%)
  Pallas kernels  19.6 us (15%)
  matrix products  18 us (14%)
  between operations  13.5 us (11%)
  starting transfers between devices  5.84 us (5%)
  local copies, waits for them, and re-layouts  4.19 us (3%)
  waiting for transfers between devices  2.54 us (2%)
  other arithmetic  1.34 us (1%)
    all_to_all x3, blocking collectives, exchange(): lax.all_to_all(array, axis_name, split_axis=0, concat_axis=0, tiled=True)  62.4 us
    pallas_call x1, Pallas kernels, attention_gradient(): pl.pallas_call(functools.partial(attention_kernel, step_rows, sub_rows),...  19.6 us
    dot_general x1, matrix products, learn_tokens(): jnp.dot(frames.reshape(-1, width_all), map_weight, preferred_element_type...  7.1 us
    all_to_all x1, starting transfers between devices, exchange(): lax.all_to_all(array, axis_name, split_axis=0, concat_axis=0, tiled=True)  5.84 us
    dot_general x1, matrix products, body(): jnp.dot(normed, qkv_weight, preferred_element_type=F32).astype(BF16)  5.38 us
    dot_general x1, matrix products, matmul(): return lax.dot_general(a, b, (dims, ((), ())), preferred_element_type=F32)  3.93 us
  transfers between devices with their start and end apart: 2, of which 1 were waited for; matrix products, arithmetic and copies ran while one was open for 5% of the time, Pallas kernels for 15%

profile of v1, /device:TPU:0, one launch (start us, length us, event | category | flops | bytes accessed | tf_op | source)
XLA Modules:
  0.0 127.3 jit_solution(3466013842915711728)
XLA Ops:
  6.5 0.0 copy-start
  6.5 0.0 all-gather.2.cloned.1.call-start
  6.5 0.0 copy-start.1
  6.5 0.7 copy-done
  7.3 7.1 %fusion.6 = bf16[4096,8]{0,1:T(8,128)(2,1)S(1)} fusion(bf16[4096,1280]{1,0:T(8,128)(2,1)} %bitcast.31, bf16[1280,8]{0,1:T(8,128)(2,1)S(1)} %copy-done), kind=kOutput, calls=%fused_computation.8 | convolution fusion | flops 84017152 | bytes 10571776 | tf_op jit(solution)/shard_map/dot_general | solution.py:30
  14.4 0.0 copy-start.2
  14.4 0.0 copy-done.1
  14.4 1.5 %fusion.9 = (f32[16,8]{1,0:T(8,128)S(1)}, f32[16,8,1280]{2,1,0:T(8,128)S(1)}) fusion(bf16[16,256,8]{1,2,0:T(8,128)(2,1)S(1)} %bitcast.34, bf16[1,16,256,1280]{3,2,1,0:T(8,128)(2,1)S(1)} %copy-done.1), kind=kOutput, calls=%fused_computation.17 | convolution fusion | flops 84049792 | bytes 11207168 | tf_op jit(solution)/shard_map/fps,fpd->fsd/dot_general | solution.py:32
  15.9 0.1 div.13
  16.0 0.2 multiply_reduce_fusion
  16.3 0.1 rsqrt.12
  16.4 0.9 fusion.8
  17.2 0.0 all-gather.2.cloned.1.call-update
  17.3 0.0 copy-done.2
  17.3 0.9 copy.8
  18.2 5.8 %all-to-all-start.1 = ((bf16[16,80,128]{2,1,0:T(8,128)(2,1)}), bf16[16,80,128]{2,1,0:T(8,128)(2,1)S(1)}, u32[]{:S(2)}, u32[]{:S(2)}) async-start(bf16[16,80,128]{2,1,0:T(8,128)(2,1)} %bitcast.8), calls=%async_computation.1 | async-start | bytes 655360 | tf_op jit(solution)/shard_map/all_to_all | solution.py:117
  24.0 5.4 %fusion.2 = bf16[3840,128]{0,1:T(8,128)(2,1)S(1)} fusion(bf16[128,1280]{1,0:T(8,128)(2,1)} %fusion.8, bf16[1280,3840]{1,0:T(8,128)(2,1)} %param.6), kind=kOutput, calls=%fused_computation.3 | convolution fusion | flops 1258782720 | bytes 11141120 | tf_op jit(solution)/shard_map/dot_general | solution.py:124
  29.4 0.7 copy.7
  30.1 2.5 %all-to-all-done.1.cot_ref = bf16[16,80,128]{2,1,0:T(8,128)(2,1)S(1)} async-done(((bf16[16,80,128]{2,1,0:T(8,128)(2,1)}), bf16[16,80,128]{2,1,0:T(8,128)(2,1)S(1)}, u32[]{:S(2)}, u32[]{:S(2)}) %all-to-all-start.1) | async-done | bytes 327712 | tf_op jit(solution)/shard_map/all_to_all | solution.py:117
  32.6 25.4 %all_to_all.20.qkv_ref = bf16[16,240,128]{2,1,0:T(8,128)(2,1)S(1)} all-to-all(bf16[16,240,128]{2,1,0:T(8,128)(2,1)S(1)} %bitcast.32), channel_id=1, replica_groups=mesh['dp'=8,'seq'=16] {'seq'}, dimensions={0} | all-to-all | bytes 1966080 | tf_op jit(solution)/shard_map/all_to_all | solution.py:117
  58.0 19.6 %attention_gradient.1 = bf16[240,2048]{1,0:T(8,128)(2,1)S(1)} custom-call(bf16[16,240,128]{2,1,0:T(8,128)(2,1)S(1)} %all_to_all.20.qkv_ref, bf16[16,80,128]{2,1,0:T(8,128)(2,1)S(1)} %all-to-all-done.1.cot_ref), custom_call_target="tpu_custom_call" | custom-call | flops 6442450944 | bytes 4194304 | tf_op jit(solution)/shard_map/attention_gradient/pallas_call | solution.py:94
  77.5 0.0 all-gather.2.cloned.1.call-done
  77.6 3.9 %convolution_convert_fusion.1 = bf16[1280,240]{0,1:T(8,128)(2,1)S(1)} fusion(bf16[240,2048]{1,0:T(8,128)(2,1)S(1)} %attention_gradient.1, bf16[2048,1280]{1,0:T(8,128)(2,1)} %all-gather.2.cloned.1.call-done), kind=kOutput, calls=%fused_computation.9 | convolution fusion | flops 1258598400 | bytes 6840320 | tf_op jit(solution)/shard_map/dot_general | solution.py:17
  81.5 0.2 copy.9
  81.7 21.5 %all_to_all.21 = bf16[8,160,240]{2,1,0:T(8,128)(2,1)S(1)} all-to-all(bf16[8,160,240]{2,1,0:T(8,128)(2,1)S(1)} %bitcast.33), channel_id=1, replica_groups=mesh['dp'=8,'seq'=16] {'dp'}, dimensions={0} | all-to-all | bytes 1228800 | tf_op jit(solution)/shard_map/all_to_all | solution.py:117
  103.2 0.1 reduce_sum.32
  103.4 15.5 %all_to_all.22 = bf16[8,160,240]{2,1,0:T(8,128)(2,1)S(1)} all-to-all(bf16[8,160,240]{2,1,0:T(8,128)(2,1)S(1)} %broadcast_in_dim.2), channel_id=1, replica_groups=mesh['dp'=8,'seq'=16] {'dp'}, dimensions={0} | all-to-all | bytes 1228800 | tf_op jit(solution)/shard_map/all_to_all | solution.py:117
  118.9 0.1 bitcast_convert_fusion
  119.0 1.4 %copy.10 = f32[1280,240]{0,1:T(8,128)} copy(f32[1280,240]{1,0:T(8,128)S(1)} %bitcast_convert_fusion) | data formatting | bytes 2457600 | tf_op jit(solution)/shard_map/convert_element_type | solution.py:132
  (3 shorter events, 0.1 us)
Async XLA Ops:
  6.5 0.7 copy-start
  6.5 71.0 %all-gather.2.cloned.1.call-start = ((), (), s32[]{:S(2)}) async-start(), calls=%async_computation.4 | async-start | bytes 5570560 | tf_op jit(solution)/shard_map/all_gather | solution.py:126
  6.5 7.8 %copy-start.1 = (bf16[1,16,256,1280]{3,2,1,0:T(8,128)(2,1)S(1)}, bf16[1,16,256,1280]{3,2,1,0:T(8,128)(2,1)}, u32[]{:S(2)}) copy-start(bf16[1,16,256,1280]{3,2,1,0:T(8,128)(2,1)} %param.4) | copy-start | bytes 31457284
  14.4 2.9 %copy-start.2 = (bf16[1,128,1280]{2,1,0:T(8,128)(2,1)S(1)}, bf16[1,128,1280]{2,1,0:T(8,128)(2,1)}, u32[]{:S(2)}) copy-start(bf16[1,128,1280]{2,1,0:T(8,128)(2,1)} %param.7) | copy-start | bytes 983044
  18.2 14.4 %all-to-all-start.1 = ((bf16[16,80,128]{2,1,0:T(8,128)(2,1)}), bf16[16,80,128]{2,1,0:T(8,128)(2,1)S(1)}, u32[]{:S(2)}, u32[]{:S(2)}) async-start(bf16[16,80,128]{2,1,0:T(8,128)(2,1)} %bitcast.8), calls=%async_computation.1 | async-start | bytes 655360 | tf_op jit(solution)/shard_map/all_to_all | solution.py:117
Sparse Core Ops, SparseCore 0:
  17.4 51.8 all-gather.1

commit v2 on v1

--- a/solution.py
+++ b/solution.py
@@ -24,30 +24,117 @@
     return high, middle, (rest - middle.astype(F32)).astype(BF16)
 
 
-def learn_tokens(frames, map_weight):
-    frame_count = frames.shape[0]
-    width_all = frames.shape[2]
-    logits = jnp.dot(frames.reshape(-1, width_all), map_weight, preferred_element_type=F32)
-    token_maps = jax.nn.sigmoid(logits).astype(BF16).reshape(frame_count, frames.shape[1], -1)
-    pooled = jnp.einsum("fps,fpd->fsd", token_maps, frames, preferred_element_type=F32)
-    pooled = pooled.reshape(-1, width_all)
-    centred = pooled - jnp.mean(pooled, axis=-1, keepdims=True)
-    variance = jnp.mean(centred * centred, axis=-1, keepdims=True)
-    return (centred * lax.rsqrt(variance + 1e-06)).astype(BF16)
-
-
-def attention_kernel(step_rows, sub_rows, qkv_ref, cot_ref, out_ref, x, c, k3, v1, dk, dv):
+def tokens_kernel(
+    group, frames, map_weight, weight, cot, normed, send, held, weight_held, map_weight_t, cot_held, sems, weight_sem
+):
+    count, _, width = frames.shape
+    heads, rows, _ = send.shape
+    own = weight.shape[1] // heads
+    slots = map_weight_t.shape[0]
+    parts = [pl.ds(g * group, group) for g in range(count // group)]
+    loads = [
+        pltpu.make_async_copy(frames.at[part], held.at[part], sems.at[g])
+        for g, part in enumerate(parts)
+    ]
+    weight_load = pltpu.make_async_copy(weight, weight_held, weight_sem.at[0])
+    map_load = pltpu.make_async_copy(map_weight, map_weight_t, weight_sem.at[1])
+    cot_load = pltpu.make_async_copy(cot, cot_held, weight_sem.at[2])
+    for load in (map_load, *loads, cot_load):
+        load.start()
+    map_load.wait()
+    for g, load in enumerate(loads):
+        load.wait()
+        if g == 0:
+            weight_load.start()
+        blocks = [held[g * group + k] for k in range(group)]
+        logits = [matmul(map_weight_t[...], block, ((1,), (1,))) for block in blocks]
+        maps = [jax.nn.sigmoid(l).astype(BF16) for l in logits]
+        pooled = jnp.concatenate([matmul(m, block) for m, block in zip(maps, blocks)], axis=0)
+        centred = pooled - jnp.mean(pooled, axis=-1, keepdims=True)
+        variance = jnp.mean(centred * centred, axis=-1, keepdims=True)
+        at = g * group * slots
+        normed[at : at + group * slots, :] = (centred * lax.rsqrt(variance + 1e-06)).astype(BF16)
+    cot_load.wait()
+    cot_t = cot_held[...].T
+    for h in range(heads):
+        send[h, own:rows, :] = cot_t[h * (rows - own) : (h + 1) * (rows - own), :]
+    tokens = normed[...]
+    weight_load.wait()
+    for start in range(0, weight.shape[1], 256):
+        block = matmul(tokens, weight_held[:, start : start + 256]).T.astype(BF16)
+        at = start
+        while at < start + 256:
+            h = at // own
+            end = min((h + 1) * own, start + 256)
+            send[h, at - h * own : end - h * own, :] = block[at - start : end - start, :]
+            at = end
+
+
+def learn_tokens(frames, map_weight, weight, cot, heads):
+    count, patches, width = frames.shape
+    tokens, columns = cot.shape[0], weight.shape[1]
+    group = math.gcd(count, 4)
+    vmem, hbm = pl.BlockSpec(memory_space=pltpu.VMEM), pl.BlockSpec(memory_space=pltpu.HBM)
+    return pl.pallas_call(
+        functools.partial(tokens_kernel, group),
+        out_shape=(
+            jax.ShapeDtypeStruct((tokens, width), BF16),
+            jax.ShapeDtypeStruct((heads, (columns + width) // heads, tokens), BF16),
+        ),
+        in_specs=[hbm, hbm, hbm, hbm],
+        out_specs=(vmem, vmem),
+        scratch_shapes=[
+            pltpu.VMEM(frames.shape, BF16),
+            pltpu.VMEM(weight.shape, BF16),
+            pltpu.VMEM(map_weight.shape[::-1], BF16),
+            pltpu.VMEM(cot.shape, BF16),
+            pltpu.SemaphoreType.DMA((count // group,)),
+            pltpu.SemaphoreType.DMA((3,)),
+        ],
+        compiler_params=pltpu.CompilerParams(vmem_limit_bytes=48 << 20),
+        name="learn_tokens",
+    )(frames, map_weight.T, weight, cot)
+
+
+def weight_kernel(grads_ref, tokens, out_ref, held, sems):
+    chunks = sems.shape[0]
+    block = tokens.shape[0] // chunks
+    parts = [pl.ds(i * block, block) for i in range(chunks)]
+    loads = [pltpu.make_async_copy(tokens.at[p], held.at[p], sems.at[i]) for i, p in enumerate(parts)]
+    for load in loads:
+        load.start()
+    total = None
+    for part, load in zip(parts, loads):
+        load.wait()
+        term = matmul(grads_ref[:, part], held[part, :])
+        total = term if total is None else total + term
+    out_ref[...] = total.astype(BF16)
+
+
+def weight_gradient(grads, tokens):
+    vmem, hbm = pl.BlockSpec(memory_space=pltpu.VMEM), pl.BlockSpec(memory_space=pltpu.HBM)
+    return pl.pallas_call(
+        weight_kernel,
+        out_shape=jax.ShapeDtypeStruct((grads.shape[0], tokens.shape[1]), BF16),
+        in_specs=[vmem, hbm],
+        out_specs=vmem,
+        scratch_shapes=[pltpu.VMEM(tokens.shape, BF16), pltpu.SemaphoreType.DMA((4,))],
+        compiler_params=pltpu.CompilerParams(vmem_limit_bytes=32 << 20),
+        name="weight_gradient",
+    )(grads, tokens)
+
+
+def attention_kernel(step_rows, sub_rows, x_ref, out_ref, x, k3, v1, dk, dv):
     step = pl.program_id(0)
     hd = HEAD_DIM
     scale = 1.0 / math.sqrt(hd)
-    pieces, _, width = qkv_ref.shape
+    pieces, _, width = x_ref.shape
 
     @pl.when(step == 0)
     def _():
         for piece in range(pieces):
             columns = slice(piece * width, (piece + 1) * width)
-            x[:, columns] = qkv_ref[piece]
-            c[:, columns] = cot_ref[piece]
+            x[:, columns] = x_ref[piece]
         key = x[hd : 2 * hd, :]
         k3[...] = jnp.concatenate([key, key, key], axis=0)
         row = lax.broadcasted_iota(jnp.int32, (LANES - hd, pieces * width), 0)
@@ -60,7 +147,7 @@
     for sub in range(step_rows // sub_rows):
         rows = pl.ds(pl.multiple_of(step * step_rows + sub * sub_rows, sub_rows), sub_rows)
         query_t = x[0:hd, rows].astype(F32)
-        cot_t = c[:, rows]
+        cot_t = x[3 * hd :, rows]
         cot = cot_t.T
         terms = jnp.concatenate(thirds(query_t * (scale * math.log2(math.e))), axis=0).T
         scores = matmul(terms, k3[...])
@@ -84,22 +171,22 @@
     def _():
         out_ref[hd : 2 * hd, :] = dk[...].astype(BF16)
         out_ref[2 * hd : 3 * hd, :] = dv[...].astype(BF16)
-
-
-def attention_gradient(qkv, cot):
-    pieces, columns, width = qkv.shape
+        out_ref[3 * hd :, :] = jnp.zeros((out_ref.shape[0] - 3 * hd, out_ref.shape[1]), BF16)
+
+
+def attention_gradient(x, rows):
+    pieces, columns, width = x.shape
     tokens = pieces * width
     step_rows, sub_rows = min(1024, tokens), min(256, tokens)
     whole = lambda shape: pl.BlockSpec(shape, lambda i: (0,) * len(shape))
     return pl.pallas_call(
         functools.partial(attention_kernel, step_rows, sub_rows),
-        out_shape=jax.ShapeDtypeStruct((columns, tokens), BF16),
+        out_shape=jax.ShapeDtypeStruct((rows, tokens), BF16),
         grid=(tokens // step_rows,),
-        in_specs=[whole(qkv.shape), whole(cot.shape)],
-        out_specs=whole((columns, tokens)),
+        in_specs=[whole(x.shape)],
+        out_specs=whole((rows, tokens)),
         scratch_shapes=[
             pltpu.VMEM((columns, tokens), BF16),
-            pltpu.VMEM((HEAD_DIM, tokens), BF16),
             pltpu.VMEM((3 * HEAD_DIM, tokens), BF16),
             pltpu.VMEM((LANES, tokens), BF16),
             pltpu.VMEM((HEAD_DIM, tokens), F32),
@@ -110,7 +197,7 @@
             flops=12 * tokens * tokens * 128, bytes_accessed=4 << 20, transcendentals=tokens * tokens
         ),
         name="attention_gradient",
-    )(qkv, cot)
+    )(x)
 
 
 def exchange(array, axis_name):
@@ -119,17 +206,16 @@
 
 def body(frames, map_weight, qkv_weight, cotangent):
     seq, dp = lax.axis_size("seq"), lax.axis_size("dp")
-    cot = exchange(cotangent[0].T.reshape(seq, -1, cotangent.shape[1]), "seq")
-    normed = learn_tokens(frames[0], map_weight)
-    projected = jnp.dot(normed, qkv_weight, preferred_element_type=F32).astype(BF16)
-    qkv = exchange(projected.T.reshape(seq, -1, normed.shape[0]), "seq")
+    columns = qkv_weight.shape[1] // seq
+    padded = -(-columns // (16 * dp)) * 16 * dp
+    normed, send = learn_tokens(frames[0], map_weight, qkv_weight, cotangent[0], seq)
     tokens = lax.all_gather(normed, "seq", tiled=True)
-    grads = attention_gradient(qkv, cot)
-    term = matmul(grads, tokens).T.astype(BF16)
+    grads = attention_gradient(exchange(send, "seq"), padded)
+    term = weight_gradient(grads, tokens)
     pieces = exchange(term.reshape(dp, -1, term.shape[1]), "dp")
     summed = jnp.sum(pieces.astype(F32), axis=0).astype(BF16)
     whole = exchange(jnp.broadcast_to(summed[None], (dp,) + summed.shape), "dp")
-    return whole.reshape(term.shape).astype(F32)
+    return whole.reshape(term.shape)[:columns].astype(F32).T
 
 
 def solution(mesh):

time: 128 us -> 119 us (0.930)
  matrix products: 18 us -> 0 us
  Pallas kernels: 19.6 us -> 30.8 us
  blocking collectives: 62.4 us -> 68.7 us
  starting transfers between devices: 5.84 us -> 0.01 us
  waiting for transfers between devices: 2.54 us -> 0.04 us
    dot_general x4 -> x0, matrix products: 18 us -> none  [the longest x1 7.1 us: learn_tokens(): jnp.dot(frames.reshape(-1, width_all), map_weight, preferred_element_type...]
    pallas_call x0 -> x2, Pallas kernels: none -> 11.2 us  [the longest x1 8.88 us: learn_tokens(): pl.pallas_call(functools.partial(tokens_kernel, group), out_shape=(jax.Sh...]
    all_to_all x3, blocking collectives: 62.4 us -> 68.7 us  [exchange(): lax.all_to_all(array, axis_name, split_axis=0, concat_axis=0, tiled=True)]
    all_to_all x1 -> x0, starting transfers between devices: 5.84 us -> none  [exchange(): lax.all_to_all(array, axis_name, split_axis=0, concat_axis=0, tiled=True)]
    unnamed x6, local copies, waits for them, and re-layouts: 0.73 us -> 4.18 us
    all_to_all x1 -> x0, waiting for transfers between devices: 2.5 us -> none  [exchange(): lax.all_to_all(array, axis_name, split_axis=0, concat_axis=0, tiled=True)]
    convert_element_type x3 -> x0, local copies, waits for them, and re-layouts: 2.32 us -> none  [the longest x1 1.43 us: body(): return whole.reshape(term.shape).astype(F32)]
  transfers between devices with their start and end apart: 2 -> 1, of which waited for: 1 -> 0; matrix products, arithmetic and copies ran while one was open for 5% -> 0% of each run, Pallas kernels for 15% -> 16%
where the time goes in v2:
time: 119 us; the launch traced here: 118 us
  blocking collectives  68.7 us (58%)
  Pallas kernels  30.8 us (26%)
  between operations  13.4 us (11%)
  local copies, waits for them, and re-layouts  4.22 us (4%)
  other arithmetic  1.2 us (1%)
    all_to_all x3, blocking collectives, exchange(): lax.all_to_all(array, axis_name, split_axis=0, concat_axis=0, tiled=True)  68.7 us
    pallas_call x1, Pallas kernels, attention_gradient(): pl.pallas_call(functools.partial(attention_kernel, step_rows, sub_rows),...  19.5 us
    pallas_call x1, Pallas kernels, learn_tokens(): pl.pallas_call(functools.partial(tokens_kernel, group), out_shape=(jax.Sh...  8.88 us
    unnamed x6, local copies, waits for them, and re-layouts  4.18 us
  transfers between devices with their start and end apart: 1, of which 0 were waited for; matrix products, arithmetic and copies ran while one was open for 0% of the time, Pallas kernels for 16%

profile of v2, /device:TPU:0, one launch (start us, length us, event | category | flops | bytes accessed | tf_op | source)
XLA Modules:
  0.0 118.4 jit_solution(7810307132463111850)
XLA Ops:
  6.5 0.0 all-gather.2.cloned.1.call-start
  6.5 0.0 copy-start.1
  6.5 1.0 copy-done.1
  7.5 0.0 copy-start.2
  7.5 0.7 copy-done.2
  8.2 8.9 %learn_tokens.1 = (bf16[128,1280]{1,0:T(8,128)(2,1)}, bf16[16,320,128]{2,1,0:T(8,128)(2,1)S(1)}) custom-call(bf16[16,256,1280]{2,1,0:T(8,128)(2,1)} %bitcast.10, bf16[8,1280]{1,0:T(8,128)(2,1)S(1)} %bitcast.9, bf16[1280,3840]{1,0:T(8,128)(2,1)} %weight.1, bf16[128,1280]{1,0:T(8,128)(2,1)S(1)} %bitcast.8), custom_call_target="tpu_custom_call" | custom-call | tf_op jit(solution)/shard_map/learn_tokens/pallas_call | solution.py:78
  17.1 0.0 all-gather.2.cloned.1.call-update
  17.1 31.5 %all_to_all.15.x_ref = bf16[16,320,128]{2,1,0:T(8,128)(2,1)S(1)} all-to-all(bf16[16,320,128]{2,1,0:T(8,128)(2,1)S(1)} %get-tuple-element.7), channel_id=1, replica_groups=mesh['dp'=8,'seq'=16] {'seq'}, dimensions={0} | all-to-all | bytes 2621440 | tf_op jit(solution)/shard_map/all_to_all | solution.py:204
  48.6 19.5 %attention_gradient.1.grads_ref = bf16[256,2048]{1,0:T(8,128)(2,1)S(1)} custom-call(bf16[16,320,128]{2,1,0:T(8,128)(2,1)S(1)} %all_to_all.15.x_ref), custom_call_target="tpu_custom_call" | custom-call | flops 6442450944 | bytes 4194304 | tf_op jit(solution)/shard_map/attention_gradient/pallas_call | solution.py:182
  68.2 0.0 all-gather.2.cloned.1.call-done.tokens
  68.2 0.0 copy-start
  68.2 2.5 %copy-done = bf16[2048,1280]{1,0:T(8,128)(2,1)S(1)} copy-done((bf16[2048,1280]{1,0:T(8,128)(2,1)S(1)}, bf16[2048,1280]{1,0:T(8,128)(2,1)}, u32[]{:S(2)}) %copy-start) | copy-done | bytes 5242904
  70.7 2.4 %weight_gradient.1 = bf16[256,1280]{1,0:T(8,128)(2,1)S(1)} custom-call(bf16[256,2048]{1,0:T(8,128)(2,1)S(1)} %attention_gradient.1.grads_ref, bf16[2048,1280]{1,0:T(8,128)(2,1)S(1)} %copy-done), custom_call_target="tpu_custom_call" | custom-call | tf_op jit(solution)/shard_map/weight_gradient/pallas_call | solution.py:116
  73.1 21.0 %all_to_all.16 = bf16[8,32,1280]{2,1,0:T(8,128)(2,1)S(1)} all-to-all(bf16[8,32,1280]{2,1,0:T(8,128)(2,1)S(1)} %bitcast.7), channel_id=1, replica_groups=mesh['dp'=8,'seq'=16] {'dp'}, dimensions={0} | all-to-all | bytes 1310720 | tf_op jit(solution)/shard_map/all_to_all | solution.py:204
  94.1 0.1 reduce_sum.12
  94.3 16.2 %all_to_all.17 = bf16[8,32,1280]{2,1,0:T(8,128)(2,1)S(1)} all-to-all(bf16[8,32,1280]{2,1,0:T(8,128)(2,1)S(1)} %broadcast_in_dim.2), channel_id=1, replica_groups=mesh['dp'=8,'seq'=16] {'dp'}, dimensions={0} | all-to-all | bytes 1310720 | tf_op jit(solution)/shard_map/all_to_all | solution.py:204
  110.4 1.1 convert_bitcast_fusion
  (1 shorter events, 0.0 us)
Async XLA Ops:
  6.5 61.7 %all-gather.2.cloned.1.call-start = ((), (), s32[]{:S(2)}) async-start(), calls=%async_computation.3 | async-start | bytes 5570560 | tf_op jit(solution)/shard_map/all_gather | solution.py:212
  6.5 1.0 copy-start.1
  7.5 0.7 copy-start.2
  68.2 2.5 %copy-start = (bf16[2048,1280]{1,0:T(8,128)(2,1)S(1)}, bf16[2048,1280]{1,0:T(8,128)(2,1)}, u32[]{:S(2)}) copy-start(bf16[2048,1280]{1,0:T(8,128)(2,1)} %all-gather.2.cloned.1.call-done.tokens) | copy-start | bytes 15728644
Sparse Core Ops, SparseCore 0:
  17.3 50.1 all-gather.1

commit v3 on v1

v3 whole, which is shorter than its diff:
```python
import functools
import math

import jax
import jax.numpy as jnp
from jax import lax
from jax.experimental import pallas as pl
from jax.experimental.pallas import tpu as pltpu
from jax.sharding import PartitionSpec as P

HEAD_DIM = 80
F32, BF16 = jnp.float32, jnp.bfloat16
LANES = 128


def matmul(a, b, dims=((1,), (0,))):
    return lax.dot_general(a, b, (dims, ((), ())), preferred_element_type=F32)


def thirds(value):
    high = value.astype(BF16)
    rest = value - high.astype(F32)
    middle = rest.astype(BF16)
    return high, middle, (rest - middle.astype(F32)).astype(BF16)


def tokens_kernel(group, frames, map_weight, cot, normed, send, held, map_weight_t, cot_held, sems, own_sems):
    count = frames.shape[0]
    slots = map_weight_t.shape[0]
    parts = [pl.ds(g * group, group) for g in range(count // group)]
    loads = [
        pltpu.make_async_copy(frames.at[part], held.at[part], sems.at[g])
        for g, part in enumerate(parts)
    ]
    map_load = pltpu.make_async_copy(map_weight, map_weight_t, own_sems.at[0])
    cot_load = pltpu.make_async_copy(cot, cot_held, own_sems.at[1])
    for load in (map_load, cot_load, *loads):
        load.start()
    map_load.wait()
    cot_load.wait()
    send[...] = cot_held[...].T.reshape(send.shape)
    for g, load in enumerate(loads):
        load.wait()
        blocks = [held[g * group + k] for k in range(group)]
        logits = [matmul(map_weight_t[...], block, ((1,), (1,))) for block in blocks]
        maps = [jax.nn.sigmoid(l).astype(BF16) for l in logits]
        pooled = jnp.concatenate([matmul(m, block) for m, block in zip(maps, blocks)], axis=0)
        centred = pooled - jnp.mean(pooled, axis=-1, keepdims=True)
        variance = jnp.mean(centred * centred, axis=-1, keepdims=True)
        at = g * group * slots
        normed[at : at + group * slots, :] = (centred * lax.rsqrt(variance + 1e-06)).astype(BF16)


def learn_tokens(frames, map_weight, cot, heads):
    count = frames.shape[0]
    tokens, width = cot.shape
    group = math.gcd(count, 4)
    vmem, hbm = pl.BlockSpec(memory_space=pltpu.VMEM), pl.BlockSpec(memory_space=pltpu.HBM)
    return pl.pallas_call(
        functools.partial(tokens_kernel, group),
        out_shape=(
            jax.ShapeDtypeStruct((tokens, width), BF16),
            jax.ShapeDtypeStruct((heads, width // heads, tokens), BF16),
        ),
        in_specs=[hbm, hbm, hbm],
        out_specs=(vmem, vmem),
        scratch_shapes=[
            pltpu.VMEM(frames.shape, BF16),
            pltpu.VMEM(map_weight.shape[::-1], BF16),
            pltpu.VMEM(cot.shape, BF16),
            pltpu.SemaphoreType.DMA((count // group,)),
            pltpu.SemaphoreType.DMA((2,)),
        ],
        compiler_params=pltpu.CompilerParams(vmem_limit_bytes=62 << 20),
        name="learn_tokens",
    )(frames, map_weight.T, cot)


def head_kernel(sub, order_ref, cot_ref, weight_ref, *refs):
    pieces = cot_ref.shape[0]
    chunks, out_ref = refs[:pieces], refs[pieces]
    x, k3, v1, grads, query_scaled, cot_scaled, shifted_all, scores_all = refs[pieces + 1 :]
    hd = HEAD_DIM
    scale = 1.0 / math.sqrt(hd)
    width = cot_ref.shape[2]
    count = pieces * width
    join = 4
    for at in range(0, pieces, join):
        tokens = jnp.concatenate([chunk[...] for chunk in chunks[at : at + join]], axis=0)
        columns = slice(at * width, (at + join) * width)
        x[0 : 3 * hd, columns] = matmul(tokens, weight_ref[...]).T.astype(BF16)
    for piece in range(pieces):
        x[3 * hd :, piece * width : (piece + 1) * width] = cot_ref[order_ref[piece]]
    key = x[hd : 2 * hd, :]
    k3[...] = jnp.concatenate([key, key, key], axis=0)
    row = lax.broadcasted_iota(jnp.int32, (LANES - hd, count), 0)
    ones = jnp.where(row < 3, 1.0, 0.0).astype(BF16)
    v1[...] = jnp.concatenate([x[2 * hd : 3 * hd, :], ones], axis=0)
    lane = lax.broadcasted_iota(jnp.int32, (sub, LANES - hd), 1)
    blocks = count // sub
    state = [{} for _ in range(blocks)]

    def rows(s):
        return slice(s * sub, (s + 1) * sub)

    def score(s):
        query = x[0:hd, rows(s)].astype(F32)
        terms = jnp.concatenate(thirds(query * (scale * math.log2(math.e))), axis=0).T
        state[s].update(query=query, scores=matmul(terms, k3[...]))

    def exponent(s):
        scores = state[s].pop("scores")
        shifted = jnp.exp2(scores - jnp.max(scores, axis=-1, keepdims=True)).astype(BF16)
        shifted_all[rows(s), :] = shifted
        state[s]["shifted"] = shifted

    def attend(s):
        cot_t = x[3 * hd :, rows(s)]
        cot = cot_t.T
        attended = matmul(state[s]["shifted"], v1[...], ((1,), (1,)))
        inverse = 1.0 / attended[:, hd : hd + 1]
        row_dot = jnp.sum(cot.astype(F32) * attended[:, 0:hd], axis=-1, keepdims=True) * inverse
        first, second, third = (t.astype(F32) for t in thirds(-row_dot))
        tail = jnp.where(
            lane == 0, first, jnp.where(lane == 1, second, jnp.where(lane == 2, third, 0.0))
        ).astype(BF16)
        difference = matmul(jnp.concatenate([cot, tail], axis=1), v1[...])
        state[s].update(cot_t=cot_t, inverse=inverse, difference=difference)

    def grad_score(s):
        grad_scores = (state[s]["shifted"].astype(F32) * state[s].pop("difference")).astype(BF16)
        scores_all[rows(s), :] = grad_scores
        state[s]["grad_scores"] = grad_scores

    def grad_query(s):
        inverse = state[s]["inverse"]
        product = matmul(state[s]["grad_scores"], k3[0:hd, :], ((1,), (1,))) * (inverse * scale)
        grads[0:hd, rows(s)] = product.T.astype(BF16)
        inverse_t = jnp.broadcast_to(inverse, (sub, LANES)).T[0:1, :]
        query_scaled[:, rows(s)] = (state[s]["query"] * (inverse_t * scale)).astype(BF16)
        cot_scaled[:, rows(s)] = (state[s]["cot_t"].astype(F32) * inverse_t).astype(BF16)
        state[s].clear()

    def both(stage, pair):
        for s in (2 * pair, 2 * pair + 1):
            if s < blocks:
                stage(s)

    both(score, 0)
    both(exponent, 0)
    for pair in range(blocks // 2):
        both(score, pair + 1)
        both(attend, pair)
        both(exponent, pair + 1)
        both(grad_score, pair)
        both(grad_query, pair)
    grads[hd : 2 * hd, :] = matmul(query_scaled[...], scores_all[...]).astype(BF16)
    grads[2 * hd : 3 * hd, :] = matmul(cot_scaled[...], shifted_all[...]).astype(BF16)
    grads[3 * hd :, :] = jnp.zeros((grads.shape[0] - 3 * hd, count), BF16)
    total = None
    for at in range(0, pieces, join):
        tokens = jnp.concatenate([chunk[...] for chunk in chunks[at : at + join]], axis=0)
        term = matmul(grads[:, at * width : (at + join) * width], tokens)
        total = term if total is None else total + term
    out_ref[...] = total.astype(BF16)


def head_gradient(order, cot, weight, chunks, rows):
    pieces, _, width = cot.shape
    count = pieces * width
    vmem = pl.BlockSpec(memory_space=pltpu.VMEM)
    return pl.pallas_call(
        functools.partial(head_kernel, 256),
        out_shape=jax.ShapeDtypeStruct((rows, chunks[0].shape[1]), BF16),
        in_specs=[pl.BlockSpec(memory_space=pltpu.SMEM)] + [vmem] * (2 + pieces),
        out_specs=vmem,
        scratch_shapes=[
            pltpu.VMEM((4 * HEAD_DIM, count), BF16),
            pltpu.VMEM((3 * HEAD_DIM, count), BF16),
            pltpu.VMEM((LANES, count), BF16),
            pltpu.VMEM((rows, count), BF16),
            pltpu.VMEM((HEAD_DIM, count), BF16),
            pltpu.VMEM((HEAD_DIM, count), BF16),
            pltpu.VMEM((count, count), BF16),
            pltpu.VMEM((count, count), BF16),
        ],
        compiler_params=pltpu.CompilerParams(vmem_limit_bytes=52 << 20),
        cost_estimate=pl.CostEstimate(
            flops=12 * count * count * LANES, bytes_accessed=8 << 20, transcendentals=count * count
        ),
        name="head_gradient",
    )(order, cot, weight, *chunks)


def exchange(array, axis_name):
    return lax.all_to_all(array, axis_name, split_axis=0, concat_axis=0, tiled=True)


RING, CORES = 4, 2


def gather_pieces(own):
    count = lax.axis_size("seq")
    me = lax.axis_index("seq")

    def over(index, dz, dx, dc):
        plane, x, core = index // (RING * CORES), index // CORES % RING, index % CORES
        return (plane ^ dz) * RING * CORES + (x + dx) % RING * CORES + (core ^ dc)

    def send(array, *by):
        return lax.ppermute(array, "seq", [(i, over(i, *by)) for i in range(count)])

    right, left = send(own, 0, 1, 0), send(own, 0, -1, 0)
    other = send(own, 1, 0, 0)
    other_right, other_left = send(other, 0, 1, 0), send(other, 0, -1, 0)
    across, other_across = send(right, 0, 1, 0), send(other_left, 0, -1, 0)
    near = [own, other, right, left, other_right, other_left, across, other_across]
    places = [(0, 0), (1, 0), (0, -1), (0, 1), (1, -1), (1, 1), (0, -2), (1, 2)]
    pieces, order = list(near), [over(me, dz, dx, 0) for dz, dx in places]
    for array, (dz, dx) in zip(near, places):
        pieces.append(send(array, 0, 0, 1))
        order.append(over(me, dz, dx, 1))
    return pieces, jnp.stack(order).astype(jnp.int32)


def body(frames, map_weight, qkv_weight, cotangent):
    seq, dp = lax.axis_size("seq"), lax.axis_size("dp")
    columns = qkv_weight.shape[1] // seq
    padded = -(-columns // (16 * dp)) * 16 * dp
    normed, send = learn_tokens(frames[0], map_weight, cotangent[0], seq)
    pieces, order = gather_pieces(normed)
    own_weight = lax.dynamic_slice_in_dim(qkv_weight, lax.axis_index("seq") * columns, columns, 1)
    term = head_gradient(order, exchange(send, "seq"), own_weight, pieces, padded)
    parts = exchange(term.reshape(dp, -1, term.shape[1]), "dp")
    summed = jnp.sum(parts.astype(F32), axis=0).astype(BF16)
    whole = exchange(jnp.broadcast_to(summed[None], (dp,) + summed.shape), "dp")
    return whole.reshape(term.shape)[:columns].astype(F32).T


def solution(mesh):
    placed = (P("dp", "seq", None, None), P(), P(), P("dp", "seq", None))
    return jax.shard_map(
        body, mesh=mesh, in_specs=placed, out_specs=P(None, "seq"), check_vma=False
    )
```

time: 128 us -> 111 us (0.87)
  blocking collectives: 62.4 us -> 34.2 us
  waiting for transfers between devices: 2.54 us -> 27.4 us
  matrix products: 18 us -> 0 us
  between operations: 13.5 us -> 0.29 us
  starting transfers between devices: 5.84 us -> 16.1 us
  Pallas kernels: 19.6 us -> 27.8 us
    all_to_all x3 -> x2, blocking collectives: 62.4 us -> 34.2 us  [exchange(): lax.all_to_all(array, axis_name, split_axis=0, concat_axis=0, tiled=True)]
    ppermute x0 -> x15, waiting for transfers between devices: none -> 21.6 us  [send(): return lax.ppermute(array, 'seq', [(i, over(i, *by)) for i in range(count)])]
    dot_general x4 -> x0, matrix products: 18 us -> none  [the longest x1 7.1 us: learn_tokens(): jnp.dot(frames.reshape(-1, width_all), map_weight, preferred_element_type...]
    ppermute x0 -> x15, starting transfers between devices: none -> 12.4 us  [send(): return lax.ppermute(array, 'seq', [(i, over(i, *by)) for i in range(count)])]
    pallas_call x1 -> x2, Pallas kernels: 19.6 us -> 27.8 us  [the longest x1 18.3 us: head_gradient(): pl.pallas_call(functools.partial(head_kernel, 256), out_shape=jax.ShapeDt...]
    all_to_all x1, waiting for transfers between devices: 2.5 us -> 5.75 us  [exchange(): lax.all_to_all(array, axis_name, split_axis=0, concat_axis=0, tiled=True)]
    dynamic_slice x0 -> x1, local copies, waits for them, and re-layouts: none -> 2.33 us  [body(): lax.dynamic_slice_in_dim(qkv_weight, lax.axis_index('seq') * columns, col...]
    convert_element_type x3 -> x0, local copies, waits for them, and re-layouts: 2.32 us -> none  [the longest x1 1.43 us: body(): return whole.reshape(term.shape).astype(F32)]
  transfers between devices with their start and end apart: 2 -> 16, of which waited for: 1 -> 6; matrix products, arithmetic and copies ran while one was open for 5% -> 2% of each run, Pallas kernels for 15% -> 0%
where the time goes in v3:
time: 111 us; the launch traced here: 110 us
  blocking collectives  34.2 us (31%)
  Pallas kernels  27.8 us (25%)
  waiting for transfers between devices  27.4 us (25%)
  starting transfers between devices  16.1 us (15%)
  local copies, waits for them, and re-layouts  3.45 us (3%)
  other arithmetic  1.2 us (1%)
    all_to_all x2, blocking collectives, exchange(): lax.all_to_all(array, axis_name, split_axis=0, concat_axis=0, tiled=True)  34.2 us
    ppermute x15, waiting for transfers between devices, send(): return lax.ppermute(array, 'seq', [(i, over(i, *by)) for i in range(count)])  21.6 us
    pallas_call x1, Pallas kernels, head_gradient(): pl.pallas_call(functools.partial(head_kernel, 256), out_shape=jax.ShapeDt...  18.3 us
    ppermute x15, starting transfers between devices, send(): return lax.ppermute(array, 'seq', [(i, over(i, *by)) for i in range(count)])  12.4 us
    pallas_call x1, Pallas kernels, learn_tokens(): pl.pallas_call(functools.partial(tokens_kernel, group), out_shape=(jax.Sh...  9.46 us
    all_to_all x1, waiting for transfers between devices, exchange(): lax.all_to_all(array, axis_name, split_axis=0, concat_axis=0, tiled=True)  5.75 us
    all_to_all x1, starting transfers between devices, exchange(): lax.all_to_all(array, axis_name, split_axis=0, concat_axis=0, tiled=True)  3.72 us
    dynamic_slice x1, local copies, waits for them, and re-layouts, body(): lax.dynamic_slice_in_dim(qkv_weight, lax.axis_index('seq') * columns, col...  2.33 us
  transfers between devices with their start and end apart: 16, of which 6 were waited for; matrix products, arithmetic and copies ran while one was open for 2% of the time, Pallas kernels for 0%

profile of v3, /device:TPU:0, one launch (start us, length us, event | category | flops | bytes accessed | tf_op | source)
XLA Modules:
  0.0 110.4 jit_solution(10975458882782992211)
XLA Ops:
  0.0 9.5 %learn_tokens.1 = (bf16[128,1280]{1,0:T(8,128)(2,1)}, bf16[16,80,128]{2,1,0:T(8,128)(2,1)}) custom-call(bf16[16,256,1280]{2,1,0:T(8,128)(2,1)} %bitcast.23, bf16[8,1280]{1,0:T(8,128)(2,1)} %bitcast.27, bf16[128,1280]{1,0:T(8,128)(2,1)} %bitcast.26), custom_call_target="tpu_custom_call" | custom-call | tf_op jit(solution)/shard_map/learn_tokens/pallas_call | solution.py:59
  9.5 2.1 %collective-permute-start = (bf16[128,1280]{1,0:T(8,128)(2,1)}, bf16[128,1280]{1,0:T(8,128)(2,1)S(1)}, u32[]{:S(2)}, u32[]{:S(2)}) collective-permute-start(bf16[128,1280]{1,0:T(8,128)(2,1)} %get-tuple-element.8.refs_0_), channel_id=1, source_target_pairs={{0,8},{1,9},{2,10},{3,11},{4,12},{5,13},{6,14},{7,15},{8,0},{9,1},... | collective-permute-start | bytes 983048 | tf_op jit(solution)/shard_map/ppermute | solution.py:211
  11.6 2.8 %collective-permute-start.2 = (bf16[128,1280]{1,0:T(8,128)(2,1)}, bf16[128,1280]{1,0:T(8,128)(2,1)S(1)}, u32[]{:S(2)}, u32[]{:S(2)}) collective-permute-start(bf16[128,1280]{1,0:T(8,128)(2,1)} %get-tuple-element.8.refs_0_), channel_id=1, source_target_pairs={{0,6},{1,7},{2,0},{3,1},{4,2},{5,3},{6,4},{7,5},{8,14},{9,15},{10,... | collective-permute-start | bytes 983048 | tf_op jit(solution)/shard_map/ppermute | solution.py:211
  14.3 0.0 collective-permute-start.1
  14.3 0.0 collective-permute-start.7
  14.3 5.2 %collective-permute-done.refs_1_ = bf16[128,1280]{1,0:T(8,128)(2,1)S(1)} collective-permute-done((bf16[128,1280]{1,0:T(8,128)(2,1)}, bf16[128,1280]{1,0:T(8,128)(2,1)S(1)}, u32[]{:S(2)}, u32[]{:S(2)}) %collective-permute-start) | collective-permute-done | bytes 327712 | tf_op jit(solution)/shard_map/ppermute | solution.py:211
  19.5 2.8 %collective-permute-start.4 = (bf16[128,1280]{1,0:T(8,128)(2,1)S(1)}, bf16[128,1280]{1,0:T(8,128)(2,1)S(1)}, u32[]{:S(2)}, u32[]{:S(2)}) collective-permute-start(bf16[128,1280]{1,0:T(8,128)(2,1)S(1)} %collective-permute-done.refs_1_), channel_id=1, source_target_pairs={{0,6},{1,7},{2,0},{3,1},{4,2},{5,3},{6,4},{7,5},{8,14},{9,15},{10,... | collective-permute-start | bytes 983048 | tf_op jit(solution)/shard_map/ppermute | solution.py:211
  22.2 0.0 collective-permute-done.2.refs_3_
  22.2 0.0 collective-permute-start.10
  22.2 2.4 %collective-permute-done.1.refs_2_ = bf16[128,1280]{1,0:T(8,128)(2,1)S(1)} collective-permute-done((bf16[128,1280]{1,0:T(8,128)(2,1)}, bf16[128,1280]{1,0:T(8,128)(2,1)S(1)}, u32[]{:S(2)}, u32[]{:S(2)}) %collective-permute-start.1) | collective-permute-done | bytes 327712 | tf_op jit(solution)/shard_map/ppermute | solution.py:211
  24.6 0.0 collective-permute-start.9
  24.6 0.0 collective-permute-start.5
  24.6 0.0 collective-permute-done.7.refs_8_
  24.6 0.0 copy-start.1
  24.6 0.1 collective-permute-start.3
  24.7 3.8 %collective-permute-done.4.refs_5_ = bf16[128,1280]{1,0:T(8,128)(2,1)S(1)} collective-permute-done((bf16[128,1280]{1,0:T(8,128)(2,1)S(1)}, bf16[128,1280]{1,0:T(8,128)(2,1)S(1)}, u32[]{:S(2)}, u32[]{:S(2)}) %collective-permute-start.4) | collective-permute-done | bytes 327712 | tf_op jit(solution)/shard_map/ppermute | solution.py:211
  28.5 3.7 %collective-permute-start.6 = (bf16[128,1280]{1,0:T(8,128)(2,1)S(1)}, bf16[128,1280]{1,0:T(8,128)(2,1)}, u32[]{:S(2)}, u32[]{:S(2)}) collective-permute-start(bf16[128,1280]{1,0:T(8,128)(2,1)S(1)} %collective-permute-done.4.refs_5_), channel_id=1, source_target_pairs={{0,6},{1,7},{2,0},{3,1},{4,2},{5,3},{6,4},{7,5},{8,14},{9,15},{10,... | collective-permute-start | bytes 983048 | tf_op jit(solution)/shard_map/ppermute | solution.py:211
  32.2 0.0 collective-permute-done.10.refs_11_
  32.2 0.0 collective-permute-start.8
  32.2 0.0 collective-permute-done.9.refs_10_
  32.2 0.0 copy-start.4
  32.3 0.5 collective-permute-start.12
  32.7 3.6 %collective-permute-done.5.refs_6_ = bf16[128,1280]{1,0:T(8,128)(2,1)S(1)} collective-permute-done((bf16[128,1280]{1,0:T(8,128)(2,1)S(1)}, bf16[128,1280]{1,0:T(8,128)(2,1)S(1)}, u32[]{:S(2)}, u32[]{:S(2)}) %collective-permute-start.5) | collective-permute-done | bytes 327712 | tf_op jit(solution)/shard_map/ppermute | solution.py:211
  36.3 0.0 collective-permute-start.13
  36.3 6.6 %collective-permute-done.3.refs_4_ = bf16[128,1280]{1,0:T(8,128)(2,1)S(1)} collective-permute-done((bf16[128,1280]{1,0:T(8,128)(2,1)S(1)}, bf16[128,1280]{1,0:T(8,128)(2,1)S(1)}, u32[]{:S(2)}, u32[]{:S(2)}) %collective-permute-start.3) | collective-permute-done | bytes 327712 | tf_op jit(solution)/shard_map/ppermute | solution.py:211
  43.0 0.0 collective-permute-start.11
  43.0 0.0 collective-permute-done.6.refs_7_
  43.0 0.5 collective-permute-start.14
  43.5 3.7 %all-to-all-start = ((bf16[16,80,128]{2,1,0:T(8,128)(2,1)}), bf16[16,80,128]{2,1,0:T(8,128)(2,1)S(1)}, u32[]{:S(2)}, u32[]{:S(2)}) async-start(bf16[16,80,128]{2,1,0:T(8,128)(2,1)} %get-tuple-element.7), calls=%async_computation | async-start | bytes 655360 | tf_op jit(solution)/shard_map/all_to_all | solution.py:196
  47.4 0.1 stack.67.order_ref
  47.5 2.3 %constant_dynamic-slice_fusion.weight_ref = bf16[1280,240]{1,0:T(8,128)(2,1)} fusion(bf16[1280,3840]{1,0:T(8,128)(2,1)} %param.6, s32[]{:T(128)S(6)} %select_n.162), kind=kLoop, calls=%fused_computation.1 | loop fusion | bytes 1228804 | tf_op jit(solution)/shard_map/dynamic_slice | solution.py:232
  49.8 5.8 %all-to-all-done.cot_ref = bf16[16,80,128]{2,1,0:T(8,128)(2,1)S(1)} async-done(((bf16[16,80,128]{2,1,0:T(8,128)(2,1)}), bf16[16,80,128]{2,1,0:T(8,128)(2,1)S(1)}, u32[]{:S(2)}, u32[]{:S(2)}) %all-to-all-start) | async-done | bytes 327712 | tf_op jit(solution)/shard_map/all_to_all | solution.py:196
  55.6 0.0 collective-permute-done.8.refs_9_
  55.6 0.0 collective-permute-done.13.refs_14_
  55.6 0.0 collective-permute-done.12.refs_13_
  55.6 0.0 collective-permute-done.11.refs_12_
  55.6 0.0 collective-permute-done.14.refs_15_
  55.6 0.0 copy-done.1
  55.6 0.0 copy-done.2
  55.6 0.0 copy-done.3
  55.6 0.0 copy-done.4
  55.6 0.0 copy-done.5
  55.7 1.0 copy-done
  56.6 18.3 %head_gradient.1 = bf16[256,1280]{1,0:T(8,128)(2,1)} custom-call(s32[16]{0:T(128)S(1)} %stack.67.order_ref, bf16[16,80,128]{2,1,0:T(8,128)(2,1)S(1)} %all-to-all-done.cot_ref, bf16[1280,240]{1,0:T(8,128)(2,1)} %constant_dynamic-slice_fusion.weight_ref, bf16[128,1280]{1,0:T(8,128)(2,1)S(1)} %copy-done, bf16[128,1280]{1,0:T(8,128)(2,1)S(1)} %collective-permute-done.refs_1_, ...), custom_call_target="tpu_custom_call" | custom-call | flops 6442450944 | bytes 8388608 | tf_op jit(solution)/shard_map/head_gradient/pallas_call | solution.py:172
  74.9 20.0 %all_to_all.15 = bf16[8,32,1280]{2,1,0:T(8,128)(2,1)S(1)} all-to-all(bf16[8,32,1280]{2,1,0:T(8,128)(2,1)} %bitcast.25), channel_id=1, replica_groups=mesh['dp'=8,'seq'=16] {'dp'}, dimensions={0} | all-to-all | bytes 1310720 | tf_op jit(solution)/shard_map/all_to_all | solution.py:196
  94.9 0.1 reduce_sum.12
  95.1 14.3 %all_to_all.16 = bf16[8,32,1280]{2,1,0:T(8,128)(2,1)S(1)} all-to-all(bf16[8,32,1280]{2,1,0:T(8,128)(2,1)S(1)} %broadcast_in_dim.2), channel_id=1, replica_groups=mesh['dp'=8,'seq'=16] {'dp'}, dimensions={0} | all-to-all | bytes 1310720 | tf_op jit(solution)/shard_map/all_to_all | solution.py:196
  109.3 1.1 %convert_bitcast_fusion = f32[1280,240]{0,1:T(8,128)} fusion(bf16[256,1280]{1,0:T(8,128)(2,1)S(1)} %bitcast.24), kind=kLoop, calls=%fused_computation | loop fusion | flops 307200 | bytes 1843200 | tf_op jit(solution)/shard_map/transpose | solution.py:237
  (5 shorter events, 0.1 us)
Async XLA Ops:
  9.5 10.0 %collective-permute-start = (bf16[128,1280]{1,0:T(8,128)(2,1)}, bf16[128,1280]{1,0:T(8,128)(2,1)S(1)}, u32[]{:S(2)}, u32[]{:S(2)}) collective-permute-start(bf16[128,1280]{1,0:T(8,128)(2,1)} %get-tuple-element.8.refs_0_), channel_id=1, source_target_pairs={{0,8},{1,9},{2,10},{3,11},{4,12},{5,13},{6,14},{7,15},{8,0},{9,1},... | collective-permute-start | bytes 983048 | tf_op jit(solution)/shard_map/ppermute | solution.py:211
  11.6 10.7 %collective-permute-start.2 = (bf16[128,1280]{1,0:T(8,128)(2,1)}, bf16[128,1280]{1,0:T(8,128)(2,1)S(1)}, u32[]{:S(2)}, u32[]{:S(2)}) collective-permute-start(bf16[128,1280]{1,0:T(8,128)(2,1)} %get-tuple-element.8.refs_0_), channel_id=1, source_target_pairs={{0,6},{1,7},{2,0},{3,1},{4,2},{5,3},{6,4},{7,5},{8,14},{9,15},{10,... | collective-permute-start | bytes 983048 | tf_op jit(solution)/shard_map/ppermute | solution.py:211
  14.3 10.3 %collective-permute-start.1 = (bf16[128,1280]{1,0:T(8,128)(2,1)}, bf16[128,1280]{1,0:T(8,128)(2,1)S(1)}, u32[]{:S(2)}, u32[]{:S(2)}) collective-permute-start(bf16[128,1280]{1,0:T(8,128)(2,1)} %get-tuple-element.8.refs_0_), channel_id=1, source_target_pairs={{0,2},{1,3},{2,4},{3,5},{4,6},{5,7},{6,0},{7,1},{8,10},{9,11},{10,... | collective-permute-start | bytes 983048 | tf_op jit(solution)/shard_map/ppermute | solution.py:211
  14.3 10.3 %collective-permute-start.7 = (bf16[128,1280]{1,0:T(8,128)(2,1)}, bf16[128,1280]{1,0:T(8,128)(2,1)S(1)}, u32[]{:S(2)}, u32[]{:S(2)}) collective-permute-start(bf16[128,1280]{1,0:T(8,128)(2,1)} %get-tuple-element.8.refs_0_), channel_id=1, source_target_pairs={{0,1},{1,0},{2,3},{3,2},{4,5},{5,4},{6,7},{7,6},{8,9},{9,8},{10,11... | collective-permute-start | bytes 983048 | tf_op jit(solution)/shard_map/ppermute | solution.py:211
  19.5 9.1 %collective-permute-start.4 = (bf16[128,1280]{1,0:T(8,128)(2,1)S(1)}, bf16[128,1280]{1,0:T(8,128)(2,1)S(1)}, u32[]{:S(2)}, u32[]{:S(2)}) collective-permute-start(bf16[128,1280]{1,0:T(8,128)(2,1)S(1)} %collective-permute-done.refs_1_), channel_id=1, source_target_pairs={{0,6},{1,7},{2,0},{3,1},{4,2},{5,3},{6,4},{7,5},{8,14},{9,15},{10,... | collective-permute-start | bytes 983048 | tf_op jit(solution)/shard_map/ppermute | solution.py:211
  22.2 10.0 %collective-permute-start.10 = (bf16[128,1280]{1,0:T(8,128)(2,1)S(1)}, bf16[128,1280]{1,0:T(8,128)(2,1)S(1)}, u32[]{:S(2)}, u32[]{:S(2)}) collective-permute-start(bf16[128,1280]{1,0:T(8,128)(2,1)S(1)} %collective-permute-done.2.refs_3_), channel_id=1, source_target_pairs={{0,1},{1,0},{2,3},{3,2},{4,5},{5,4},{6,7},{7,6},{8,9},{9,8},{10,11... | collective-permute-start | bytes 983048 | tf_op jit(solution)/shard_map/ppermute | solution.py:211
  24.6 7.6 %collective-permute-start.9 = (bf16[128,1280]{1,0:T(8,128)(2,1)S(1)}, bf16[128,1280]{1,0:T(8,128)(2,1)S(1)}, u32[]{:S(2)}, u32[]{:S(2)}) collective-permute-start(bf16[128,1280]{1,0:T(8,128)(2,1)S(1)} %collective-permute-done.1.refs_2_), channel_id=1, source_target_pairs={{0,1},{1,0},{2,3},{3,2},{4,5},{5,4},{6,7},{7,6},{8,9},{9,8},{10,11... | collective-permute-start | bytes 983048 | tf_op jit(solution)/shard_map/ppermute | solution.py:211
  24.6 11.7 %collective-permute-start.5 = (bf16[128,1280]{1,0:T(8,128)(2,1)S(1)}, bf16[128,1280]{1,0:T(8,128)(2,1)S(1)}, u32[]{:S(2)}, u32[]{:S(2)}) collective-permute-start(bf16[128,1280]{1,0:T(8,128)(2,1)S(1)} %collective-permute-done.1.refs_2_), channel_id=1, source_target_pairs={{0,2},{1,3},{2,4},{3,5},{4,6},{5,7},{6,0},{7,1},{8,10},{9,11},{10,... | collective-permute-start | bytes 983048 | tf_op jit(solution)/shard_map/ppermute | solution.py:211
  24.6 31.0 %copy-start.1 = (bf16[128,1280]{1,0:T(8,128)(2,1)}, bf16[128,1280]{1,0:T(8,128)(2,1)S(1)}, u32[]{:S(2)}) copy-start(bf16[128,1280]{1,0:T(8,128)(2,1)S(1)} %collective-permute-done.7.refs_8_) | copy-start | bytes 983044
  24.6 18.4 %collective-permute-start.3 = (bf16[128,1280]{1,0:T(8,128)(2,1)S(1)}, bf16[128,1280]{1,0:T(8,128)(2,1)S(1)}, u32[]{:S(2)}, u32[]{:S(2)}) collective-permute-start(bf16[128,1280]{1,0:T(8,128)(2,1)S(1)} %collective-permute-done.refs_1_), channel_id=1, source_target_pairs={{0,2},{1,3},{2,4},{3,5},{4,6},{5,7},{6,0},{7,1},{8,10},{9,11},{10,... | collective-permute-start | bytes 983048 | tf_op jit(solution)/shard_map/ppermute | solution.py:211
  28.5 27.1 %copy-start.2 = (bf16[128,1280]{1,0:T(8,128)(2,1)}, bf16[128,1280]{1,0:T(8,128)(2,1)S(1)}, u32[]{:S(2)}) copy-start(bf16[128,1280]{1,0:T(8,128)(2,1)S(1)} %collective-permute-done.4.refs_5_) | copy-start | bytes 983044
  28.5 14.5 %collective-permute-start.6 = (bf16[128,1280]{1,0:T(8,128)(2,1)S(1)}, bf16[128,1280]{1,0:T(8,128)(2,1)}, u32[]{:S(2)}, u32[]{:S(2)}) collective-permute-start(bf16[128,1280]{1,0:T(8,128)(2,1)S(1)} %collective-permute-done.4.refs_5_), channel_id=1, source_target_pairs={{0,6},{1,7},{2,0},{3,1},{4,2},{5,3},{6,4},{7,5},{8,14},{9,15},{10,... | collective-permute-start | bytes 983048 | tf_op jit(solution)/shard_map/ppermute | solution.py:211
  32.2 23.4 %copy-start.3 = (bf16[128,1280]{1,0:T(8,128)(2,1)}, bf16[128,1280]{1,0:T(8,128)(2,1)S(1)}, u32[]{:S(2)}) copy-start(bf16[128,1280]{1,0:T(8,128)(2,1)S(1)} %collective-permute-done.10.refs_11_) | copy-start | bytes 983044
  32.2 23.3 %collective-permute-start.8 = (bf16[128,1280]{1,0:T(8,128)(2,1)S(1)}, bf16[128,1280]{1,0:T(8,128)(2,1)}, u32[]{:S(2)}, u32[]{:S(2)}) collective-permute-start(bf16[128,1280]{1,0:T(8,128)(2,1)S(1)} %collective-permute-done.refs_1_), channel_id=1, source_target_pairs={{0,1},{1,0},{2,3},{3,2},{4,5},{5,4},{6,7},{7,6},{8,9},{9,8},{10,11... | collective-permute-start | bytes 983048 | tf_op jit(solution)/shard_map/ppermute | solution.py:211
  32.2 23.4 %copy-start.4 = (bf16[128,1280]{1,0:T(8,128)(2,1)}, bf16[128,1280]{1,0:T(8,128)(2,1)S(1)}, u32[]{:S(2)}) copy-start(bf16[128,1280]{1,0:T(8,128)(2,1)S(1)} %collective-permute-done.9.refs_10_) | copy-start | bytes 983044
  32.3 23.3 %collective-permute-start.12 = (bf16[128,1280]{1,0:T(8,128)(2,1)S(1)}, bf16[128,1280]{1,0:T(8,128)(2,1)}, u32[]{:S(2)}, u32[]{:S(2)}) collective-permute-start(bf16[128,1280]{1,0:T(8,128)(2,1)S(1)} %collective-permute-done.4.refs_5_), channel_id=1, source_target_pairs={{0,1},{1,0},{2,3},{3,2},{4,5},{5,4},{6,7},{7,6},{8,9},{9,8},{10,11... | collective-permute-start | bytes 983048 | tf_op jit(solution)/shard_map/ppermute | solution.py:211
  36.3 19.3 %copy-start.5 = (bf16[128,1280]{1,0:T(8,128)(2,1)}, bf16[128,1280]{1,0:T(8,128)(2,1)S(1)}, u32[]{:S(2)}) copy-start(bf16[128,1280]{1,0:T(8,128)(2,1)S(1)} %collective-permute-done.5.refs_6_) | copy-start | bytes 983044
  36.3 19.2 %collective-permute-start.13 = (bf16[128,1280]{1,0:T(8,128)(2,1)S(1)}, bf16[128,1280]{1,0:T(8,128)(2,1)}, u32[]{:S(2)}, u32[]{:S(2)}) collective-permute-start(bf16[128,1280]{1,0:T(8,128)(2,1)S(1)} %collective-permute-done.5.refs_6_), channel_id=1, source_target_pairs={{0,1},{1,0},{2,3},{3,2},{4,5},{5,4},{6,7},{7,6},{8,9},{9,8},{10,11... | collective-permute-start | bytes 983048 | tf_op jit(solution)/shard_map/ppermute | solution.py:211
  43.0 12.6 %collective-permute-start.11 = (bf16[128,1280]{1,0:T(8,128)(2,1)S(1)}, bf16[128,1280]{1,0:T(8,128)(2,1)}, u32[]{:S(2)}, u32[]{:S(2)}) collective-permute-start(bf16[128,1280]{1,0:T(8,128)(2,1)S(1)} %collective-permute-done.3.refs_4_), channel_id=1, source_target_pairs={{0,1},{1,0},{2,3},{3,2},{4,5},{5,4},{6,7},{7,6},{8,9},{9,8},{10,11... | collective-permute-start | bytes 983048 | tf_op jit(solution)/shard_map/ppermute | solution.py:211
  43.0 12.6 %collective-permute-start.14 = (bf16[128,1280]{1,0:T(8,128)(2,1)}, bf16[128,1280]{1,0:T(8,128)(2,1)}, u32[]{:S(2)}, u32[]{:S(2)}) collective-permute-start(bf16[128,1280]{1,0:T(8,128)(2,1)} %collective-permute-done.6.refs_7_), channel_id=1, source_target_pairs={{0,1},{1,0},{2,3},{3,2},{4,5},{5,4},{6,7},{7,6},{8,9},{9,8},{10,11... | collective-permute-start | bytes 983048 | tf_op jit(solution)/shard_map/ppermute | solution.py:211
  43.5 12.0 %all-to-all-start = ((bf16[16,80,128]{2,1,0:T(8,128)(2,1)}), bf16[16,80,128]{2,1,0:T(8,128)(2,1)S(1)}, u32[]{:S(2)}, u32[]{:S(2)}) async-start(bf16[16,80,128]{2,1,0:T(8,128)(2,1)} %get-tuple-element.7), calls=%async_computation | async-start | bytes 655360 | tf_op jit(solution)/shard_map/all_to_all | solution.py:196
  55.6 1.0 copy-start

commit v4 on v3

--- a/solution.py
+++ b/solution.py
@@ -24,40 +24,52 @@
     return high, middle, (rest - middle.astype(F32)).astype(BF16)
 
 
-def tokens_kernel(group, frames, map_weight, cot, normed, send, held, map_weight_t, cot_held, sems, own_sems):
+def tokens_kernel(
+    group, ahead, frames, map_weight, cot, normed, send, held, map_weight_t, cot_held, pooled, sems, own_sems
+):
     count = frames.shape[0]
     slots = map_weight_t.shape[0]
-    parts = [pl.ds(g * group, group) for g in range(count // group)]
+    step = count // sems.shape[0]
+    parts = [pl.ds(i * step, step) for i in range(sems.shape[0])]
     loads = [
-        pltpu.make_async_copy(frames.at[part], held.at[part], sems.at[g])
-        for g, part in enumerate(parts)
+        pltpu.make_async_copy(frames.at[part], held.at[part], sems.at[i])
+        for i, part in enumerate(parts)
     ]
     map_load = pltpu.make_async_copy(map_weight, map_weight_t, own_sems.at[0])
     cot_load = pltpu.make_async_copy(cot, cot_held, own_sems.at[1])
-    for load in (map_load, cot_load, *loads):
+    map_load.start()
+    waiting = loads + [cot_load]
+    for load in waiting[:ahead]:
         load.start()
+    waiting = waiting[ahead:]
     map_load.wait()
-    cot_load.wait()
-    send[...] = cot_held[...].T.reshape(send.shape)
-    for g, load in enumerate(loads):
-        load.wait()
+    for g in range(count // group):
+        for load in loads[g * group // step : (g + 1) * group // step]:
+            load.wait()
+            if waiting:
+                waiting.pop(0).start()
         blocks = [held[g * group + k] for k in range(group)]
         logits = [matmul(map_weight_t[...], block, ((1,), (1,))) for block in blocks]
         maps = [jax.nn.sigmoid(l).astype(BF16) for l in logits]
-        pooled = jnp.concatenate([matmul(m, block) for m, block in zip(maps, blocks)], axis=0)
-        centred = pooled - jnp.mean(pooled, axis=-1, keepdims=True)
-        variance = jnp.mean(centred * centred, axis=-1, keepdims=True)
         at = g * group * slots
-        normed[at : at + group * slots, :] = (centred * lax.rsqrt(variance + 1e-06)).astype(BF16)
+        pooled[at : at + group * slots, :] = jnp.concatenate(
+            [matmul(m, block) for m, block in zip(maps, blocks)], axis=0
+        )
+    for load in waiting:
+        load.start()
+    centred = pooled[...] - jnp.mean(pooled[...], axis=-1, keepdims=True)
+    variance = jnp.mean(centred * centred, axis=-1, keepdims=True)
+    normed[...] = (centred * lax.rsqrt(variance + 1e-06)).astype(BF16)
+    cot_load.wait()
+    send[...] = cot_held[...].T.reshape(send.shape)
 
 
 def learn_tokens(frames, map_weight, cot, heads):
     count = frames.shape[0]
     tokens, width = cot.shape
-    group = math.gcd(count, 4)
     vmem, hbm = pl.BlockSpec(memory_space=pltpu.VMEM), pl.BlockSpec(memory_space=pltpu.HBM)
     return pl.pallas_call(
-        functools.partial(tokens_kernel, group),
+        functools.partial(tokens_kernel, math.gcd(count, 4), 4),
         out_shape=(
             jax.ShapeDtypeStruct((tokens, width), BF16),
             jax.ShapeDtypeStruct((heads, width // heads, tokens), BF16),
@@ -68,7 +80,8 @@
             pltpu.VMEM(frames.shape, BF16),
             pltpu.VMEM(map_weight.shape[::-1], BF16),
             pltpu.VMEM(cot.shape, BF16),
-            pltpu.SemaphoreType.DMA((count // group,)),
+            pltpu.VMEM(cot.shape, F32),
+            pltpu.SemaphoreType.DMA((count // math.gcd(count, 2),)),
             pltpu.SemaphoreType.DMA((2,)),
         ],
         compiler_params=pltpu.CompilerParams(vmem_limit_bytes=62 << 20),
@@ -79,18 +92,25 @@
 def head_kernel(sub, order_ref, cot_ref, weight_ref, *refs):
     pieces = cot_ref.shape[0]
     chunks, out_ref = refs[:pieces], refs[pieces]
-    x, k3, v1, grads, query_scaled, cot_scaled, shifted_all, scores_all = refs[pieces + 1 :]
+    held, sems, x, k3, v1, grads, query_scaled, cot_scaled, shifted_all, scores_all = refs[pieces + 1 :]
     hd = HEAD_DIM
     scale = 1.0 / math.sqrt(hd)
     width = cot_ref.shape[2]
     count = pieces * width
     join = 4
-    for at in range(0, pieces, join):
-        tokens = jnp.concatenate([chunk[...] for chunk in chunks[at : at + join]], axis=0)
-        columns = slice(at * width, (at + join) * width)
-        x[0 : 3 * hd, columns] = matmul(tokens, weight_ref[...]).T.astype(BF16)
+    loads = [
+        pltpu.make_async_copy(chunk, held.at[pl.ds(i * width, width)], sems.at[i])
+        for i, chunk in enumerate(chunks)
+    ]
+    for load in loads:
+        load.start()
     for piece in range(pieces):
         x[3 * hd :, piece * width : (piece + 1) * width] = cot_ref[order_ref[piece]]
+    for at in range(0, pieces, join):
+        for load in loads[at : at + join]:
+            load.wait()
+        columns = slice(at * width, (at + join) * width)
+        x[0 : 3 * hd, columns] = matmul(held[columns, :], weight_ref[...]).T.astype(BF16)
     key = x[hd : 2 * hd, :]
     k3[...] = jnp.concatenate([key, key, key], axis=0)
     row = lax.broadcasted_iota(jnp.int32, (LANES - hd, count), 0)
@@ -157,12 +177,7 @@
     grads[hd : 2 * hd, :] = matmul(query_scaled[...], scores_all[...]).astype(BF16)
     grads[2 * hd : 3 * hd, :] = matmul(cot_scaled[...], shifted_all[...]).astype(BF16)
     grads[3 * hd :, :] = jnp.zeros((grads.shape[0] - 3 * hd, count), BF16)
-    total = None
-    for at in range(0, pieces, join):
-        tokens = jnp.concatenate([chunk[...] for chunk in chunks[at : at + join]], axis=0)
-        term = matmul(grads[:, at * width : (at + join) * width], tokens)
-        total = term if total is None else total + term
-    out_ref[...] = total.astype(BF16)
+    out_ref[...] = matmul(grads[...], held[...]).astype(BF16)
 
 
 def head_gradient(order, cot, weight, chunks, rows):
@@ -172,9 +187,11 @@
     return pl.pallas_call(
         functools.partial(head_kernel, 256),
         out_shape=jax.ShapeDtypeStruct((rows, chunks[0].shape[1]), BF16),
-        in_specs=[pl.BlockSpec(memory_space=pltpu.SMEM)] + [vmem] * (2 + pieces),
+        in_specs=[pl.BlockSpec(memory_space=pltpu.SMEM)] + [vmem] * 2 + [pl.BlockSpec(memory_space=pl.ANY)] * pieces,
         out_specs=vmem,
         scratch_shapes=[
+            pltpu.VMEM((count, chunks[0].shape[1]), BF16),
+            pltpu.SemaphoreType.DMA((pieces,)),
             pltpu.VMEM((4 * HEAD_DIM, count), BF16),
             pltpu.VMEM((3 * HEAD_DIM, count), BF16),
             pltpu.VMEM((LANES, count), BF16),
@@ -184,7 +201,7 @@
             pltpu.VMEM((count, count), BF16),
             pltpu.VMEM((count, count), BF16),
         ],
-        compiler_params=pltpu.CompilerParams(vmem_limit_bytes=52 << 20),
+        compiler_params=pltpu.CompilerParams(vmem_limit_bytes=48 << 20),
         cost_estimate=pl.CostEstimate(
             flops=12 * count * count * LANES, bytes_accessed=8 << 20, transcendentals=count * count
         ),
@@ -199,7 +216,7 @@
 RING, CORES = 4, 2
 
 
-def gather_pieces(own):
+def gather_pieces(own, weight, cot):
     count = lax.axis_size("seq")
     me = lax.axis_index("seq")
 
@@ -213,14 +230,16 @@
     right, left = send(own, 0, 1, 0), send(own, 0, -1, 0)
     other = send(own, 1, 0, 0)
     other_right, other_left = send(other, 0, 1, 0), send(other, 0, -1, 0)
+    right, weight = lax.optimization_barrier((right, weight))
     across, other_across = send(right, 0, 1, 0), send(other_left, 0, -1, 0)
+    across, cot = lax.optimization_barrier((across, exchange(cot, "seq")))
     near = [own, other, right, left, other_right, other_left, across, other_across]
     places = [(0, 0), (1, 0), (0, -1), (0, 1), (1, -1), (1, 1), (0, -2), (1, 2)]
     pieces, order = list(near), [over(me, dz, dx, 0) for dz, dx in places]
     for array, (dz, dx) in zip(near, places):
         pieces.append(send(array, 0, 0, 1))
         order.append(over(me, dz, dx, 1))
-    return pieces, jnp.stack(order).astype(jnp.int32)
+    return pieces, jnp.stack(order).astype(jnp.int32), weight, cot
 
 
 def body(frames, map_weight, qkv_weight, cotangent):
@@ -228,9 +247,9 @@
     columns = qkv_weight.shape[1] // seq
     padded = -(-columns // (16 * dp)) * 16 * dp
     normed, send = learn_tokens(frames[0], map_weight, cotangent[0], seq)
-    pieces, order = gather_pieces(normed)
     own_weight = lax.dynamic_slice_in_dim(qkv_weight, lax.axis_index("seq") * columns, columns, 1)
-    term = head_gradient(order, exchange(send, "seq"), own_weight, pieces, padded)
+    pieces, order, own_weight, cot = gather_pieces(normed, own_weight, send)
+    term = head_gradient(order, cot, own_weight, pieces, padded)
     parts = exchange(term.reshape(dp, -1, term.shape[1]), "dp")
     summed = jnp.sum(parts.astype(F32), axis=0).astype(BF16)
     whole = exchange(jnp.broadcast_to(summed[None], (dp,) + summed.shape), "dp")

time: 111 us -> 106 us (0.955)
  blocking collectives: 34.2 us -> 48 us
  waiting for transfers between devices: 27.4 us -> 14.2 us
  starting transfers between devices: 16.1 us -> 10.4 us
    all_to_all x2 -> x3, blocking collectives: 34.2 us -> 48 us  [exchange(): lax.all_to_all(array, axis_name, split_axis=0, concat_axis=0, tiled=True)]
    ppermute x15, waiting for transfers between devices: 21.6 us -> 14.2 us  [send(): return lax.ppermute(array, 'seq', [(i, over(i, *by)) for i in range(count)])]
    all_to_all x1 -> x0, waiting for transfers between devices: 5.75 us -> none  [exchange(): lax.all_to_all(array, axis_name, split_axis=0, concat_axis=0, tiled=True)]
    all_to_all x1 -> x0, starting transfers between devices: 3.72 us -> none  [exchange(): lax.all_to_all(array, axis_name, split_axis=0, concat_axis=0, tiled=True)]
    ppermute x15, starting transfers between devices: 12.4 us -> 10.4 us  [send(): return lax.ppermute(array, 'seq', [(i, over(i, *by)) for i in range(count)])]
    pallas_call x1, Pallas kernels: 18.3 us -> 20.2 us  [head_gradient(): pl.pallas_call(functools.partial(head_kernel, 256), out_shape=jax.ShapeDt...]
    pallas_call x1, Pallas kernels: 9.46 us -> 7.6 us  [learn_tokens(): pl.pallas_call(functools.partial(tokens_kernel, math.gcd(count, 4), 4), o...]
  transfers between devices with their start and end apart: 16 -> 15, of which waited for: 6 -> 8; matrix products, arithmetic and copies ran while one was open for 2% -> 2% of each run, Pallas kernels for 0% -> 0%
where the time goes in v4:
time: 106 us; the launch traced here: 105 us
  blocking collectives  48 us (45%)
  Pallas kernels  27.8 us (26%)
  waiting for transfers between devices  14.2 us (13%)
  starting transfers between devices  10.4 us (10%)
  local copies, waits for them, and re-layouts  3.42 us (3%)
  other arithmetic  1.2 us (1%)
    all_to_all x3, blocking collectives, exchange(): lax.all_to_all(array, axis_name, split_axis=0, concat_axis=0, tiled=True)  48 us
    pallas_call x1, Pallas kernels, head_gradient(): pl.pallas_call(functools.partial(head_kernel, 256), out_shape=jax.ShapeDt...  20.2 us
    ppermute x15, waiting for transfers between devices, send(): return lax.ppermute(array, 'seq', [(i, over(i, *by)) for i in range(count)])  14.2 us
    ppermute x15, starting transfers between devices, send(): return lax.ppermute(array, 'seq', [(i, over(i, *by)) for i in range(count)])  10.4 us
    pallas_call x1, Pallas kernels, learn_tokens(): pl.pallas_call(functools.partial(tokens_kernel, math.gcd(count, 4), 4), o...  7.6 us
    dynamic_slice x1, local copies, waits for them, and re-layouts, body(): lax.dynamic_slice_in_dim(qkv_weight, lax.axis_index('seq') * columns, col...  2.32 us
  transfers between devices with their start and end apart: 15, of which 8 were waited for; matrix products, arithmetic and copies ran while one was open for 2% of the time, Pallas kernels for 0%

profile of v4, /device:TPU:0, one launch (start us, length us, event | category | flops | bytes accessed | tf_op | source)
XLA Modules:
  0.0 105.2 jit_solution(15128679492473250761)
XLA Ops:
  0.0 7.6 %learn_tokens.1 = (bf16[128,1280]{1,0:T(8,128)(2,1)}, bf16[16,80,128]{2,1,0:T(8,128)(2,1)}) custom-call(bf16[16,256,1280]{2,1,0:T(8,128)(2,1)} %bitcast.23, bf16[8,1280]{1,0:T(8,128)(2,1)} %bitcast.27, bf16[128,1280]{1,0:T(8,128)(2,1)} %bitcast.26), custom_call_target="tpu_custom_call" | custom-call | tf_op jit(solution)/shard_map/learn_tokens/pallas_call | solution.py:71
  7.6 1.6 %collective-permute-start = (bf16[128,1280]{1,0:T(8,128)(2,1)}, bf16[128,1280]{1,0:T(8,128)(2,1)S(1)}, u32[]{:S(2)}, u32[]{:S(2)}) collective-permute-start(bf16[128,1280]{1,0:T(8,128)(2,1)} %get-tuple-element.11.refs_0_), channel_id=1, source_target_pairs={{0,2},{1,3},{2,4},{3,5},{4,6},{5,7},{6,0},{7,1},{8,10},{9,11},{10,... | collective-permute-start | bytes 983048 | tf_op jit(solution)/shard_map/ppermute | solution.py:228
  9.2 1.9 %collective-permute-start.2 = (bf16[128,1280]{1,0:T(8,128)(2,1)}, bf16[128,1280]{1,0:T(8,128)(2,1)S(1)}, u32[]{:S(2)}, u32[]{:S(2)}) collective-permute-start(bf16[128,1280]{1,0:T(8,128)(2,1)} %get-tuple-element.11.refs_0_), channel_id=1, source_target_pairs={{0,8},{1,9},{2,10},{3,11},{4,12},{5,13},{6,14},{7,15},{8,0},{9,1},... | collective-permute-start | bytes 983048 | tf_op jit(solution)/shard_map/ppermute | solution.py:228
  11.2 1.7 %collective-permute-start.3 = (bf16[128,1280]{1,0:T(8,128)(2,1)}, bf16[128,1280]{1,0:T(8,128)(2,1)S(1)}, u32[]{:S(2)}, u32[]{:S(2)}) collective-permute-start(bf16[128,1280]{1,0:T(8,128)(2,1)} %get-tuple-element.11.refs_0_), channel_id=1, source_target_pairs={{0,6},{1,7},{2,0},{3,1},{4,2},{5,3},{6,4},{7,5},{8,14},{9,15},{10,... | collective-permute-start | bytes 983048 | tf_op jit(solution)/shard_map/ppermute | solution.py:228
  12.9 2.3 %constant_dynamic-slice_fusion.weight_ref = bf16[1280,240]{1,0:T(8,128)(2,1)} fusion(bf16[1280,3840]{1,0:T(8,128)(2,1)} %param.6, s32[]{:T(128)S(6)} %select_n.162), kind=kLoop, calls=%fused_computation.1 | loop fusion | bytes 1228804 | tf_op jit(solution)/shard_map/dynamic_slice | solution.py:250
  15.2 3.2 %collective-permute-done.refs_2_ = bf16[128,1280]{1,0:T(8,128)(2,1)S(1)} collective-permute-done((bf16[128,1280]{1,0:T(8,128)(2,1)}, bf16[128,1280]{1,0:T(8,128)(2,1)S(1)}, u32[]{:S(2)}, u32[]{:S(2)}) %collective-permute-start) | collective-permute-done | bytes 327712 | tf_op jit(solution)/shard_map/ppermute | solution.py:228
  18.4 0.4 collective-permute-done.2.refs_1_
  18.8 1.7 %collective-permute-start.5 = (bf16[128,1280]{1,0:T(8,128)(2,1)S(1)}, bf16[128,1280]{1,0:T(8,128)(2,1)S(1)}, u32[]{:S(2)}, u32[]{:S(2)}) collective-permute-start(bf16[128,1280]{1,0:T(8,128)(2,1)S(1)} %collective-permute-done.2.refs_1_), channel_id=1, source_target_pairs={{0,6},{1,7},{2,0},{3,1},{4,2},{5,3},{6,4},{7,5},{8,14},{9,15},{10,... | collective-permute-start | bytes 983048 | tf_op jit(solution)/shard_map/ppermute | solution.py:228
  20.6 0.3 collective-permute-start.1
  20.9 0.0 collective-permute-start.7
  20.9 0.0 collective-permute-done.3.refs_3_
  20.9 0.5 collective-permute-start.10
  21.4 0.0 collective-permute-start.8
  21.4 5.9 %collective-permute-done.5.refs_5_ = bf16[128,1280]{1,0:T(8,128)(2,1)S(1)} collective-permute-done((bf16[128,1280]{1,0:T(8,128)(2,1)S(1)}, bf16[128,1280]{1,0:T(8,128)(2,1)S(1)}, u32[]{:S(2)}, u32[]{:S(2)}) %collective-permute-start.5) | collective-permute-done | bytes 327712 | tf_op jit(solution)/shard_map/ppermute | solution.py:228
  27.3 1.5 %collective-permute-start.4 = (bf16[128,1280]{1,0:T(8,128)(2,1)S(1)}, bf16[128,1280]{1,0:T(8,128)(2,1)S(1)}, u32[]{:S(2)}, u32[]{:S(2)}) collective-permute-start(bf16[128,1280]{1,0:T(8,128)(2,1)S(1)} %collective-permute-done.2.refs_1_), channel_id=1, source_target_pairs={{0,2},{1,3},{2,4},{3,5},{4,6},{5,7},{6,0},{7,1},{8,10},{9,11},{10,... | collective-permute-start | bytes 983048 | tf_op jit(solution)/shard_map/ppermute | solution.py:228
  28.8 2.0 %collective-permute-done.1.refs_6_ = bf16[128,1280]{1,0:T(8,128)(2,1)S(1)} collective-permute-done((bf16[128,1280]{1,0:T(8,128)(2,1)S(1)}, bf16[128,1280]{1,0:T(8,128)(2,1)S(1)}, u32[]{:S(2)}, u32[]{:S(2)}) %collective-permute-start.1) | collective-permute-done | bytes 327712 | tf_op jit(solution)/shard_map/ppermute | solution.py:228
  30.8 0.0 collective-permute-start.6
  30.9 12.7 %all_to_all.15.cot_ref = bf16[16,80,128]{2,1,0:T(8,128)(2,1)S(1)} all-to-all(bf16[16,80,128]{2,1,0:T(8,128)(2,1)} %get-tuple-element.13), channel_id=1, replica_groups=mesh['dp'=8,'seq'=16] {'seq'}, dimensions={0} | all-to-all | bytes 655360 | tf_op jit(solution)/shard_map/all_to_all | solution.py:213
  43.6 0.0 collective-permute-done.7.refs_8_
  43.6 0.0 collective-permute-start.9
  43.6 0.0 collective-permute-done.10.refs_11_
  43.6 0.5 collective-permute-start.13
  44.1 0.0 collective-permute-done.8.refs_9_
  44.1 0.1 collective-permute-start.12
  44.2 0.0 collective-permute-done.4.refs_4_
  44.2 0.4 collective-permute-start.11
  44.6 0.0 collective-permute-done.6.refs_7_
  44.6 0.1 collective-permute-start.14
  44.7 0.1 stack.67.order_ref
  44.8 0.5 collective-permute-done.9.refs_10_
  45.3 0.9 collective-permute-done.12.refs_13_
  46.3 0.9 collective-permute-done.11.refs_12_
  47.2 0.0 collective-permute-done.13.refs_14_
  47.2 0.2 collective-permute-done.14.refs_15_
  47.4 0.0 copy-start
  47.4 1.0 copy-done
  48.4 20.2 %head_gradient.1 = bf16[256,1280]{1,0:T(8,128)(2,1)} custom-call(s32[16]{0:T(128)S(1)} %stack.67.order_ref, bf16[16,80,128]{2,1,0:T(8,128)(2,1)S(1)} %all_to_all.15.cot_ref, bf16[1280,240]{1,0:T(8,128)(2,1)} %constant_dynamic-slice_fusion.weight_ref, bf16[128,1280]{1,0:T(8,128)(2,1)S(1)} %copy-done, bf16[128,1280]{1,0:T(8,128)(2,1)S(1)} %collective-permute-done.2.refs_1_, ...), custom_call_target="tpu_custom_call" | custom-call | flops 6442450944 | bytes 8388608 | tf_op jit(solution)/shard_map/head_gradient/pallas_call | solution.py:187
  68.6 20.6 %all_to_all.16 = bf16[8,32,1280]{2,1,0:T(8,128)(2,1)S(1)} all-to-all(bf16[8,32,1280]{2,1,0:T(8,128)(2,1)} %bitcast.25), channel_id=1, replica_groups=mesh['dp'=8,'seq'=16] {'dp'}, dimensions={0} | all-to-all | bytes 1310720 | tf_op jit(solution)/shard_map/all_to_all | solution.py:213
  89.2 0.1 reduce_sum.12
  89.4 14.7 %all_to_all.17 = bf16[8,32,1280]{2,1,0:T(8,128)(2,1)S(1)} all-to-all(bf16[8,32,1280]{2,1,0:T(8,128)(2,1)S(1)} %broadcast_in_dim.2), channel_id=1, replica_groups=mesh['dp'=8,'seq'=16] {'dp'}, dimensions={0} | all-to-all | bytes 1310720 | tf_op jit(solution)/shard_map/all_to_all | solution.py:213
  104.0 1.1 %convert_bitcast_fusion = f32[1280,240]{0,1:T(8,128)} fusion(bf16[256,1280]{1,0:T(8,128)(2,1)S(1)} %bitcast.24), kind=kLoop, calls=%fused_computation | loop fusion | flops 307200 | bytes 1843200 | tf_op jit(solution)/shard_map/transpose | solution.py:256
  (1 shorter events, 0.0 us)
Async XLA Ops:
  7.6 10.8 %collective-permute-start = (bf16[128,1280]{1,0:T(8,128)(2,1)}, bf16[128,1280]{1,0:T(8,128)(2,1)S(1)}, u32[]{:S(2)}, u32[]{:S(2)}) collective-permute-start(bf16[128,1280]{1,0:T(8,128)(2,1)} %get-tuple-element.11.refs_0_), channel_id=1, source_target_pairs={{0,2},{1,3},{2,4},{3,5},{4,6},{5,7},{6,0},{7,1},{8,10},{9,11},{10,... | collective-permute-start | bytes 983048 | tf_op jit(solution)/shard_map/ppermute | solution.py:228
  9.2 9.6 %collective-permute-start.2 = (bf16[128,1280]{1,0:T(8,128)(2,1)}, bf16[128,1280]{1,0:T(8,128)(2,1)S(1)}, u32[]{:S(2)}, u32[]{:S(2)}) collective-permute-start(bf16[128,1280]{1,0:T(8,128)(2,1)} %get-tuple-element.11.refs_0_), channel_id=1, source_target_pairs={{0,8},{1,9},{2,10},{3,11},{4,12},{5,13},{6,14},{7,15},{8,0},{9,1},... | collective-permute-start | bytes 983048 | tf_op jit(solution)/shard_map/ppermute | solution.py:228
  11.2 9.7 %collective-permute-start.3 = (bf16[128,1280]{1,0:T(8,128)(2,1)}, bf16[128,1280]{1,0:T(8,128)(2,1)S(1)}, u32[]{:S(2)}, u32[]{:S(2)}) collective-permute-start(bf16[128,1280]{1,0:T(8,128)(2,1)} %get-tuple-element.11.refs_0_), channel_id=1, source_target_pairs={{0,6},{1,7},{2,0},{3,1},{4,2},{5,3},{6,4},{7,5},{8,14},{9,15},{10,... | collective-permute-start | bytes 983048 | tf_op jit(solution)/shard_map/ppermute | solution.py:228
  18.8 8.5 %collective-permute-start.5 = (bf16[128,1280]{1,0:T(8,128)(2,1)S(1)}, bf16[128,1280]{1,0:T(8,128)(2,1)S(1)}, u32[]{:S(2)}, u32[]{:S(2)}) collective-permute-start(bf16[128,1280]{1,0:T(8,128)(2,1)S(1)} %collective-permute-done.2.refs_1_), channel_id=1, source_target_pairs={{0,6},{1,7},{2,0},{3,1},{4,2},{5,3},{6,4},{7,5},{8,14},{9,15},{10,... | collective-permute-start | bytes 983048 | tf_op jit(solution)/shard_map/ppermute | solution.py:228
  20.6 10.3 %collective-permute-start.1 = (bf16[128,1280]{1,0:T(8,128)(2,1)S(1)}, bf16[128,1280]{1,0:T(8,128)(2,1)S(1)}, u32[]{:S(2)}, u32[]{:S(2)}) collective-permute-start(bf16[128,1280]{1,0:T(8,128)(2,1)S(1)} %collective-permute-done.refs_2_), channel_id=1, source_target_pairs={{0,2},{1,3},{2,4},{3,5},{4,6},{5,7},{6,0},{7,1},{8,10},{9,11},{10,... | collective-permute-start | bytes 983048 | tf_op jit(solution)/shard_map/ppermute | solution.py:228
  20.9 22.7 %collective-permute-start.7 = (bf16[128,1280]{1,0:T(8,128)(2,1)}, bf16[128,1280]{1,0:T(8,128)(2,1)S(1)}, u32[]{:S(2)}, u32[]{:S(2)}) collective-permute-start(bf16[128,1280]{1,0:T(8,128)(2,1)} %get-tuple-element.11.refs_0_), channel_id=1, source_target_pairs={{0,1},{1,0},{2,3},{3,2},{4,5},{5,4},{6,7},{7,6},{8,9},{9,8},{10,11... | collective-permute-start | bytes 983048 | tf_op jit(solution)/shard_map/ppermute | solution.py:228
  20.9 22.7 %collective-permute-start.10 = (bf16[128,1280]{1,0:T(8,128)(2,1)S(1)}, bf16[128,1280]{1,0:T(8,128)(2,1)S(1)}, u32[]{:S(2)}, u32[]{:S(2)}) collective-permute-start(bf16[128,1280]{1,0:T(8,128)(2,1)S(1)} %collective-permute-done.3.refs_3_), channel_id=1, source_target_pairs={{0,1},{1,0},{2,3},{3,2},{4,5},{5,4},{6,7},{7,6},{8,9},{9,8},{10,11... | collective-permute-start | bytes 983048 | tf_op jit(solution)/shard_map/ppermute | solution.py:228
  21.4 22.7 %collective-permute-start.8 = (bf16[128,1280]{1,0:T(8,128)(2,1)S(1)}, bf16[128,1280]{1,0:T(8,128)(2,1)S(1)}, u32[]{:S(2)}, u32[]{:S(2)}) collective-permute-start(bf16[128,1280]{1,0:T(8,128)(2,1)S(1)} %collective-permute-done.2.refs_1_), channel_id=1, source_target_pairs={{0,1},{1,0},{2,3},{3,2},{4,5},{5,4},{6,7},{7,6},{8,9},{9,8},{10,11... | collective-permute-start | bytes 983048 | tf_op jit(solution)/shard_map/ppermute | solution.py:228
  27.3 16.8 %collective-permute-start.4 = (bf16[128,1280]{1,0:T(8,128)(2,1)S(1)}, bf16[128,1280]{1,0:T(8,128)(2,1)S(1)}, u32[]{:S(2)}, u32[]{:S(2)}) collective-permute-start(bf16[128,1280]{1,0:T(8,128)(2,1)S(1)} %collective-permute-done.2.refs_1_), channel_id=1, source_target_pairs={{0,2},{1,3},{2,4},{3,5},{4,6},{5,7},{6,0},{7,1},{8,10},{9,11},{10,... | collective-permute-start | bytes 983048 | tf_op jit(solution)/shard_map/ppermute | solution.py:228
  30.8 13.7 %collective-permute-start.6 = (bf16[128,1280]{1,0:T(8,128)(2,1)S(1)}, bf16[128,1280]{1,0:T(8,128)(2,1)}, u32[]{:S(2)}, u32[]{:S(2)}) collective-permute-start(bf16[128,1280]{1,0:T(8,128)(2,1)S(1)} %collective-permute-done.5.refs_5_), channel_id=1, source_target_pairs={{0,6},{1,7},{2,0},{3,1},{4,2},{5,3},{6,4},{7,5},{8,14},{9,15},{10,... | collective-permute-start | bytes 983048 | tf_op jit(solution)/shard_map/ppermute | solution.py:228
  43.6 1.8 %collective-permute-start.9 = (bf16[128,1280]{1,0:T(8,128)(2,1)S(1)}, bf16[128,1280]{1,0:T(8,128)(2,1)}, u32[]{:S(2)}, u32[]{:S(2)}) collective-permute-start(bf16[128,1280]{1,0:T(8,128)(2,1)S(1)} %collective-permute-done.refs_2_), channel_id=1, source_target_pairs={{0,1},{1,0},{2,3},{3,2},{4,5},{5,4},{6,7},{7,6},{8,9},{9,8},{10,11... | collective-permute-start | bytes 983048 | tf_op jit(solution)/shard_map/ppermute | solution.py:228
  43.6 3.6 %collective-permute-start.13 = (bf16[128,1280]{1,0:T(8,128)(2,1)S(1)}, bf16[128,1280]{1,0:T(8,128)(2,1)}, u32[]{:S(2)}, u32[]{:S(2)}) collective-permute-start(bf16[128,1280]{1,0:T(8,128)(2,1)S(1)} %collective-permute-done.1.refs_6_), channel_id=1, source_target_pairs={{0,1},{1,0},{2,3},{3,2},{4,5},{5,4},{6,7},{7,6},{8,9},{9,8},{10,11... | collective-permute-start | bytes 983048 | tf_op jit(solution)/shard_map/ppermute | solution.py:228
  44.1 2.2 %collective-permute-start.12 = (bf16[128,1280]{1,0:T(8,128)(2,1)S(1)}, bf16[128,1280]{1,0:T(8,128)(2,1)}, u32[]{:S(2)}, u32[]{:S(2)}) collective-permute-start(bf16[128,1280]{1,0:T(8,128)(2,1)S(1)} %collective-permute-done.5.refs_5_), channel_id=1, source_target_pairs={{0,1},{1,0},{2,3},{3,2},{4,5},{5,4},{6,7},{7,6},{8,9},{9,8},{10,11... | collective-permute-start | bytes 983048 | tf_op jit(solution)/shard_map/ppermute | solution.py:228
  44.2 3.0 %collective-permute-start.11 = (bf16[128,1280]{1,0:T(8,128)(2,1)S(1)}, bf16[128,1280]{1,0:T(8,128)(2,1)}, u32[]{:S(2)}, u32[]{:S(2)}) collective-permute-start(bf16[128,1280]{1,0:T(8,128)(2,1)S(1)} %collective-permute-done.4.refs_4_), channel_id=1, source_target_pairs={{0,1},{1,0},{2,3},{3,2},{4,5},{5,4},{6,7},{7,6},{8,9},{9,8},{10,11... | collective-permute-start | bytes 983048 | tf_op jit(solution)/shard_map/ppermute | solution.py:228
  44.6 2.8 %collective-permute-start.14 = (bf16[128,1280]{1,0:T(8,128)(2,1)}, bf16[128,1280]{1,0:T(8,128)(2,1)}, u32[]{:S(2)}, u32[]{:S(2)}) collective-permute-start(bf16[128,1280]{1,0:T(8,128)(2,1)} %collective-permute-done.6.refs_7_), channel_id=1, source_target_pairs={{0,1},{1,0},{2,3},{3,2},{4,5},{5,4},{6,7},{7,6},{8,9},{9,8},{10,11... | collective-permute-start | bytes 983048 | tf_op jit(solution)/shard_map/ppermute | solution.py:228
  47.4 1.0 copy-start

commit v5 on v4

--- a/solution.py
+++ b/solution.py
@@ -92,25 +92,19 @@
 def head_kernel(sub, order_ref, cot_ref, weight_ref, *refs):
     pieces = cot_ref.shape[0]
     chunks, out_ref = refs[:pieces], refs[pieces]
-    held, sems, x, k3, v1, grads, query_scaled, cot_scaled, shifted_all, scores_all = refs[pieces + 1 :]
+    x, k3, v1, grads, query_scaled, cot_scaled, shifted_all, scores_all = refs[pieces + 1 :]
     hd = HEAD_DIM
     scale = 1.0 / math.sqrt(hd)
     width = cot_ref.shape[2]
     count = pieces * width
     join = 4
-    loads = [
-        pltpu.make_async_copy(chunk, held.at[pl.ds(i * width, width)], sems.at[i])
-        for i, chunk in enumerate(chunks)
-    ]
-    for load in loads:
-        load.start()
     for piece in range(pieces):
         x[3 * hd :, piece * width : (piece + 1) * width] = cot_ref[order_ref[piece]]
+    weight_t = weight_ref[...].T
     for at in range(0, pieces, join):
-        for load in loads[at : at + join]:
-            load.wait()
+        tokens = jnp.concatenate([chunk[...] for chunk in chunks[at : at + join]], axis=0)
         columns = slice(at * width, (at + join) * width)
-        x[0 : 3 * hd, columns] = matmul(held[columns, :], weight_ref[...]).T.astype(BF16)
+        x[0 : 3 * hd, columns] = matmul(weight_t, tokens, ((1,), (1,))).astype(BF16)
     key = x[hd : 2 * hd, :]
     k3[...] = jnp.concatenate([key, key, key], axis=0)
     row = lax.broadcasted_iota(jnp.int32, (LANES - hd, count), 0)
@@ -177,7 +171,12 @@
     grads[hd : 2 * hd, :] = matmul(query_scaled[...], scores_all[...]).astype(BF16)
     grads[2 * hd : 3 * hd, :] = matmul(cot_scaled[...], shifted_all[...]).astype(BF16)
     grads[3 * hd :, :] = jnp.zeros((grads.shape[0] - 3 * hd, count), BF16)
-    out_ref[...] = matmul(grads[...], held[...]).astype(BF16)
+    total = None
+    for at in range(0, pieces, join):
+        tokens = jnp.concatenate([chunk[...] for chunk in chunks[at : at + join]], axis=0)
+        term = matmul(grads[:, at * width : (at + join) * width], tokens)
+        total = term if total is None else total + term
+    out_ref[...] = total.astype(BF16)
 
 
 def head_gradient(order, cot, weight, chunks, rows):
@@ -187,11 +186,9 @@
     return pl.pallas_call(
         functools.partial(head_kernel, 256),
         out_shape=jax.ShapeDtypeStruct((rows, chunks[0].shape[1]), BF16),
-        in_specs=[pl.BlockSpec(memory_space=pltpu.SMEM)] + [vmem] * 2 + [pl.BlockSpec(memory_space=pl.ANY)] * pieces,
+        in_specs=[pl.BlockSpec(memory_space=pltpu.SMEM)] + [vmem] * (2 + pieces),
         out_specs=vmem,
         scratch_shapes=[
-            pltpu.VMEM((count, chunks[0].shape[1]), BF16),
-            pltpu.SemaphoreType.DMA((pieces,)),
             pltpu.VMEM((4 * HEAD_DIM, count), BF16),
             pltpu.VMEM((3 * HEAD_DIM, count), BF16),
             pltpu.VMEM((LANES, count), BF16),
@@ -201,7 +198,7 @@
             pltpu.VMEM((count, count), BF16),
             pltpu.VMEM((count, count), BF16),
         ],
-        compiler_params=pltpu.CompilerParams(vmem_limit_bytes=48 << 20),
+        compiler_params=pltpu.CompilerParams(vmem_limit_bytes=42 << 20),
         cost_estimate=pl.CostEstimate(
             flops=12 * count * count * LANES, bytes_accessed=8 << 20, transcendentals=count * count
         ),

time: 106 us -> 103 us (0.972)
  Pallas kernels: 27.8 us -> 24 us
    pallas_call x1, Pallas kernels: 20.2 us -> 16.4 us  [head_gradient(): pl.pallas_call(functools.partial(head_kernel, 256), out_shape=jax.ShapeDt...]
    unnamed x2 -> x6, local copies, waits for them, and re-layouts: 0.97 us -> 2.68 us
  transfers between devices with their start and end apart: 15 -> 15, of which waited for: 8 -> 7; matrix products, arithmetic and copies ran while one was open for 2% -> 2% of each run, Pallas kernels for 0% -> 0%
where the time goes in v5:
time: 103 us; the launch traced here: 102 us
  blocking collectives  47.8 us (46%)
  Pallas kernels  24 us (23%)
  waiting for transfers between devices  14.5 us (14%)
  starting transfers between devices  10.6 us (10%)
  local copies, waits for them, and re-layouts  4.29 us (4%)
  other arithmetic  1.2 us (1%)
    all_to_all x3, blocking collectives, exchange(): lax.all_to_all(array, axis_name, split_axis=0, concat_axis=0, tiled=True)  47.8 us
    pallas_call x1, Pallas kernels, head_gradient(): pl.pallas_call(functools.partial(head_kernel, 256), out_shape=jax.ShapeDt...  16.4 us
    ppermute x15, waiting for transfers between devices, send(): return lax.ppermute(array, 'seq', [(i, over(i, *by)) for i in range(count)])  14.5 us
    ppermute x15, starting transfers between devices, send(): return lax.ppermute(array, 'seq', [(i, over(i, *by)) for i in range(count)])  10.6 us
    pallas_call x1, Pallas kernels, learn_tokens(): pl.pallas_call(functools.partial(tokens_kernel, math.gcd(count, 4), 4), o...  7.6 us
    unnamed x6, local copies, waits for them, and re-layouts  2.68 us
  transfers between devices with their start and end apart: 15, of which 7 were waited for; matrix products, arithmetic and copies ran while one was open for 2% of the time, Pallas kernels for 0%

profile of v5, /device:TPU:0, one launch (start us, length us, event | category | flops | bytes accessed | tf_op | source)
XLA Modules:
  0.0 102.4 jit_solution(7428171159977104825)
XLA Ops:
  0.0 7.6 %learn_tokens.1 = (bf16[128,1280]{1,0:T(8,128)(2,1)}, bf16[16,80,128]{2,1,0:T(8,128)(2,1)}) custom-call(bf16[16,256,1280]{2,1,0:T(8,128)(2,1)} %bitcast.24, bf16[8,1280]{1,0:T(8,128)(2,1)} %bitcast.27, bf16[128,1280]{1,0:T(8,128)(2,1)} %bitcast.26), custom_call_target="tpu_custom_call" | custom-call | tf_op jit(solution)/shard_map/learn_tokens/pallas_call | solution.py:71
  7.6 1.6 %collective-permute-start = (bf16[128,1280]{1,0:T(8,128)(2,1)}, bf16[128,1280]{1,0:T(8,128)(2,1)S(1)}, u32[]{:S(2)}, u32[]{:S(2)}) collective-permute-start(bf16[128,1280]{1,0:T(8,128)(2,1)} %get-tuple-element.11.refs_0_), channel_id=1, source_target_pairs={{0,2},{1,3},{2,4},{3,5},{4,6},{5,7},{6,0},{7,1},{8,10},{9,11},{10,... | collective-permute-start | bytes 983048 | tf_op jit(solution)/shard_map/ppermute | solution.py:225
  9.3 1.9 %collective-permute-start.2 = (bf16[128,1280]{1,0:T(8,128)(2,1)}, bf16[128,1280]{1,0:T(8,128)(2,1)S(1)}, u32[]{:S(2)}, u32[]{:S(2)}) collective-permute-start(bf16[128,1280]{1,0:T(8,128)(2,1)} %get-tuple-element.11.refs_0_), channel_id=1, source_target_pairs={{0,8},{1,9},{2,10},{3,11},{4,12},{5,13},{6,14},{7,15},{8,0},{9,1},... | collective-permute-start | bytes 983048 | tf_op jit(solution)/shard_map/ppermute | solution.py:225
  11.2 1.7 %collective-permute-start.3 = (bf16[128,1280]{1,0:T(8,128)(2,1)}, bf16[128,1280]{1,0:T(8,128)(2,1)S(1)}, u32[]{:S(2)}, u32[]{:S(2)}) collective-permute-start(bf16[128,1280]{1,0:T(8,128)(2,1)} %get-tuple-element.11.refs_0_), channel_id=1, source_target_pairs={{0,6},{1,7},{2,0},{3,1},{4,2},{5,3},{6,4},{7,5},{8,14},{9,15},{10,... | collective-permute-start | bytes 983048 | tf_op jit(solution)/shard_map/ppermute | solution.py:225
  12.9 1.5 %constant_dynamic-slice_fusion.weight_ref = bf16[1280,240]{1,0:T(8,128)(2,1)S(1)} fusion(bf16[1280,3840]{1,0:T(8,128)(2,1)} %param.6, s32[]{:T(128)S(6)} %select_n.162), kind=kLoop, calls=%fused_computation.1 | loop fusion | bytes 1228804 | tf_op jit(solution)/shard_map/dynamic_slice | solution.py:247
  14.4 4.0 %collective-permute-done.refs_2_ = bf16[128,1280]{1,0:T(8,128)(2,1)S(1)} collective-permute-done((bf16[128,1280]{1,0:T(8,128)(2,1)}, bf16[128,1280]{1,0:T(8,128)(2,1)S(1)}, u32[]{:S(2)}, u32[]{:S(2)}) %collective-permute-start) | collective-permute-done | bytes 327712 | tf_op jit(solution)/shard_map/ppermute | solution.py:225
  18.4 0.4 collective-permute-done.2.refs_1_
  18.8 1.7 %collective-permute-start.5 = (bf16[128,1280]{1,0:T(8,128)(2,1)S(1)}, bf16[128,1280]{1,0:T(8,128)(2,1)S(1)}, u32[]{:S(2)}, u32[]{:S(2)}) collective-permute-start(bf16[128,1280]{1,0:T(8,128)(2,1)S(1)} %collective-permute-done.2.refs_1_), channel_id=1, source_target_pairs={{0,6},{1,7},{2,0},{3,1},{4,2},{5,3},{6,4},{7,5},{8,14},{9,15},{10,... | collective-permute-start | bytes 983048 | tf_op jit(solution)/shard_map/ppermute | solution.py:225
  20.6 0.3 collective-permute-start.1
  20.9 0.0 collective-permute-start.7
  20.9 0.0 collective-permute-done.3.refs_3_
  20.9 0.5 collective-permute-start.10
  21.4 0.0 collective-permute-start.8
  21.4 5.9 %collective-permute-done.5.refs_5_ = bf16[128,1280]{1,0:T(8,128)(2,1)S(1)} collective-permute-done((bf16[128,1280]{1,0:T(8,128)(2,1)S(1)}, bf16[128,1280]{1,0:T(8,128)(2,1)S(1)}, u32[]{:S(2)}, u32[]{:S(2)}) %collective-permute-start.5) | collective-permute-done | bytes 327712 | tf_op jit(solution)/shard_map/ppermute | solution.py:225
  27.3 1.5 %collective-permute-start.4 = (bf16[128,1280]{1,0:T(8,128)(2,1)S(1)}, bf16[128,1280]{1,0:T(8,128)(2,1)}, u32[]{:S(2)}, u32[]{:S(2)}) collective-permute-start(bf16[128,1280]{1,0:T(8,128)(2,1)S(1)} %collective-permute-done.2.refs_1_), channel_id=1, source_target_pairs={{0,2},{1,3},{2,4},{3,5},{4,6},{5,7},{6,0},{7,1},{8,10},{9,11},{10,... | collective-permute-start | bytes 983048 | tf_op jit(solution)/shard_map/ppermute | solution.py:225
  28.8 2.0 %collective-permute-done.1.refs_6_ = bf16[128,1280]{1,0:T(8,128)(2,1)S(1)} collective-permute-done((bf16[128,1280]{1,0:T(8,128)(2,1)S(1)}, bf16[128,1280]{1,0:T(8,128)(2,1)S(1)}, u32[]{:S(2)}, u32[]{:S(2)}) %collective-permute-start.1) | collective-permute-done | bytes 327712 | tf_op jit(solution)/shard_map/ppermute | solution.py:225
  30.9 0.0 collective-permute-start.6
  30.9 12.7 %all_to_all.15.cot_ref = bf16[16,80,128]{2,1,0:T(8,128)(2,1)S(1)} all-to-all(bf16[16,80,128]{2,1,0:T(8,128)(2,1)} %get-tuple-element.13), channel_id=1, replica_groups=mesh['dp'=8,'seq'=16] {'seq'}, dimensions={0} | all-to-all | bytes 655360 | tf_op jit(solution)/shard_map/all_to_all | solution.py:210
  43.6 0.0 collective-permute-done.7.refs_8_
  43.6 0.0 collective-permute-start.9
  43.6 0.0 collective-permute-done.10.refs_11_
  43.6 0.5 collective-permute-start.13
  44.1 0.0 collective-permute-done.8.refs_9_
  44.1 0.0 copy-start.1
  44.1 0.7 copy-done.1
  44.8 0.1 collective-permute-start.12
  44.9 0.0 collective-permute-done.4.refs_4_
  44.9 0.4 collective-permute-start.11
  45.3 0.0 collective-permute-done.6.refs_7_
  45.3 0.3 collective-permute-start.14
  45.6 0.1 stack.67.order_ref
  45.7 0.0 collective-permute-done.9.refs_10_
  45.7 0.9 collective-permute-done.12.refs_13_
  46.6 0.7 collective-permute-done.11.refs_12_
  47.3 0.0 collective-permute-done.13.refs_14_
  47.3 0.5 collective-permute-done.14.refs_15_
  47.7 0.0 copy-start
  47.7 1.0 copy-done
  48.7 0.0 copy-start.2
  48.7 1.0 copy-done.2
  49.7 16.4 %head_gradient.1 = bf16[256,1280]{1,0:T(8,128)(2,1)S(1)} custom-call(s32[16]{0:T(128)S(1)} %stack.67.order_ref, bf16[16,80,128]{2,1,0:T(8,128)(2,1)S(1)} %all_to_all.15.cot_ref, bf16[1280,240]{1,0:T(8,128)(2,1)S(1)} %constant_dynamic-slice_fusion.weight_ref, bf16[128,1280]{1,0:T(8,128)(2,1)S(1)} %copy-done, ...), custom_call_target="tpu_custom_call" | custom-call | flops 6442450944 | bytes 8388608 | tf_op jit(solution)/shard_map/head_gradient/pallas_call | solution.py:186
  66.1 20.4 %all_to_all.16 = bf16[8,32,1280]{2,1,0:T(8,128)(2,1)S(1)} all-to-all(bf16[8,32,1280]{2,1,0:T(8,128)(2,1)S(1)} %bitcast.23), channel_id=1, replica_groups=mesh['dp'=8,'seq'=16] {'dp'}, dimensions={0} | all-to-all | bytes 1310720 | tf_op jit(solution)/shard_map/all_to_all | solution.py:210
  86.5 0.1 reduce_sum.12
  86.6 14.7 %all_to_all.17 = bf16[8,32,1280]{2,1,0:T(8,128)(2,1)S(1)} all-to-all(bf16[8,32,1280]{2,1,0:T(8,128)(2,1)S(1)} %broadcast_in_dim.2), channel_id=1, replica_groups=mesh['dp'=8,'seq'=16] {'dp'}, dimensions={0} | all-to-all | bytes 1310720 | tf_op jit(solution)/shard_map/all_to_all | solution.py:210
  101.3 1.1 %convert_bitcast_fusion = f32[1280,240]{0,1:T(8,128)} fusion(bf16[256,1280]{1,0:T(8,128)(2,1)S(1)} %bitcast.25), kind=kLoop, calls=%fused_computation | loop fusion | flops 307200 | bytes 1843200 | tf_op jit(solution)/shard_map/transpose | solution.py:253
  (1 shorter events, 0.0 us)
Async XLA Ops:
  7.6 10.8 %collective-permute-start = (bf16[128,1280]{1,0:T(8,128)(2,1)}, bf16[128,1280]{1,0:T(8,128)(2,1)S(1)}, u32[]{:S(2)}, u32[]{:S(2)}) collective-permute-start(bf16[128,1280]{1,0:T(8,128)(2,1)} %get-tuple-element.11.refs_0_), channel_id=1, source_target_pairs={{0,2},{1,3},{2,4},{3,5},{4,6},{5,7},{6,0},{7,1},{8,10},{9,11},{10,... | collective-permute-start | bytes 983048 | tf_op jit(solution)/shard_map/ppermute | solution.py:225
  9.3 9.6 %collective-permute-start.2 = (bf16[128,1280]{1,0:T(8,128)(2,1)}, bf16[128,1280]{1,0:T(8,128)(2,1)S(1)}, u32[]{:S(2)}, u32[]{:S(2)}) collective-permute-start(bf16[128,1280]{1,0:T(8,128)(2,1)} %get-tuple-element.11.refs_0_), channel_id=1, source_target_pairs={{0,8},{1,9},{2,10},{3,11},{4,12},{5,13},{6,14},{7,15},{8,0},{9,1},... | collective-permute-start | bytes 983048 | tf_op jit(solution)/shard_map/ppermute | solution.py:225
  11.2 9.7 %collective-permute-start.3 = (bf16[128,1280]{1,0:T(8,128)(2,1)}, bf16[128,1280]{1,0:T(8,128)(2,1)S(1)}, u32[]{:S(2)}, u32[]{:S(2)}) collective-permute-start(bf16[128,1280]{1,0:T(8,128)(2,1)} %get-tuple-element.11.refs_0_), channel_id=1, source_target_pairs={{0,6},{1,7},{2,0},{3,1},{4,2},{5,3},{6,4},{7,5},{8,14},{9,15},{10,... | collective-permute-start | bytes 983048 | tf_op jit(solution)/shard_map/ppermute | solution.py:225
  18.8 8.5 %collective-permute-start.5 = (bf16[128,1280]{1,0:T(8,128)(2,1)S(1)}, bf16[128,1280]{1,0:T(8,128)(2,1)S(1)}, u32[]{:S(2)}, u32[]{:S(2)}) collective-permute-start(bf16[128,1280]{1,0:T(8,128)(2,1)S(1)} %collective-permute-done.2.refs_1_), channel_id=1, source_target_pairs={{0,6},{1,7},{2,0},{3,1},{4,2},{5,3},{6,4},{7,5},{8,14},{9,15},{10,... | collective-permute-start | bytes 983048 | tf_op jit(solution)/shard_map/ppermute | solution.py:225
  20.6 10.3 %collective-permute-start.1 = (bf16[128,1280]{1,0:T(8,128)(2,1)S(1)}, bf16[128,1280]{1,0:T(8,128)(2,1)S(1)}, u32[]{:S(2)}, u32[]{:S(2)}) collective-permute-start(bf16[128,1280]{1,0:T(8,128)(2,1)S(1)} %collective-permute-done.refs_2_), channel_id=1, source_target_pairs={{0,2},{1,3},{2,4},{3,5},{4,6},{5,7},{6,0},{7,1},{8,10},{9,11},{10,... | collective-permute-start | bytes 983048 | tf_op jit(solution)/shard_map/ppermute | solution.py:225
  20.9 22.7 %collective-permute-start.7 = (bf16[128,1280]{1,0:T(8,128)(2,1)}, bf16[128,1280]{1,0:T(8,128)(2,1)S(1)}, u32[]{:S(2)}, u32[]{:S(2)}) collective-permute-start(bf16[128,1280]{1,0:T(8,128)(2,1)} %get-tuple-element.11.refs_0_), channel_id=1, source_target_pairs={{0,1},{1,0},{2,3},{3,2},{4,5},{5,4},{6,7},{7,6},{8,9},{9,8},{10,11... | collective-permute-start | bytes 983048 | tf_op jit(solution)/shard_map/ppermute | solution.py:225
  20.9 22.7 %collective-permute-start.10 = (bf16[128,1280]{1,0:T(8,128)(2,1)S(1)}, bf16[128,1280]{1,0:T(8,128)(2,1)S(1)}, u32[]{:S(2)}, u32[]{:S(2)}) collective-permute-start(bf16[128,1280]{1,0:T(8,128)(2,1)S(1)} %collective-permute-done.3.refs_3_), channel_id=1, source_target_pairs={{0,1},{1,0},{2,3},{3,2},{4,5},{5,4},{6,7},{7,6},{8,9},{9,8},{10,11... | collective-permute-start | bytes 983048 | tf_op jit(solution)/shard_map/ppermute | solution.py:225
  21.4 22.7 %collective-permute-start.8 = (bf16[128,1280]{1,0:T(8,128)(2,1)S(1)}, bf16[128,1280]{1,0:T(8,128)(2,1)S(1)}, u32[]{:S(2)}, u32[]{:S(2)}) collective-permute-start(bf16[128,1280]{1,0:T(8,128)(2,1)S(1)} %collective-permute-done.2.refs_1_), channel_id=1, source_target_pairs={{0,1},{1,0},{2,3},{3,2},{4,5},{5,4},{6,7},{7,6},{8,9},{9,8},{10,11... | collective-permute-start | bytes 983048 | tf_op jit(solution)/shard_map/ppermute | solution.py:225
  27.3 17.6 %collective-permute-start.4 = (bf16[128,1280]{1,0:T(8,128)(2,1)S(1)}, bf16[128,1280]{1,0:T(8,128)(2,1)}, u32[]{:S(2)}, u32[]{:S(2)}) collective-permute-start(bf16[128,1280]{1,0:T(8,128)(2,1)S(1)} %collective-permute-done.2.refs_1_), channel_id=1, source_target_pairs={{0,2},{1,3},{2,4},{3,5},{4,6},{5,7},{6,0},{7,1},{8,10},{9,11},{10,... | collective-permute-start | bytes 983048 | tf_op jit(solution)/shard_map/ppermute | solution.py:225
  30.9 14.5 %collective-permute-start.6 = (bf16[128,1280]{1,0:T(8,128)(2,1)S(1)}, bf16[128,1280]{1,0:T(8,128)(2,1)}, u32[]{:S(2)}, u32[]{:S(2)}) collective-permute-start(bf16[128,1280]{1,0:T(8,128)(2,1)S(1)} %collective-permute-done.5.refs_5_), channel_id=1, source_target_pairs={{0,6},{1,7},{2,0},{3,1},{4,2},{5,3},{6,4},{7,5},{8,14},{9,15},{10,... | collective-permute-start | bytes 983048 | tf_op jit(solution)/shard_map/ppermute | solution.py:225
  43.6 2.1 %collective-permute-start.9 = (bf16[128,1280]{1,0:T(8,128)(2,1)S(1)}, bf16[128,1280]{1,0:T(8,128)(2,1)}, u32[]{:S(2)}, u32[]{:S(2)}) collective-permute-start(bf16[128,1280]{1,0:T(8,128)(2,1)S(1)} %collective-permute-done.refs_2_), channel_id=1, source_target_pairs={{0,1},{1,0},{2,3},{3,2},{4,5},{5,4},{6,7},{7,6},{8,9},{9,8},{10,11... | collective-permute-start | bytes 983048 | tf_op jit(solution)/shard_map/ppermute | solution.py:225
  43.6 3.7 %collective-permute-start.13 = (bf16[128,1280]{1,0:T(8,128)(2,1)S(1)}, bf16[128,1280]{1,0:T(8,128)(2,1)}, u32[]{:S(2)}, u32[]{:S(2)}) collective-permute-start(bf16[128,1280]{1,0:T(8,128)(2,1)S(1)} %collective-permute-done.1.refs_6_), channel_id=1, source_target_pairs={{0,1},{1,0},{2,3},{3,2},{4,5},{5,4},{6,7},{7,6},{8,9},{9,8},{10,11... | collective-permute-start | bytes 983048 | tf_op jit(solution)/shard_map/ppermute | solution.py:225
  44.1 0.7 copy-start.1
  44.8 1.8 %collective-permute-start.12 = (bf16[128,1280]{1,0:T(8,128)(2,1)S(1)}, bf16[128,1280]{1,0:T(8,128)(2,1)}, u32[]{:S(2)}, u32[]{:S(2)}) collective-permute-start(bf16[128,1280]{1,0:T(8,128)(2,1)S(1)} %collective-permute-done.5.refs_5_), channel_id=1, source_target_pairs={{0,1},{1,0},{2,3},{3,2},{4,5},{5,4},{6,7},{7,6},{8,9},{9,8},{10,11... | collective-permute-start | bytes 983048 | tf_op jit(solution)/shard_map/ppermute | solution.py:225
  44.9 2.4 %collective-permute-start.11 = (bf16[128,1280]{1,0:T(8,128)(2,1)}, bf16[128,1280]{1,0:T(8,128)(2,1)}, u32[]{:S(2)}, u32[]{:S(2)}) collective-permute-start(bf16[128,1280]{1,0:T(8,128)(2,1)} %collective-permute-done.4.refs_4_), channel_id=1, source_target_pairs={{0,1},{1,0},{2,3},{3,2},{4,5},{5,4},{6,7},{7,6},{8,9},{9,8},{10,11... | collective-permute-start | bytes 983048 | tf_op jit(solution)/shard_map/ppermute | solution.py:225
  45.3 2.4 %collective-permute-start.14 = (bf16[128,1280]{1,0:T(8,128)(2,1)}, bf16[128,1280]{1,0:T(8,128)(2,1)}, u32[]{:S(2)}, u32[]{:S(2)}) collective-permute-start(bf16[128,1280]{1,0:T(8,128)(2,1)} %collective-permute-done.6.refs_7_), channel_id=1, source_target_pairs={{0,1},{1,0},{2,3},{3,2},{4,5},{5,4},{6,7},{7,6},{8,9},{9,8},{10,11... | collective-permute-start | bytes 983048 | tf_op jit(solution)/shard_map/ppermute | solution.py:225
  47.7 1.0 copy-start
  48.7 1.0 copy-start.2

commit v6 on v5

--- a/solution.py
+++ b/solution.py
@@ -224,11 +224,14 @@
     def send(array, *by):
         return lax.ppermute(array, "seq", [(i, over(i, *by)) for i in range(count)])
 
+    other = send(own, 1, 0, 0)
     right, left = send(own, 0, 1, 0), send(own, 0, -1, 0)
-    other = send(own, 1, 0, 0)
-    other_right, other_left = send(other, 0, 1, 0), send(other, 0, -1, 0)
+    other_left = send(other, 0, -1, 0)
+    other_right = send(right, 1, 0, 0)
     right, weight = lax.optimization_barrier((right, weight))
-    across, other_across = send(right, 0, 1, 0), send(other_left, 0, -1, 0)
+    across = send(right, 0, 1, 0)
+    other_right, other_left = lax.optimization_barrier((other_right, other_left))
+    other_across = send(other_left, 0, -1, 0)
     across, cot = lax.optimization_barrier((across, exchange(cot, "seq")))
     near = [own, other, right, left, other_right, other_left, across, other_across]
     places = [(0, 0), (1, 0), (0, -1), (0, 1), (1, -1), (1, 1), (0, -2), (1, 2)]

time: 103 us -> 101 us (0.981)
  blocking collectives: 47.8 us -> 35 us
  starting transfers between devices: 10.6 us -> 16.9 us
  waiting for transfers between devices: 14.5 us -> 19.7 us
  local copies, waits for them, and re-layouts: 4.29 us -> 2.59 us
    all_to_all x3 -> x2, blocking collectives: 47.8 us -> 35 us  [exchange(): lax.all_to_all(array, axis_name, split_axis=0, concat_axis=0, tiled=True)]
    all_to_all x0 -> x1, waiting for transfers between devices: none -> 8.12 us  [exchange(): lax.all_to_all(array, axis_name, split_axis=0, concat_axis=0, tiled=True)]
    all_to_all x0 -> x1, starting transfers between devices: none -> 3.54 us  [exchange(): lax.all_to_all(array, axis_name, split_axis=0, concat_axis=0, tiled=True)]
    ppermute x15, waiting for transfers between devices: 14.5 us -> 11.5 us  [send(): return lax.ppermute(array, 'seq', [(i, over(i, *by)) for i in range(count)])]
    ppermute x15, starting transfers between devices: 10.6 us -> 13.3 us  [send(): return lax.ppermute(array, 'seq', [(i, over(i, *by)) for i in range(count)])]
    unnamed x6 -> x2, local copies, waits for them, and re-layouts: 2.68 us -> 0.97 us
  transfers between devices with their start and end apart: 15 -> 16, of which waited for: 7 -> 7; matrix products, arithmetic and copies ran while one was open for 2% -> 2% of each run, Pallas kernels for 0% -> 0%
where the time goes in v6:
time: 101 us; the launch traced here: 99.5 us
  blocking collectives  35 us (35%)
  Pallas kernels  24.1 us (24%)
  waiting for transfers between devices  19.7 us (20%)
  starting transfers between devices  16.9 us (17%)
  local copies, waits for them, and re-layouts  2.59 us (3%)
  other arithmetic  1.2 us (1%)
    all_to_all x2, blocking collectives, exchange(): lax.all_to_all(array, axis_name, split_axis=0, concat_axis=0, tiled=True)  35 us
    pallas_call x1, Pallas kernels, head_gradient(): pl.pallas_call(functools.partial(head_kernel, 256), out_shape=jax.ShapeDt...  16.5 us
    ppermute x15, starting transfers between devices, send(): return lax.ppermute(array, 'seq', [(i, over(i, *by)) for i in range(count)])  13.3 us
    ppermute x15, waiting for transfers between devices, send(): return lax.ppermute(array, 'seq', [(i, over(i, *by)) for i in range(count)])  11.5 us
    all_to_all x1, waiting for transfers between devices, exchange(): lax.all_to_all(array, axis_name, split_axis=0, concat_axis=0, tiled=True)  8.12 us
    pallas_call x1, Pallas kernels, learn_tokens(): pl.pallas_call(functools.partial(tokens_kernel, math.gcd(count, 4), 4), o...  7.58 us
    all_to_all x1, starting transfers between devices, exchange(): lax.all_to_all(array, axis_name, split_axis=0, concat_axis=0, tiled=True)  3.54 us
  transfers between devices with their start and end apart: 16, of which 7 were waited for; matrix products, arithmetic and copies ran while one was open for 2% of the time, Pallas kernels for 0%

profile of v6, /device:TPU:0, one launch (start us, length us, event | category | flops | bytes accessed | tf_op | source)
XLA Modules:
  0.0 99.5 jit_solution(13234121486965961334)
XLA Ops:
  0.0 7.6 %learn_tokens.1 = (bf16[128,1280]{1,0:T(8,128)(2,1)}, bf16[16,80,128]{2,1,0:T(8,128)(2,1)}) custom-call(bf16[16,256,1280]{2,1,0:T(8,128)(2,1)} %bitcast.24, bf16[8,1280]{1,0:T(8,128)(2,1)} %bitcast.27, bf16[128,1280]{1,0:T(8,128)(2,1)} %bitcast.26), custom_call_target="tpu_custom_call" | custom-call | tf_op jit(solution)/shard_map/learn_tokens/pallas_call | solution.py:71
  7.6 2.1 %collective-permute-start.2 = (bf16[128,1280]{1,0:T(8,128)(2,1)}, bf16[128,1280]{1,0:T(8,128)(2,1)S(1)}, u32[]{:S(2)}, u32[]{:S(2)}) collective-permute-start(bf16[128,1280]{1,0:T(8,128)(2,1)} %get-tuple-element.13.refs_0_), channel_id=1, source_target_pairs={{0,8},{1,9},{2,10},{3,11},{4,12},{5,13},{6,14},{7,15},{8,0},{9,1},... | collective-permute-start | bytes 983048 | tf_op jit(solution)/shard_map/ppermute | solution.py:225
  9.7 1.5 %collective-permute-start = (bf16[128,1280]{1,0:T(8,128)(2,1)}, bf16[128,1280]{1,0:T(8,128)(2,1)S(1)}, u32[]{:S(2)}, u32[]{:S(2)}) collective-permute-start(bf16[128,1280]{1,0:T(8,128)(2,1)} %get-tuple-element.13.refs_0_), channel_id=1, source_target_pairs={{0,2},{1,3},{2,4},{3,5},{4,6},{5,7},{6,0},{7,1},{8,10},{9,11},{10,... | collective-permute-start | bytes 983048 | tf_op jit(solution)/shard_map/ppermute | solution.py:225
  11.2 1.7 %collective-permute-start.3 = (bf16[128,1280]{1,0:T(8,128)(2,1)}, bf16[128,1280]{1,0:T(8,128)(2,1)S(1)}, u32[]{:S(2)}, u32[]{:S(2)}) collective-permute-start(bf16[128,1280]{1,0:T(8,128)(2,1)} %get-tuple-element.13.refs_0_), channel_id=1, source_target_pairs={{0,6},{1,7},{2,0},{3,1},{4,2},{5,3},{6,4},{7,5},{8,14},{9,15},{10,... | collective-permute-start | bytes 983048 | tf_op jit(solution)/shard_map/ppermute | solution.py:225
  12.9 4.7 %collective-permute-done.2.refs_1_ = bf16[128,1280]{1,0:T(8,128)(2,1)S(1)} collective-permute-done((bf16[128,1280]{1,0:T(8,128)(2,1)}, bf16[128,1280]{1,0:T(8,128)(2,1)S(1)}, u32[]{:S(2)}, u32[]{:S(2)}) %collective-permute-start.2) | collective-permute-done | bytes 327712 | tf_op jit(solution)/shard_map/ppermute | solution.py:225
  17.6 2.8 %collective-permute-start.5 = (bf16[128,1280]{1,0:T(8,128)(2,1)S(1)}, bf16[128,1280]{1,0:T(8,128)(2,1)S(1)}, u32[]{:S(2)}, u32[]{:S(2)}) collective-permute-start(bf16[128,1280]{1,0:T(8,128)(2,1)S(1)} %collective-permute-done.2.refs_1_), channel_id=1, source_target_pairs={{0,6},{1,7},{2,0},{3,1},{4,2},{5,3},{6,4},{7,5},{8,14},{9,15},{10,... | collective-permute-start | bytes 983048 | tf_op jit(solution)/shard_map/ppermute | solution.py:225
  20.4 0.0 collective-permute-done.refs_2_
  20.4 1.7 %collective-permute-start.4 = (bf16[128,1280]{1,0:T(8,128)(2,1)S(1)}, bf16[128,1280]{1,0:T(8,128)(2,1)S(1)}, u32[]{:S(2)}, u32[]{:S(2)}) collective-permute-start(bf16[128,1280]{1,0:T(8,128)(2,1)S(1)} %collective-permute-done.refs_2_), channel_id=1, source_target_pairs={{0,8},{1,9},{2,10},{3,11},{4,12},{5,13},{6,14},{7,15},{8,0},{9,1},... | collective-permute-start | bytes 983048 | tf_op jit(solution)/shard_map/ppermute | solution.py:225
  22.1 1.5 %constant_dynamic-slice_fusion.weight_ref = bf16[1280,240]{1,0:T(8,128)(2,1)S(1)} fusion(bf16[1280,3840]{1,0:T(8,128)(2,1)} %param.6, s32[]{:T(128)S(6)} %select_n.162), kind=kLoop, calls=%fused_computation.1 | loop fusion | bytes 1228804 | tf_op jit(solution)/shard_map/dynamic_slice | solution.py:250
  23.6 0.1 collective-permute-start.1
  23.7 0.1 collective-permute-start.7
  23.8 0.0 collective-permute-done.3.refs_3_
  23.8 0.5 collective-permute-start.10
  24.3 3.0 %collective-permute-done.5.refs_5_ = bf16[128,1280]{1,0:T(8,128)(2,1)S(1)} collective-permute-done((bf16[128,1280]{1,0:T(8,128)(2,1)S(1)}, bf16[128,1280]{1,0:T(8,128)(2,1)S(1)}, u32[]{:S(2)}, u32[]{:S(2)}) %collective-permute-start.5) | collective-permute-done | bytes 327712 | tf_op jit(solution)/shard_map/ppermute | solution.py:225
  27.3 0.0 collective-permute-start.8
  27.3 1.6 %collective-permute-done.4.refs_4_ = bf16[128,1280]{1,0:T(8,128)(2,1)S(1)} collective-permute-done((bf16[128,1280]{1,0:T(8,128)(2,1)S(1)}, bf16[128,1280]{1,0:T(8,128)(2,1)S(1)}, u32[]{:S(2)}, u32[]{:S(2)}) %collective-permute-start.4) | collective-permute-done | bytes 327712 | tf_op jit(solution)/shard_map/ppermute | solution.py:225
  28.9 1.5 %collective-permute-start.6 = (bf16[128,1280]{1,0:T(8,128)(2,1)S(1)}, bf16[128,1280]{1,0:T(8,128)(2,1)}, u32[]{:S(2)}, u32[]{:S(2)}) collective-permute-start(bf16[128,1280]{1,0:T(8,128)(2,1)S(1)} %collective-permute-done.5.refs_5_), channel_id=1, source_target_pairs={{0,6},{1,7},{2,0},{3,1},{4,2},{5,3},{6,4},{7,5},{8,14},{9,15},{10,... | collective-permute-start | bytes 983048 | tf_op jit(solution)/shard_map/ppermute | solution.py:225
  30.3 3.5 %all-to-all-start = ((bf16[16,80,128]{2,1,0:T(8,128)(2,1)}), bf16[16,80,128]{2,1,0:T(8,128)(2,1)S(1)}, u32[]{:S(2)}, u32[]{:S(2)}) async-start(bf16[16,80,128]{2,1,0:T(8,128)(2,1)} %get-tuple-element.15), calls=%async_computation | async-start | bytes 655360 | tf_op jit(solution)/shard_map/all_to_all | solution.py:210
  33.9 0.0 collective-permute-done.1.refs_6_
  33.9 0.4 collective-permute-start.9
  34.3 8.1 %all-to-all-done.cot_ref = bf16[16,80,128]{2,1,0:T(8,128)(2,1)S(1)} async-done(((bf16[16,80,128]{2,1,0:T(8,128)(2,1)}), bf16[16,80,128]{2,1,0:T(8,128)(2,1)S(1)}, u32[]{:S(2)}, u32[]{:S(2)}) %all-to-all-start) | async-done | bytes 327712 | tf_op jit(solution)/shard_map/all_to_all | solution.py:210
  42.4 0.0 collective-permute-done.7.refs_8_
  42.4 0.0 collective-permute-start.12
  42.4 0.0 collective-permute-done.10.refs_11_
  42.4 0.5 collective-permute-start.13
  42.9 0.0 collective-permute-done.8.refs_9_
  42.9 0.1 collective-permute-start.11
  43.0 0.0 collective-permute-done.6.refs_7_
  43.0 0.4 collective-permute-start.14
  43.4 0.1 stack.67.order_ref
  43.5 0.0 collective-permute-done.9.refs_10_
  43.5 1.1 %collective-permute-done.13.refs_14_ = bf16[128,1280]{1,0:T(8,128)(2,1)} collective-permute-done((bf16[128,1280]{1,0:T(8,128)(2,1)S(1)}, bf16[128,1280]{1,0:T(8,128)(2,1)}, u32[]{:S(2)}, u32[]{:S(2)}) %collective-permute-start.13) | collective-permute-done | bytes 327712 | tf_op jit(solution)/shard_map/ppermute | solution.py:225
  44.6 0.9 collective-permute-done.11.refs_12_
  45.6 0.0 collective-permute-done.12.refs_13_
  45.6 0.2 collective-permute-done.14.refs_15_
  45.8 0.0 copy-start
  45.8 1.0 copy-done
  46.8 16.5 %head_gradient.1 = bf16[256,1280]{1,0:T(8,128)(2,1)S(1)} custom-call(s32[16]{0:T(128)S(1)} %stack.67.order_ref, bf16[16,80,128]{2,1,0:T(8,128)(2,1)S(1)} %all-to-all-done.cot_ref, bf16[1280,240]{1,0:T(8,128)(2,1)S(1)} %constant_dynamic-slice_fusion.weight_ref, bf16[128,1280]{1,0:T(8,128)(2,1)S(1)} %copy-done, ...), custom_call_target="tpu_custom_call" | custom-call | flops 6442450944 | bytes 8388608 | tf_op jit(solution)/shard_map/head_gradient/pallas_call | solution.py:186
  63.3 20.3 %all_to_all.15 = bf16[8,32,1280]{2,1,0:T(8,128)(2,1)S(1)} all-to-all(bf16[8,32,1280]{2,1,0:T(8,128)(2,1)S(1)} %bitcast.23), channel_id=1, replica_groups=mesh['dp'=8,'seq'=16] {'dp'}, dimensions={0} | all-to-all | bytes 1310720 | tf_op jit(solution)/shard_map/all_to_all | solution.py:210
  83.6 0.1 reduce_sum.12
  83.7 14.7 %all_to_all.16 = bf16[8,32,1280]{2,1,0:T(8,128)(2,1)S(1)} all-to-all(bf16[8,32,1280]{2,1,0:T(8,128)(2,1)S(1)} %broadcast_in_dim.2), channel_id=1, replica_groups=mesh['dp'=8,'seq'=16] {'dp'}, dimensions={0} | all-to-all | bytes 1310720 | tf_op jit(solution)/shard_map/all_to_all | solution.py:210
  98.4 1.1 %convert_bitcast_fusion = f32[1280,240]{0,1:T(8,128)} fusion(bf16[256,1280]{1,0:T(8,128)(2,1)S(1)} %bitcast.25), kind=kLoop, calls=%fused_computation | loop fusion | flops 307200 | bytes 1843200 | tf_op jit(solution)/shard_map/transpose | solution.py:256
  (1 shorter events, 0.0 us)
Async XLA Ops:
  7.6 10.0 %collective-permute-start.2 = (bf16[128,1280]{1,0:T(8,128)(2,1)}, bf16[128,1280]{1,0:T(8,128)(2,1)S(1)}, u32[]{:S(2)}, u32[]{:S(2)}) collective-permute-start(bf16[128,1280]{1,0:T(8,128)(2,1)} %get-tuple-element.13.refs_0_), channel_id=1, source_target_pairs={{0,8},{1,9},{2,10},{3,11},{4,12},{5,13},{6,14},{7,15},{8,0},{9,1},... | collective-permute-start | bytes 983048 | tf_op jit(solution)/shard_map/ppermute | solution.py:225
  9.7 10.7 %collective-permute-start = (bf16[128,1280]{1,0:T(8,128)(2,1)}, bf16[128,1280]{1,0:T(8,128)(2,1)S(1)}, u32[]{:S(2)}, u32[]{:S(2)}) collective-permute-start(bf16[128,1280]{1,0:T(8,128)(2,1)} %get-tuple-element.13.refs_0_), channel_id=1, source_target_pairs={{0,2},{1,3},{2,4},{3,5},{4,6},{5,7},{6,0},{7,1},{8,10},{9,11},{10,... | collective-permute-start | bytes 983048 | tf_op jit(solution)/shard_map/ppermute | solution.py:225
  11.2 12.6 %collective-permute-start.3 = (bf16[128,1280]{1,0:T(8,128)(2,1)}, bf16[128,1280]{1,0:T(8,128)(2,1)S(1)}, u32[]{:S(2)}, u32[]{:S(2)}) collective-permute-start(bf16[128,1280]{1,0:T(8,128)(2,1)} %get-tuple-element.13.refs_0_), channel_id=1, source_target_pairs={{0,6},{1,7},{2,0},{3,1},{4,2},{5,3},{6,4},{7,5},{8,14},{9,15},{10,... | collective-permute-start | bytes 983048 | tf_op jit(solution)/shard_map/ppermute | solution.py:225
  17.6 9.7 %collective-permute-start.5 = (bf16[128,1280]{1,0:T(8,128)(2,1)S(1)}, bf16[128,1280]{1,0:T(8,128)(2,1)S(1)}, u32[]{:S(2)}, u32[]{:S(2)}) collective-permute-start(bf16[128,1280]{1,0:T(8,128)(2,1)S(1)} %collective-permute-done.2.refs_1_), channel_id=1, source_target_pairs={{0,6},{1,7},{2,0},{3,1},{4,2},{5,3},{6,4},{7,5},{8,14},{9,15},{10,... | collective-permute-start | bytes 983048 | tf_op jit(solution)/shard_map/ppermute | solution.py:225
  20.4 8.5 %collective-permute-start.4 = (bf16[128,1280]{1,0:T(8,128)(2,1)S(1)}, bf16[128,1280]{1,0:T(8,128)(2,1)S(1)}, u32[]{:S(2)}, u32[]{:S(2)}) collective-permute-start(bf16[128,1280]{1,0:T(8,128)(2,1)S(1)} %collective-permute-done.refs_2_), channel_id=1, source_target_pairs={{0,8},{1,9},{2,10},{3,11},{4,12},{5,13},{6,14},{7,15},{8,0},{9,1},... | collective-permute-start | bytes 983048 | tf_op jit(solution)/shard_map/ppermute | solution.py:225
  23.6 10.3 %collective-permute-start.1 = (bf16[128,1280]{1,0:T(8,128)(2,1)S(1)}, bf16[128,1280]{1,0:T(8,128)(2,1)S(1)}, u32[]{:S(2)}, u32[]{:S(2)}) collective-permute-start(bf16[128,1280]{1,0:T(8,128)(2,1)S(1)} %collective-permute-done.refs_2_), channel_id=1, source_target_pairs={{0,2},{1,3},{2,4},{3,5},{4,6},{5,7},{6,0},{7,1},{8,10},{9,11},{10,... | collective-permute-start | bytes 983048 | tf_op jit(solution)/shard_map/ppermute | solution.py:225
  23.7 18.7 %collective-permute-start.7 = (bf16[128,1280]{1,0:T(8,128)(2,1)}, bf16[128,1280]{1,0:T(8,128)(2,1)S(1)}, u32[]{:S(2)}, u32[]{:S(2)}) collective-permute-start(bf16[128,1280]{1,0:T(8,128)(2,1)} %get-tuple-element.13.refs_0_), channel_id=1, source_target_pairs={{0,1},{1,0},{2,3},{3,2},{4,5},{5,4},{6,7},{7,6},{8,9},{9,8},{10,11... | collective-permute-start | bytes 983048 | tf_op jit(solution)/shard_map/ppermute | solution.py:225
  23.8 18.6 %collective-permute-start.10 = (bf16[128,1280]{1,0:T(8,128)(2,1)S(1)}, bf16[128,1280]{1,0:T(8,128)(2,1)}, u32[]{:S(2)}, u32[]{:S(2)}) collective-permute-start(bf16[128,1280]{1,0:T(8,128)(2,1)S(1)} %collective-permute-done.3.refs_3_), channel_id=1, source_target_pairs={{0,1},{1,0},{2,3},{3,2},{4,5},{5,4},{6,7},{7,6},{8,9},{9,8},{10,11... | collective-permute-start | bytes 983048 | tf_op jit(solution)/shard_map/ppermute | solution.py:225
  27.3 15.6 %collective-permute-start.8 = (bf16[128,1280]{1,0:T(8,128)(2,1)S(1)}, bf16[128,1280]{1,0:T(8,128)(2,1)}, u32[]{:S(2)}, u32[]{:S(2)}) collective-permute-start(bf16[128,1280]{1,0:T(8,128)(2,1)S(1)} %collective-permute-done.2.refs_1_), channel_id=1, source_target_pairs={{0,1},{1,0},{2,3},{3,2},{4,5},{5,4},{6,7},{7,6},{8,9},{9,8},{10,11... | collective-permute-start | bytes 983048 | tf_op jit(solution)/shard_map/ppermute | solution.py:225
  28.9 14.2 %collective-permute-start.6 = (bf16[128,1280]{1,0:T(8,128)(2,1)S(1)}, bf16[128,1280]{1,0:T(8,128)(2,1)}, u32[]{:S(2)}, u32[]{:S(2)}) collective-permute-start(bf16[128,1280]{1,0:T(8,128)(2,1)S(1)} %collective-permute-done.5.refs_5_), channel_id=1, source_target_pairs={{0,6},{1,7},{2,0},{3,1},{4,2},{5,3},{6,4},{7,5},{8,14},{9,15},{10,... | collective-permute-start | bytes 983048 | tf_op jit(solution)/shard_map/ppermute | solution.py:225
  30.3 12.0 %all-to-all-start = ((bf16[16,80,128]{2,1,0:T(8,128)(2,1)}), bf16[16,80,128]{2,1,0:T(8,128)(2,1)S(1)}, u32[]{:S(2)}, u32[]{:S(2)}) async-start(bf16[16,80,128]{2,1,0:T(8,128)(2,1)} %get-tuple-element.15), calls=%async_computation | async-start | bytes 655360 | tf_op jit(solution)/shard_map/all_to_all | solution.py:210
  33.9 9.6 %collective-permute-start.9 = (bf16[128,1280]{1,0:T(8,128)(2,1)S(1)}, bf16[128,1280]{1,0:T(8,128)(2,1)}, u32[]{:S(2)}, u32[]{:S(2)}) collective-permute-start(bf16[128,1280]{1,0:T(8,128)(2,1)S(1)} %collective-permute-done.refs_2_), channel_id=1, source_target_pairs={{0,1},{1,0},{2,3},{3,2},{4,5},{5,4},{6,7},{7,6},{8,9},{9,8},{10,11... | collective-permute-start | bytes 983048 | tf_op jit(solution)/shard_map/ppermute | solution.py:225
  42.4 3.2 %collective-permute-start.12 = (bf16[128,1280]{1,0:T(8,128)(2,1)S(1)}, bf16[128,1280]{1,0:T(8,128)(2,1)}, u32[]{:S(2)}, u32[]{:S(2)}) collective-permute-start(bf16[128,1280]{1,0:T(8,128)(2,1)S(1)} %collective-permute-done.5.refs_5_), channel_id=1, source_target_pairs={{0,1},{1,0},{2,3},{3,2},{4,5},{5,4},{6,7},{7,6},{8,9},{9,8},{10,11... | collective-permute-start | bytes 983048 | tf_op jit(solution)/shard_map/ppermute | solution.py:225
  42.4 2.2 %collective-permute-start.13 = (bf16[128,1280]{1,0:T(8,128)(2,1)S(1)}, bf16[128,1280]{1,0:T(8,128)(2,1)}, u32[]{:S(2)}, u32[]{:S(2)}) collective-permute-start(bf16[128,1280]{1,0:T(8,128)(2,1)S(1)} %collective-permute-done.1.refs_6_), channel_id=1, source_target_pairs={{0,1},{1,0},{2,3},{3,2},{4,5},{5,4},{6,7},{7,6},{8,9},{9,8},{10,11... | collective-permute-start | bytes 983048 | tf_op jit(solution)/shard_map/ppermute | solution.py:225
  42.9 2.6 %collective-permute-start.11 = (bf16[128,1280]{1,0:T(8,128)(2,1)S(1)}, bf16[128,1280]{1,0:T(8,128)(2,1)}, u32[]{:S(2)}, u32[]{:S(2)}) collective-permute-start(bf16[128,1280]{1,0:T(8,128)(2,1)S(1)} %collective-permute-done.4.refs_4_), channel_id=1, source_target_pairs={{0,1},{1,0},{2,3},{3,2},{4,5},{5,4},{6,7},{7,6},{8,9},{9,8},{10,11... | collective-permute-start | bytes 983048 | tf_op jit(solution)/shard_map/ppermute | solution.py:225
  43.0 2.8 %collective-permute-start.14 = (bf16[128,1280]{1,0:T(8,128)(2,1)}, bf16[128,1280]{1,0:T(8,128)(2,1)}, u32[]{:S(2)}, u32[]{:S(2)}) collective-permute-start(bf16[128,1280]{1,0:T(8,128)(2,1)} %collective-permute-done.6.refs_7_), channel_id=1, source_target_pairs={{0,1},{1,0},{2,3},{3,2},{4,5},{5,4},{6,7},{7,6},{8,9},{9,8},{10,11... | collective-permute-start | bytes 983048 | tf_op jit(solution)/shard_map/ppermute | solution.py:225
  45.8 1.0 copy-start

commit v7 on v6

--- a/solution.py
+++ b/solution.py
@@ -226,9 +226,9 @@
 
     other = send(own, 1, 0, 0)
     right, left = send(own, 0, 1, 0), send(own, 0, -1, 0)
+    other, weight = lax.optimization_barrier((other, weight))
     other_left = send(other, 0, -1, 0)
     other_right = send(right, 1, 0, 0)
-    right, weight = lax.optimization_barrier((right, weight))
     across = send(right, 0, 1, 0)
     other_right, other_left = lax.optimization_barrier((other_right, other_left))
     other_across = send(other_left, 0, -1, 0)

time: 101 us -> 101 us (level)
  no operation moved by 1% of the time
where the time goes in v7:
time: 101 us; the launch traced here: 99.5 us
  blocking collectives  35 us (35%)
  Pallas kernels  24.1 us (24%)
  waiting for transfers between devices  19.8 us (20%)
  starting transfers between devices  16.8 us (17%)
  local copies, waits for them, and re-layouts  2.59 us (3%)
  other arithmetic  1.2 us (1%)
    all_to_all x2, blocking collectives, exchange(): lax.all_to_all(array, axis_name, split_axis=0, concat_axis=0, tiled=True)  35 us
    pallas_call x1, Pallas kernels, head_gradient(): pl.pallas_call(functools.partial(head_kernel, 256), out_shape=jax.ShapeDt...  16.5 us
    ppermute x15, starting transfers between devices, send(): return lax.ppermute(array, 'seq', [(i, over(i, *by)) for i in range(count)])  13.2 us
    ppermute x15, waiting for transfers between devices, send(): return lax.ppermute(array, 'seq', [(i, over(i, *by)) for i in range(count)])  11.7 us
    all_to_all x1, waiting for transfers between devices, exchange(): lax.all_to_all(array, axis_name, split_axis=0, concat_axis=0, tiled=True)  8.12 us
    pallas_call x1, Pallas kernels, learn_tokens(): pl.pallas_call(functools.partial(tokens_kernel, math.gcd(count, 4), 4), o...  7.58 us
    all_to_all x1, starting transfers between devices, exchange(): lax.all_to_all(array, axis_name, split_axis=0, concat_axis=0, tiled=True)  3.54 us
  transfers between devices with their start and end apart: 16, of which 7 were waited for; matrix products, arithmetic and copies ran while one was open for 2% of the time, Pallas kernels for 0%

profile of v7, /device:TPU:0, one launch (start us, length us, event | category | flops | bytes accessed | tf_op | source)
XLA Modules:
  0.0 99.5 jit_solution(2464957856333686690)
XLA Ops:
  0.0 7.6 %learn_tokens.1 = (bf16[128,1280]{1,0:T(8,128)(2,1)}, bf16[16,80,128]{2,1,0:T(8,128)(2,1)}) custom-call(bf16[16,256,1280]{2,1,0:T(8,128)(2,1)} %bitcast.24, bf16[8,1280]{1,0:T(8,128)(2,1)} %bitcast.27, bf16[128,1280]{1,0:T(8,128)(2,1)} %bitcast.26), custom_call_target="tpu_custom_call" | custom-call | tf_op jit(solution)/shard_map/learn_tokens/pallas_call | solution.py:71
  7.6 2.1 %collective-permute-start.2 = (bf16[128,1280]{1,0:T(8,128)(2,1)}, bf16[128,1280]{1,0:T(8,128)(2,1)S(1)}, u32[]{:S(2)}, u32[]{:S(2)}) collective-permute-start(bf16[128,1280]{1,0:T(8,128)(2,1)} %get-tuple-element.13.refs_0_), channel_id=1, source_target_pairs={{0,8},{1,9},{2,10},{3,11},{4,12},{5,13},{6,14},{7,15},{8,0},{9,1},... | collective-permute-start | bytes 983048 | tf_op jit(solution)/shard_map/ppermute | solution.py:225
  9.7 1.5 %collective-permute-start = (bf16[128,1280]{1,0:T(8,128)(2,1)}, bf16[128,1280]{1,0:T(8,128)(2,1)S(1)}, u32[]{:S(2)}, u32[]{:S(2)}) collective-permute-start(bf16[128,1280]{1,0:T(8,128)(2,1)} %get-tuple-element.13.refs_0_), channel_id=1, source_target_pairs={{0,2},{1,3},{2,4},{3,5},{4,6},{5,7},{6,0},{7,1},{8,10},{9,11},{10,... | collective-permute-start | bytes 983048 | tf_op jit(solution)/shard_map/ppermute | solution.py:225
  11.2 1.7 %collective-permute-start.3 = (bf16[128,1280]{1,0:T(8,128)(2,1)}, bf16[128,1280]{1,0:T(8,128)(2,1)S(1)}, u32[]{:S(2)}, u32[]{:S(2)}) collective-permute-start(bf16[128,1280]{1,0:T(8,128)(2,1)} %get-tuple-element.13.refs_0_), channel_id=1, source_target_pairs={{0,6},{1,7},{2,0},{3,1},{4,2},{5,3},{6,4},{7,5},{8,14},{9,15},{10,... | collective-permute-start | bytes 983048 | tf_op jit(solution)/shard_map/ppermute | solution.py:225
  12.9 1.5 %constant_dynamic-slice_fusion.weight_ref = bf16[1280,240]{1,0:T(8,128)(2,1)S(1)} fusion(bf16[1280,3840]{1,0:T(8,128)(2,1)} %param.6, s32[]{:T(128)S(6)} %select_n.162), kind=kLoop, calls=%fused_computation.1 | loop fusion | bytes 1228804 | tf_op jit(solution)/shard_map/dynamic_slice | solution.py:250
  14.4 3.2 %collective-permute-done.2.refs_1_ = bf16[128,1280]{1,0:T(8,128)(2,1)S(1)} collective-permute-done((bf16[128,1280]{1,0:T(8,128)(2,1)}, bf16[128,1280]{1,0:T(8,128)(2,1)S(1)}, u32[]{:S(2)}, u32[]{:S(2)}) %collective-permute-start.2) | collective-permute-done | bytes 327712 | tf_op jit(solution)/shard_map/ppermute | solution.py:225
  17.6 2.8 %collective-permute-start.5 = (bf16[128,1280]{1,0:T(8,128)(2,1)S(1)}, bf16[128,1280]{1,0:T(8,128)(2,1)S(1)}, u32[]{:S(2)}, u32[]{:S(2)}) collective-permute-start(bf16[128,1280]{1,0:T(8,128)(2,1)S(1)} %collective-permute-done.2.refs_1_), channel_id=1, source_target_pairs={{0,6},{1,7},{2,0},{3,1},{4,2},{5,3},{6,4},{7,5},{8,14},{9,15},{10,... | collective-permute-start | bytes 983048 | tf_op jit(solution)/shard_map/ppermute | solution.py:225
  20.4 0.0 collective-permute-done.refs_2_
  20.4 1.7 %collective-permute-start.4 = (bf16[128,1280]{1,0:T(8,128)(2,1)S(1)}, bf16[128,1280]{1,0:T(8,128)(2,1)S(1)}, u32[]{:S(2)}, u32[]{:S(2)}) collective-permute-start(bf16[128,1280]{1,0:T(8,128)(2,1)S(1)} %collective-permute-done.refs_2_), channel_id=1, source_target_pairs={{0,8},{1,9},{2,10},{3,11},{4,12},{5,13},{6,14},{7,15},{8,0},{9,1},... | collective-permute-start | bytes 983048 | tf_op jit(solution)/shard_map/ppermute | solution.py:225
  22.1 0.0 collective-permute-start.1
  22.1 0.0 collective-permute-start.7
  22.1 0.0 collective-permute-done.3.refs_3_
  22.1 0.5 collective-permute-start.10
  22.6 4.7 %collective-permute-done.5.refs_5_ = bf16[128,1280]{1,0:T(8,128)(2,1)S(1)} collective-permute-done((bf16[128,1280]{1,0:T(8,128)(2,1)S(1)}, bf16[128,1280]{1,0:T(8,128)(2,1)S(1)}, u32[]{:S(2)}, u32[]{:S(2)}) %collective-permute-start.5) | collective-permute-done | bytes 327712 | tf_op jit(solution)/shard_map/ppermute | solution.py:225
  27.3 0.0 collective-permute-start.8
  27.3 1.6 %collective-permute-done.4.refs_4_ = bf16[128,1280]{1,0:T(8,128)(2,1)S(1)} collective-permute-done((bf16[128,1280]{1,0:T(8,128)(2,1)S(1)}, bf16[128,1280]{1,0:T(8,128)(2,1)S(1)}, u32[]{:S(2)}, u32[]{:S(2)}) %collective-permute-start.4) | collective-permute-done | bytes 327712 | tf_op jit(solution)/shard_map/ppermute | solution.py:225
  28.9 1.5 %collective-permute-start.6 = (bf16[128,1280]{1,0:T(8,128)(2,1)S(1)}, bf16[128,1280]{1,0:T(8,128)(2,1)}, u32[]{:S(2)}, u32[]{:S(2)}) collective-permute-start(bf16[128,1280]{1,0:T(8,128)(2,1)S(1)} %collective-permute-done.5.refs_5_), channel_id=1, source_target_pairs={{0,6},{1,7},{2,0},{3,1},{4,2},{5,3},{6,4},{7,5},{8,14},{9,15},{10,... | collective-permute-start | bytes 983048 | tf_op jit(solution)/shard_map/ppermute | solution.py:225
  30.3 3.5 %all-to-all-start = ((bf16[16,80,128]{2,1,0:T(8,128)(2,1)}), bf16[16,80,128]{2,1,0:T(8,128)(2,1)S(1)}, u32[]{:S(2)}, u32[]{:S(2)}) async-start(bf16[16,80,128]{2,1,0:T(8,128)(2,1)} %get-tuple-element.14), calls=%async_computation | async-start | bytes 655360 | tf_op jit(solution)/shard_map/all_to_all | solution.py:210
  33.9 0.0 collective-permute-done.1.refs_6_
  33.9 0.4 collective-permute-start.9
  34.3 8.1 %all-to-all-done.cot_ref = bf16[16,80,128]{2,1,0:T(8,128)(2,1)S(1)} async-done(((bf16[16,80,128]{2,1,0:T(8,128)(2,1)}), bf16[16,80,128]{2,1,0:T(8,128)(2,1)S(1)}, u32[]{:S(2)}, u32[]{:S(2)}) %all-to-all-start) | async-done | bytes 327712 | tf_op jit(solution)/shard_map/all_to_all | solution.py:210
  42.4 0.0 collective-permute-done.7.refs_8_
  42.4 0.0 collective-permute-start.12
  42.4 0.0 collective-permute-done.10.refs_11_
  42.4 0.5 collective-permute-start.11
  42.9 0.0 collective-permute-done.8.refs_9_
  42.9 0.1 collective-permute-start.13
  43.0 0.0 collective-permute-done.6.refs_7_
  43.0 0.4 collective-permute-start.14
  43.4 0.1 stack.67.order_ref
  43.5 0.0 collective-permute-done.9.refs_10_
  43.5 1.1 %collective-permute-done.11.refs_12_ = bf16[128,1280]{1,0:T(8,128)(2,1)} collective-permute-done((bf16[128,1280]{1,0:T(8,128)(2,1)S(1)}, bf16[128,1280]{1,0:T(8,128)(2,1)}, u32[]{:S(2)}, u32[]{:S(2)}) %collective-permute-start.11) | collective-permute-done | bytes 327712 | tf_op jit(solution)/shard_map/ppermute | solution.py:225
  44.6 0.0 collective-permute-done.12.refs_13_
  44.6 0.9 collective-permute-done.13.refs_14_
  45.6 0.2 collective-permute-done.14.refs_15_
  45.8 0.0 copy-start
  45.8 1.0 copy-done
  46.8 16.5 %head_gradient.1 = bf16[256,1280]{1,0:T(8,128)(2,1)S(1)} custom-call(s32[16]{0:T(128)S(1)} %stack.67.order_ref, bf16[16,80,128]{2,1,0:T(8,128)(2,1)S(1)} %all-to-all-done.cot_ref, bf16[1280,240]{1,0:T(8,128)(2,1)S(1)} %constant_dynamic-slice_fusion.weight_ref, bf16[128,1280]{1,0:T(8,128)(2,1)S(1)} %copy-done, ...), custom_call_target="tpu_custom_call" | custom-call | flops 6442450944 | bytes 8388608 | tf_op jit(solution)/shard_map/head_gradient/pallas_call | solution.py:186
  63.3 20.3 %all_to_all.15 = bf16[8,32,1280]{2,1,0:T(8,128)(2,1)S(1)} all-to-all(bf16[8,32,1280]{2,1,0:T(8,128)(2,1)S(1)} %bitcast.23), channel_id=1, replica_groups=mesh['dp'=8,'seq'=16] {'dp'}, dimensions={0} | all-to-all | bytes 1310720 | tf_op jit(solution)/shard_map/all_to_all | solution.py:210
  83.6 0.1 reduce_sum.12
  83.7 14.7 %all_to_all.16 = bf16[8,32,1280]{2,1,0:T(8,128)(2,1)S(1)} all-to-all(bf16[8,32,1280]{2,1,0:T(8,128)(2,1)S(1)} %broadcast_in_dim.2), channel_id=1, replica_groups=mesh['dp'=8,'seq'=16] {'dp'}, dimensions={0} | all-to-all | bytes 1310720 | tf_op jit(solution)/shard_map/all_to_all | solution.py:210
  98.4 1.1 %convert_bitcast_fusion = f32[1280,240]{0,1:T(8,128)} fusion(bf16[256,1280]{1,0:T(8,128)(2,1)S(1)} %bitcast.25), kind=kLoop, calls=%fused_computation | loop fusion | flops 307200 | bytes 1843200 | tf_op jit(solution)/shard_map/transpose | solution.py:256
  (1 shorter events, 0.0 us)
Async XLA Ops:
  7.6 10.0 %collective-permute-start.2 = (bf16[128,1280]{1,0:T(8,128)(2,1)}, bf16[128,1280]{1,0:T(8,128)(2,1)S(1)}, u32[]{:S(2)}, u32[]{:S(2)}) collective-permute-start(bf16[128,1280]{1,0:T(8,128)(2,1)} %get-tuple-element.13.refs_0_), channel_id=1, source_target_pairs={{0,8},{1,9},{2,10},{3,11},{4,12},{5,13},{6,14},{7,15},{8,0},{9,1},... | collective-permute-start | bytes 983048 | tf_op jit(solution)/shard_map/ppermute | solution.py:225
  9.7 10.7 %collective-permute-start = (bf16[128,1280]{1,0:T(8,128)(2,1)}, bf16[128,1280]{1,0:T(8,128)(2,1)S(1)}, u32[]{:S(2)}, u32[]{:S(2)}) collective-permute-start(bf16[128,1280]{1,0:T(8,128)(2,1)} %get-tuple-element.13.refs_0_), channel_id=1, source_target_pairs={{0,2},{1,3},{2,4},{3,5},{4,6},{5,7},{6,0},{7,1},{8,10},{9,11},{10,... | collective-permute-start | bytes 983048 | tf_op jit(solution)/shard_map/ppermute | solution.py:225
  11.2 10.9 %collective-permute-start.3 = (bf16[128,1280]{1,0:T(8,128)(2,1)}, bf16[128,1280]{1,0:T(8,128)(2,1)S(1)}, u32[]{:S(2)}, u32[]{:S(2)}) collective-permute-start(bf16[128,1280]{1,0:T(8,128)(2,1)} %get-tuple-element.13.refs_0_), channel_id=1, source_target_pairs={{0,6},{1,7},{2,0},{3,1},{4,2},{5,3},{6,4},{7,5},{8,14},{9,15},{10,... | collective-permute-start | bytes 983048 | tf_op jit(solution)/shard_map/ppermute | solution.py:225
  17.6 9.7 %collective-permute-start.5 = (bf16[128,1280]{1,0:T(8,128)(2,1)S(1)}, bf16[128,1280]{1,0:T(8,128)(2,1)S(1)}, u32[]{:S(2)}, u32[]{:S(2)}) collective-permute-start(bf16[128,1280]{1,0:T(8,128)(2,1)S(1)} %collective-permute-done.2.refs_1_), channel_id=1, source_target_pairs={{0,6},{1,7},{2,0},{3,1},{4,2},{5,3},{6,4},{7,5},{8,14},{9,15},{10,... | collective-permute-start | bytes 983048 | tf_op jit(solution)/shard_map/ppermute | solution.py:225
  20.4 8.5 %collective-permute-start.4 = (bf16[128,1280]{1,0:T(8,128)(2,1)S(1)}, bf16[128,1280]{1,0:T(8,128)(2,1)S(1)}, u32[]{:S(2)}, u32[]{:S(2)}) collective-permute-start(bf16[128,1280]{1,0:T(8,128)(2,1)S(1)} %collective-permute-done.refs_2_), channel_id=1, source_target_pairs={{0,8},{1,9},{2,10},{3,11},{4,12},{5,13},{6,14},{7,15},{8,0},{9,1},... | collective-permute-start | bytes 983048 | tf_op jit(solution)/shard_map/ppermute | solution.py:225
  22.1 11.8 %collective-permute-start.1 = (bf16[128,1280]{1,0:T(8,128)(2,1)S(1)}, bf16[128,1280]{1,0:T(8,128)(2,1)S(1)}, u32[]{:S(2)}, u32[]{:S(2)}) collective-permute-start(bf16[128,1280]{1,0:T(8,128)(2,1)S(1)} %collective-permute-done.refs_2_), channel_id=1, source_target_pairs={{0,2},{1,3},{2,4},{3,5},{4,6},{5,7},{6,0},{7,1},{8,10},{9,11},{10,... | collective-permute-start | bytes 983048 | tf_op jit(solution)/shard_map/ppermute | solution.py:225
  22.1 20.3 %collective-permute-start.7 = (bf16[128,1280]{1,0:T(8,128)(2,1)}, bf16[128,1280]{1,0:T(8,128)(2,1)S(1)}, u32[]{:S(2)}, u32[]{:S(2)}) collective-permute-start(bf16[128,1280]{1,0:T(8,128)(2,1)} %get-tuple-element.13.refs_0_), channel_id=1, source_target_pairs={{0,1},{1,0},{2,3},{3,2},{4,5},{5,4},{6,7},{7,6},{8,9},{9,8},{10,11... | collective-permute-start | bytes 983048 | tf_op jit(solution)/shard_map/ppermute | solution.py:225
  22.1 20.3 %collective-permute-start.10 = (bf16[128,1280]{1,0:T(8,128)(2,1)S(1)}, bf16[128,1280]{1,0:T(8,128)(2,1)}, u32[]{:S(2)}, u32[]{:S(2)}) collective-permute-start(bf16[128,1280]{1,0:T(8,128)(2,1)S(1)} %collective-permute-done.3.refs_3_), channel_id=1, source_target_pairs={{0,1},{1,0},{2,3},{3,2},{4,5},{5,4},{6,7},{7,6},{8,9},{9,8},{10,11... | collective-permute-start | bytes 983048 | tf_op jit(solution)/shard_map/ppermute | solution.py:225
  27.3 15.6 %collective-permute-start.8 = (bf16[128,1280]{1,0:T(8,128)(2,1)S(1)}, bf16[128,1280]{1,0:T(8,128)(2,1)}, u32[]{:S(2)}, u32[]{:S(2)}) collective-permute-start(bf16[128,1280]{1,0:T(8,128)(2,1)S(1)} %collective-permute-done.2.refs_1_), channel_id=1, source_target_pairs={{0,1},{1,0},{2,3},{3,2},{4,5},{5,4},{6,7},{7,6},{8,9},{9,8},{10,11... | collective-permute-start | bytes 983048 | tf_op jit(solution)/shard_map/ppermute | solution.py:225
  28.9 14.2 %collective-permute-start.6 = (bf16[128,1280]{1,0:T(8,128)(2,1)S(1)}, bf16[128,1280]{1,0:T(8,128)(2,1)}, u32[]{:S(2)}, u32[]{:S(2)}) collective-permute-start(bf16[128,1280]{1,0:T(8,128)(2,1)S(1)} %collective-permute-done.5.refs_5_), channel_id=1, source_target_pairs={{0,6},{1,7},{2,0},{3,1},{4,2},{5,3},{6,4},{7,5},{8,14},{9,15},{10,... | collective-permute-start | bytes 983048 | tf_op jit(solution)/shard_map/ppermute | solution.py:225
  30.3 12.0 %all-to-all-start = ((bf16[16,80,128]{2,1,0:T(8,128)(2,1)}), bf16[16,80,128]{2,1,0:T(8,128)(2,1)S(1)}, u32[]{:S(2)}, u32[]{:S(2)}) async-start(bf16[16,80,128]{2,1,0:T(8,128)(2,1)} %get-tuple-element.14), calls=%async_computation | async-start | bytes 655360 | tf_op jit(solution)/shard_map/all_to_all | solution.py:210
  33.9 9.6 %collective-permute-start.9 = (bf16[128,1280]{1,0:T(8,128)(2,1)S(1)}, bf16[128,1280]{1,0:T(8,128)(2,1)}, u32[]{:S(2)}, u32[]{:S(2)}) collective-permute-start(bf16[128,1280]{1,0:T(8,128)(2,1)S(1)} %collective-permute-done.refs_2_), channel_id=1, source_target_pairs={{0,1},{1,0},{2,3},{3,2},{4,5},{5,4},{6,7},{7,6},{8,9},{9,8},{10,11... | collective-permute-start | bytes 983048 | tf_op jit(solution)/shard_map/ppermute | solution.py:225
  42.4 2.2 %collective-permute-start.12 = (bf16[128,1280]{1,0:T(8,128)(2,1)S(1)}, bf16[128,1280]{1,0:T(8,128)(2,1)}, u32[]{:S(2)}, u32[]{:S(2)}) collective-permute-start(bf16[128,1280]{1,0:T(8,128)(2,1)S(1)} %collective-permute-done.5.refs_5_), channel_id=1, source_target_pairs={{0,1},{1,0},{2,3},{3,2},{4,5},{5,4},{6,7},{7,6},{8,9},{9,8},{10,11... | collective-permute-start | bytes 983048 | tf_op jit(solution)/shard_map/ppermute | solution.py:225
  42.4 2.2 %collective-permute-start.11 = (bf16[128,1280]{1,0:T(8,128)(2,1)S(1)}, bf16[128,1280]{1,0:T(8,128)(2,1)}, u32[]{:S(2)}, u32[]{:S(2)}) collective-permute-start(bf16[128,1280]{1,0:T(8,128)(2,1)S(1)} %collective-permute-done.4.refs_4_), channel_id=1, source_target_pairs={{0,1},{1,0},{2,3},{3,2},{4,5},{5,4},{6,7},{7,6},{8,9},{9,8},{10,11... | collective-permute-start | bytes 983048 | tf_op jit(solution)/shard_map/ppermute | solution.py:225
  42.9 2.6 %collective-permute-start.13 = (bf16[128,1280]{1,0:T(8,128)(2,1)S(1)}, bf16[128,1280]{1,0:T(8,128)(2,1)}, u32[]{:S(2)}, u32[]{:S(2)}) collective-permute-start(bf16[128,1280]{1,0:T(8,128)(2,1)S(1)} %collective-permute-done.1.refs_6_), channel_id=1, source_target_pairs={{0,1},{1,0},{2,3},{3,2},{4,5},{5,4},{6,7},{7,6},{8,9},{9,8},{10,11... | collective-permute-start | bytes 983048 | tf_op jit(solution)/shard_map/ppermute | solution.py:225
  43.0 2.8 %collective-permute-start.14 = (bf16[128,1280]{1,0:T(8,128)(2,1)}, bf16[128,1280]{1,0:T(8,128)(2,1)}, u32[]{:S(2)}, u32[]{:S(2)}) collective-permute-start(bf16[128,1280]{1,0:T(8,128)(2,1)} %collective-permute-done.6.refs_7_), channel_id=1, source_target_pairs={{0,1},{1,0},{2,3},{3,2},{4,5},{5,4},{6,7},{7,6},{8,9},{9,8},{10,11... | collective-permute-start | bytes 983048 | tf_op jit(solution)/shard_map/ppermute | solution.py:225
  45.8 1.0 copy-start

commit v8 on v7

--- a/solution.py
+++ b/solution.py
@@ -139,7 +139,9 @@
             lane == 0, first, jnp.where(lane == 1, second, jnp.where(lane == 2, third, 0.0))
         ).astype(BF16)
         difference = matmul(jnp.concatenate([cot, tail], axis=1), v1[...])
-        state[s].update(cot_t=cot_t, inverse=inverse, difference=difference)
+        inverse_t = jnp.broadcast_to(inverse, (sub, LANES)).T[0:1, :]
+        cot_scaled[:, rows(s)] = (cot_t.astype(F32) * inverse_t).astype(BF16)
+        state[s].update(inverse=inverse, inverse_t=inverse_t, difference=difference)
 
     def grad_score(s):
         grad_scores = (state[s]["shifted"].astype(F32) * state[s].pop("difference")).astype(BF16)
@@ -150,9 +152,8 @@
         inverse = state[s]["inverse"]
         product = matmul(state[s]["grad_scores"], k3[0:hd, :], ((1,), (1,))) * (inverse * scale)
         grads[0:hd, rows(s)] = product.T.astype(BF16)
-        inverse_t = jnp.broadcast_to(inverse, (sub, LANES)).T[0:1, :]
+        inverse_t = state[s]["inverse_t"]
         query_scaled[:, rows(s)] = (state[s]["query"] * (inverse_t * scale)).astype(BF16)
-        cot_scaled[:, rows(s)] = (state[s]["cot_t"].astype(F32) * inverse_t).astype(BF16)
         state[s].clear()
 
     def both(stage, pair):
@@ -166,10 +167,11 @@
         both(score, pair + 1)
         both(attend, pair)
         both(exponent, pair + 1)
+        if pair == blocks // 2 - 1:
+            grads[2 * hd : 3 * hd, :] = matmul(cot_scaled[...], shifted_all[...]).astype(BF16)
         both(grad_score, pair)
         both(grad_query, pair)
     grads[hd : 2 * hd, :] = matmul(query_scaled[...], scores_all[...]).astype(BF16)
-    grads[2 * hd : 3 * hd, :] = matmul(cot_scaled[...], shifted_all[...]).astype(BF16)
     grads[3 * hd :, :] = jnp.zeros((grads.shape[0] - 3 * hd, count), BF16)
     total = None
     for at in range(0, pieces, join):

time: 101 us -> 101 us (level)
  no operation moved by 1% of the time
where the time goes in v8:
time: 101 us; the launch traced here: 99.5 us
  blocking collectives  34.9 us (35%)
  Pallas kernels  24.2 us (24%)
  waiting for transfers between devices  19.8 us (20%)
  starting transfers between devices  16.7 us (17%)
  local copies, waits for them, and re-layouts  2.59 us (3%)
  other arithmetic  1.2 us (1%)
    all_to_all x2, blocking collectives, exchange(): lax.all_to_all(array, axis_name, split_axis=0, concat_axis=0, tiled=True)  34.9 us
    pallas_call x1, Pallas kernels, head_gradient(): pl.pallas_call(functools.partial(head_kernel, 256), out_shape=jax.ShapeDt...  16.6 us
    ppermute x15, starting transfers between devices, send(): return lax.ppermute(array, 'seq', [(i, over(i, *by)) for i in range(count)])  13.2 us
    ppermute x15, waiting for transfers between devices, send(): return lax.ppermute(array, 'seq', [(i, over(i, *by)) for i in range(count)])  11.7 us
    all_to_all x1, waiting for transfers between devices, exchange(): lax.all_to_all(array, axis_name, split_axis=0, concat_axis=0, tiled=True)  8.12 us
    pallas_call x1, Pallas kernels, learn_tokens(): pl.pallas_call(functools.partial(tokens_kernel, math.gcd(count, 4), 4), o...  7.58 us
    all_to_all x1, starting transfers between devices, exchange(): lax.all_to_all(array, axis_name, split_axis=0, concat_axis=0, tiled=True)  3.54 us
  transfers between devices with their start and end apart: 16, of which 7 were waited for; matrix products, arithmetic and copies ran while one was open for 2% of the time, Pallas kernels for 0%

profile of v8, /device:TPU:0, one launch (start us, length us, event | category | flops | bytes accessed | tf_op | source)
XLA Modules:
  0.0 99.5 jit_solution(10698734888740655030)
XLA Ops:
  0.0 7.6 %learn_tokens.1 = (bf16[128,1280]{1,0:T(8,128)(2,1)}, bf16[16,80,128]{2,1,0:T(8,128)(2,1)}) custom-call(bf16[16,256,1280]{2,1,0:T(8,128)(2,1)} %bitcast.24, bf16[8,1280]{1,0:T(8,128)(2,1)} %bitcast.27, bf16[128,1280]{1,0:T(8,128)(2,1)} %bitcast.26), custom_call_target="tpu_custom_call" | custom-call | tf_op jit(solution)/shard_map/learn_tokens/pallas_call | solution.py:71
  7.6 2.1 %collective-permute-start.2 = (bf16[128,1280]{1,0:T(8,128)(2,1)}, bf16[128,1280]{1,0:T(8,128)(2,1)S(1)}, u32[]{:S(2)}, u32[]{:S(2)}) collective-permute-start(bf16[128,1280]{1,0:T(8,128)(2,1)} %get-tuple-element.13.refs_0_), channel_id=1, source_target_pairs={{0,8},{1,9},{2,10},{3,11},{4,12},{5,13},{6,14},{7,15},{8,0},{9,1},... | collective-permute-start | bytes 983048 | tf_op jit(solution)/shard_map/ppermute | solution.py:227
  9.7 1.5 %collective-permute-start = (bf16[128,1280]{1,0:T(8,128)(2,1)}, bf16[128,1280]{1,0:T(8,128)(2,1)S(1)}, u32[]{:S(2)}, u32[]{:S(2)}) collective-permute-start(bf16[128,1280]{1,0:T(8,128)(2,1)} %get-tuple-element.13.refs_0_), channel_id=1, source_target_pairs={{0,2},{1,3},{2,4},{3,5},{4,6},{5,7},{6,0},{7,1},{8,10},{9,11},{10,... | collective-permute-start | bytes 983048 | tf_op jit(solution)/shard_map/ppermute | solution.py:227
  11.2 1.7 %collective-permute-start.3 = (bf16[128,1280]{1,0:T(8,128)(2,1)}, bf16[128,1280]{1,0:T(8,128)(2,1)S(1)}, u32[]{:S(2)}, u32[]{:S(2)}) collective-permute-start(bf16[128,1280]{1,0:T(8,128)(2,1)} %get-tuple-element.13.refs_0_), channel_id=1, source_target_pairs={{0,6},{1,7},{2,0},{3,1},{4,2},{5,3},{6,4},{7,5},{8,14},{9,15},{10,... | collective-permute-start | bytes 983048 | tf_op jit(solution)/shard_map/ppermute | solution.py:227
  12.9 1.5 %constant_dynamic-slice_fusion.weight_ref = bf16[1280,240]{1,0:T(8,128)(2,1)S(1)} fusion(bf16[1280,3840]{1,0:T(8,128)(2,1)} %param.6, s32[]{:T(128)S(6)} %select_n.162), kind=kLoop, calls=%fused_computation.1 | loop fusion | bytes 1228804 | tf_op jit(solution)/shard_map/dynamic_slice | solution.py:252
  14.4 3.2 %collective-permute-done.2.refs_1_ = bf16[128,1280]{1,0:T(8,128)(2,1)S(1)} collective-permute-done((bf16[128,1280]{1,0:T(8,128)(2,1)}, bf16[128,1280]{1,0:T(8,128)(2,1)S(1)}, u32[]{:S(2)}, u32[]{:S(2)}) %collective-permute-start.2) | collective-permute-done | bytes 327712 | tf_op jit(solution)/shard_map/ppermute | solution.py:227
  17.6 2.8 %collective-permute-start.5 = (bf16[128,1280]{1,0:T(8,128)(2,1)S(1)}, bf16[128,1280]{1,0:T(8,128)(2,1)S(1)}, u32[]{:S(2)}, u32[]{:S(2)}) collective-permute-start(bf16[128,1280]{1,0:T(8,128)(2,1)S(1)} %collective-permute-done.2.refs_1_), channel_id=1, source_target_pairs={{0,6},{1,7},{2,0},{3,1},{4,2},{5,3},{6,4},{7,5},{8,14},{9,15},{10,... | collective-permute-start | bytes 983048 | tf_op jit(solution)/shard_map/ppermute | solution.py:227
  20.4 0.0 collective-permute-done.refs_2_
  20.4 1.7 %collective-permute-start.4 = (bf16[128,1280]{1,0:T(8,128)(2,1)S(1)}, bf16[128,1280]{1,0:T(8,128)(2,1)S(1)}, u32[]{:S(2)}, u32[]{:S(2)}) collective-permute-start(bf16[128,1280]{1,0:T(8,128)(2,1)S(1)} %collective-permute-done.refs_2_), channel_id=1, source_target_pairs={{0,8},{1,9},{2,10},{3,11},{4,12},{5,13},{6,14},{7,15},{8,0},{9,1},... | collective-permute-start | bytes 983048 | tf_op jit(solution)/shard_map/ppermute | solution.py:227
  22.1 0.0 collective-permute-start.1
  22.1 0.0 collective-permute-start.7
  22.1 0.0 collective-permute-done.3.refs_3_
  22.1 0.5 collective-permute-start.10
  22.6 4.7 %collective-permute-done.5.refs_5_ = bf16[128,1280]{1,0:T(8,128)(2,1)S(1)} collective-permute-done((bf16[128,1280]{1,0:T(8,128)(2,1)S(1)}, bf16[128,1280]{1,0:T(8,128)(2,1)S(1)}, u32[]{:S(2)}, u32[]{:S(2)}) %collective-permute-start.5) | collective-permute-done | bytes 327712 | tf_op jit(solution)/shard_map/ppermute | solution.py:227
  27.3 0.0 collective-permute-start.8
  27.3 1.6 %collective-permute-done.4.refs_4_ = bf16[128,1280]{1,0:T(8,128)(2,1)S(1)} collective-permute-done((bf16[128,1280]{1,0:T(8,128)(2,1)S(1)}, bf16[128,1280]{1,0:T(8,128)(2,1)S(1)}, u32[]{:S(2)}, u32[]{:S(2)}) %collective-permute-start.4) | collective-permute-done | bytes 327712 | tf_op jit(solution)/shard_map/ppermute | solution.py:227
  28.9 1.5 %collective-permute-start.6 = (bf16[128,1280]{1,0:T(8,128)(2,1)S(1)}, bf16[128,1280]{1,0:T(8,128)(2,1)}, u32[]{:S(2)}, u32[]{:S(2)}) collective-permute-start(bf16[128,1280]{1,0:T(8,128)(2,1)S(1)} %collective-permute-done.5.refs_5_), channel_id=1, source_target_pairs={{0,6},{1,7},{2,0},{3,1},{4,2},{5,3},{6,4},{7,5},{8,14},{9,15},{10,... | collective-permute-start | bytes 983048 | tf_op jit(solution)/shard_map/ppermute | solution.py:227
  30.3 3.5 %all-to-all-start = ((bf16[16,80,128]{2,1,0:T(8,128)(2,1)}), bf16[16,80,128]{2,1,0:T(8,128)(2,1)S(1)}, u32[]{:S(2)}, u32[]{:S(2)}) async-start(bf16[16,80,128]{2,1,0:T(8,128)(2,1)} %get-tuple-element.14), calls=%async_computation | async-start | bytes 655360 | tf_op jit(solution)/shard_map/all_to_all | solution.py:212
  33.9 0.0 collective-permute-done.1.refs_6_
  33.9 0.4 collective-permute-start.9
  34.3 8.1 %all-to-all-done.cot_ref = bf16[16,80,128]{2,1,0:T(8,128)(2,1)S(1)} async-done(((bf16[16,80,128]{2,1,0:T(8,128)(2,1)}), bf16[16,80,128]{2,1,0:T(8,128)(2,1)S(1)}, u32[]{:S(2)}, u32[]{:S(2)}) %all-to-all-start) | async-done | bytes 327712 | tf_op jit(solution)/shard_map/all_to_all | solution.py:212
  42.4 0.0 collective-permute-done.7.refs_8_
  42.4 0.0 collective-permute-start.12
  42.4 0.0 collective-permute-done.10.refs_11_
  42.4 0.5 collective-permute-start.11
  42.9 0.0 collective-permute-done.8.refs_9_
  42.9 0.1 collective-permute-start.13
  43.0 0.0 collective-permute-done.6.refs_7_
  43.0 0.4 collective-permute-start.14
  43.4 0.1 stack.67.order_ref
  43.5 0.0 collective-permute-done.9.refs_10_
  43.5 1.1 %collective-permute-done.11.refs_12_ = bf16[128,1280]{1,0:T(8,128)(2,1)} collective-permute-done((bf16[128,1280]{1,0:T(8,128)(2,1)S(1)}, bf16[128,1280]{1,0:T(8,128)(2,1)}, u32[]{:S(2)}, u32[]{:S(2)}) %collective-permute-start.11) | collective-permute-done | bytes 327712 | tf_op jit(solution)/shard_map/ppermute | solution.py:227
  44.6 0.0 collective-permute-done.12.refs_13_
  44.6 0.9 collective-permute-done.13.refs_14_
  45.6 0.2 collective-permute-done.14.refs_15_
  45.8 0.0 copy-start
  45.8 1.0 copy-done
  46.8 16.6 %head_gradient.1 = bf16[256,1280]{1,0:T(8,128)(2,1)S(1)} custom-call(s32[16]{0:T(128)S(1)} %stack.67.order_ref, bf16[16,80,128]{2,1,0:T(8,128)(2,1)S(1)} %all-to-all-done.cot_ref, bf16[1280,240]{1,0:T(8,128)(2,1)S(1)} %constant_dynamic-slice_fusion.weight_ref, bf16[128,1280]{1,0:T(8,128)(2,1)S(1)} %copy-done, ...), custom_call_target="tpu_custom_call" | custom-call | flops 6442450944 | bytes 8388608 | tf_op jit(solution)/shard_map/head_gradient/pallas_call | solution.py:188
  63.3 20.3 %all_to_all.15 = bf16[8,32,1280]{2,1,0:T(8,128)(2,1)S(1)} all-to-all(bf16[8,32,1280]{2,1,0:T(8,128)(2,1)S(1)} %bitcast.23), channel_id=1, replica_groups=mesh['dp'=8,'seq'=16] {'dp'}, dimensions={0} | all-to-all | bytes 1310720 | tf_op jit(solution)/shard_map/all_to_all | solution.py:212
  83.7 0.1 reduce_sum.12
  83.8 14.6 %all_to_all.16 = bf16[8,32,1280]{2,1,0:T(8,128)(2,1)S(1)} all-to-all(bf16[8,32,1280]{2,1,0:T(8,128)(2,1)S(1)} %broadcast_in_dim.2), channel_id=1, replica_groups=mesh['dp'=8,'seq'=16] {'dp'}, dimensions={0} | all-to-all | bytes 1310720 | tf_op jit(solution)/shard_map/all_to_all | solution.py:212
  98.4 1.1 %convert_bitcast_fusion = f32[1280,240]{0,1:T(8,128)} fusion(bf16[256,1280]{1,0:T(8,128)(2,1)S(1)} %bitcast.25), kind=kLoop, calls=%fused_computation | loop fusion | flops 307200 | bytes 1843200 | tf_op jit(solution)/shard_map/transpose | solution.py:258
  (1 shorter events, 0.0 us)
Async XLA Ops:
  7.6 10.0 %collective-permute-start.2 = (bf16[128,1280]{1,0:T(8,128)(2,1)}, bf16[128,1280]{1,0:T(8,128)(2,1)S(1)}, u32[]{:S(2)}, u32[]{:S(2)}) collective-permute-start(bf16[128,1280]{1,0:T(8,128)(2,1)} %get-tuple-element.13.refs_0_), channel_id=1, source_target_pairs={{0,8},{1,9},{2,10},{3,11},{4,12},{5,13},{6,14},{7,15},{8,0},{9,1},... | collective-permute-start | bytes 983048 | tf_op jit(solution)/shard_map/ppermute | solution.py:227
  9.7 10.7 %collective-permute-start = (bf16[128,1280]{1,0:T(8,128)(2,1)}, bf16[128,1280]{1,0:T(8,128)(2,1)S(1)}, u32[]{:S(2)}, u32[]{:S(2)}) collective-permute-start(bf16[128,1280]{1,0:T(8,128)(2,1)} %get-tuple-element.13.refs_0_), channel_id=1, source_target_pairs={{0,2},{1,3},{2,4},{3,5},{4,6},{5,7},{6,0},{7,1},{8,10},{9,11},{10,... | collective-permute-start | bytes 983048 | tf_op jit(solution)/shard_map/ppermute | solution.py:227
  11.2 10.9 %collective-permute-start.3 = (bf16[128,1280]{1,0:T(8,128)(2,1)}, bf16[128,1280]{1,0:T(8,128)(2,1)S(1)}, u32[]{:S(2)}, u32[]{:S(2)}) collective-permute-start(bf16[128,1280]{1,0:T(8,128)(2,1)} %get-tuple-element.13.refs_0_), channel_id=1, source_target_pairs={{0,6},{1,7},{2,0},{3,1},{4,2},{5,3},{6,4},{7,5},{8,14},{9,15},{10,... | collective-permute-start | bytes 983048 | tf_op jit(solution)/shard_map/ppermute | solution.py:227
  17.6 9.7 %collective-permute-start.5 = (bf16[128,1280]{1,0:T(8,128)(2,1)S(1)}, bf16[128,1280]{1,0:T(8,128)(2,1)S(1)}, u32[]{:S(2)}, u32[]{:S(2)}) collective-permute-start(bf16[128,1280]{1,0:T(8,128)(2,1)S(1)} %collective-permute-done.2.refs_1_), channel_id=1, source_target_pairs={{0,6},{1,7},{2,0},{3,1},{4,2},{5,3},{6,4},{7,5},{8,14},{9,15},{10,... | collective-permute-start | bytes 983048 | tf_op jit(solution)/shard_map/ppermute | solution.py:227
  20.4 8.5 %collective-permute-start.4 = (bf16[128,1280]{1,0:T(8,128)(2,1)S(1)}, bf16[128,1280]{1,0:T(8,128)(2,1)S(1)}, u32[]{:S(2)}, u32[]{:S(2)}) collective-permute-start(bf16[128,1280]{1,0:T(8,128)(2,1)S(1)} %collective-permute-done.refs_2_), channel_id=1, source_target_pairs={{0,8},{1,9},{2,10},{3,11},{4,12},{5,13},{6,14},{7,15},{8,0},{9,1},... | collective-permute-start | bytes 983048 | tf_op jit(solution)/shard_map/ppermute | solution.py:227
  22.1 11.8 %collective-permute-start.1 = (bf16[128,1280]{1,0:T(8,128)(2,1)S(1)}, bf16[128,1280]{1,0:T(8,128)(2,1)S(1)}, u32[]{:S(2)}, u32[]{:S(2)}) collective-permute-start(bf16[128,1280]{1,0:T(8,128)(2,1)S(1)} %collective-permute-done.refs_2_), channel_id=1, source_target_pairs={{0,2},{1,3},{2,4},{3,5},{4,6},{5,7},{6,0},{7,1},{8,10},{9,11},{10,... | collective-permute-start | bytes 983048 | tf_op jit(solution)/shard_map/ppermute | solution.py:227
  22.1 20.3 %collective-permute-start.7 = (bf16[128,1280]{1,0:T(8,128)(2,1)}, bf16[128,1280]{1,0:T(8,128)(2,1)S(1)}, u32[]{:S(2)}, u32[]{:S(2)}) collective-permute-start(bf16[128,1280]{1,0:T(8,128)(2,1)} %get-tuple-element.13.refs_0_), channel_id=1, source_target_pairs={{0,1},{1,0},{2,3},{3,2},{4,5},{5,4},{6,7},{7,6},{8,9},{9,8},{10,11... | collective-permute-start | bytes 983048 | tf_op jit(solution)/shard_map/ppermute | solution.py:227
  22.1 20.3 %collective-permute-start.10 = (bf16[128,1280]{1,0:T(8,128)(2,1)S(1)}, bf16[128,1280]{1,0:T(8,128)(2,1)}, u32[]{:S(2)}, u32[]{:S(2)}) collective-permute-start(bf16[128,1280]{1,0:T(8,128)(2,1)S(1)} %collective-permute-done.3.refs_3_), channel_id=1, source_target_pairs={{0,1},{1,0},{2,3},{3,2},{4,5},{5,4},{6,7},{7,6},{8,9},{9,8},{10,11... | collective-permute-start | bytes 983048 | tf_op jit(solution)/shard_map/ppermute | solution.py:227
  27.3 15.6 %collective-permute-start.8 = (bf16[128,1280]{1,0:T(8,128)(2,1)S(1)}, bf16[128,1280]{1,0:T(8,128)(2,1)}, u32[]{:S(2)}, u32[]{:S(2)}) collective-permute-start(bf16[128,1280]{1,0:T(8,128)(2,1)S(1)} %collective-permute-done.2.refs_1_), channel_id=1, source_target_pairs={{0,1},{1,0},{2,3},{3,2},{4,5},{5,4},{6,7},{7,6},{8,9},{9,8},{10,11... | collective-permute-start | bytes 983048 | tf_op jit(solution)/shard_map/ppermute | solution.py:227
  28.9 14.2 %collective-permute-start.6 = (bf16[128,1280]{1,0:T(8,128)(2,1)S(1)}, bf16[128,1280]{1,0:T(8,128)(2,1)}, u32[]{:S(2)}, u32[]{:S(2)}) collective-permute-start(bf16[128,1280]{1,0:T(8,128)(2,1)S(1)} %collective-permute-done.5.refs_5_), channel_id=1, source_target_pairs={{0,6},{1,7},{2,0},{3,1},{4,2},{5,3},{6,4},{7,5},{8,14},{9,15},{10,... | collective-permute-start | bytes 983048 | tf_op jit(solution)/shard_map/ppermute | solution.py:227
  30.3 12.0 %all-to-all-start = ((bf16[16,80,128]{2,1,0:T(8,128)(2,1)}), bf16[16,80,128]{2,1,0:T(8,128)(2,1)S(1)}, u32[]{:S(2)}, u32[]{:S(2)}) async-start(bf16[16,80,128]{2,1,0:T(8,128)(2,1)} %get-tuple-element.14), calls=%async_computation | async-start | bytes 655360 | tf_op jit(solution)/shard_map/all_to_all | solution.py:212
  33.9 9.6 %collective-permute-start.9 = (bf16[128,1280]{1,0:T(8,128)(2,1)S(1)}, bf16[128,1280]{1,0:T(8,128)(2,1)}, u32[]{:S(2)}, u32[]{:S(2)}) collective-permute-start(bf16[128,1280]{1,0:T(8,128)(2,1)S(1)} %collective-permute-done.refs_2_), channel_id=1, source_target_pairs={{0,1},{1,0},{2,3},{3,2},{4,5},{5,4},{6,7},{7,6},{8,9},{9,8},{10,11... | collective-permute-start | bytes 983048 | tf_op jit(solution)/shard_map/ppermute | solution.py:227
  42.4 2.2 %collective-permute-start.12 = (bf16[128,1280]{1,0:T(8,128)(2,1)S(1)}, bf16[128,1280]{1,0:T(8,128)(2,1)}, u32[]{:S(2)}, u32[]{:S(2)}) collective-permute-start(bf16[128,1280]{1,0:T(8,128)(2,1)S(1)} %collective-permute-done.5.refs_5_), channel_id=1, source_target_pairs={{0,1},{1,0},{2,3},{3,2},{4,5},{5,4},{6,7},{7,6},{8,9},{9,8},{10,11... | collective-permute-start | bytes 983048 | tf_op jit(solution)/shard_map/ppermute | solution.py:227
  42.4 2.2 %collective-permute-start.11 = (bf16[128,1280]{1,0:T(8,128)(2,1)S(1)}, bf16[128,1280]{1,0:T(8,128)(2,1)}, u32[]{:S(2)}, u32[]{:S(2)}) collective-permute-start(bf16[128,1280]{1,0:T(8,128)(2,1)S(1)} %collective-permute-done.4.refs_4_), channel_id=1, source_target_pairs={{0,1},{1,0},{2,3},{3,2},{4,5},{5,4},{6,7},{7,6},{8,9},{9,8},{10,11... | collective-permute-start | bytes 983048 | tf_op jit(solution)/shard_map/ppermute | solution.py:227
  42.9 2.6 %collective-permute-start.13 = (bf16[128,1280]{1,0:T(8,128)(2,1)S(1)}, bf16[128,1280]{1,0:T(8,128)(2,1)}, u32[]{:S(2)}, u32[]{:S(2)}) collective-permute-start(bf16[128,1280]{1,0:T(8,128)(2,1)S(1)} %collective-permute-done.1.refs_6_), channel_id=1, source_target_pairs={{0,1},{1,0},{2,3},{3,2},{4,5},{5,4},{6,7},{7,6},{8,9},{9,8},{10,11... | collective-permute-start | bytes 983048 | tf_op jit(solution)/shard_map/ppermute | solution.py:227
  43.0 2.8 %collective-permute-start.14 = (bf16[128,1280]{1,0:T(8,128)(2,1)}, bf16[128,1280]{1,0:T(8,128)(2,1)}, u32[]{:S(2)}, u32[]{:S(2)}) collective-permute-start(bf16[128,1280]{1,0:T(8,128)(2,1)} %collective-permute-done.6.refs_7_), channel_id=1, source_target_pairs={{0,1},{1,0},{2,3},{3,2},{4,5},{5,4},{6,7},{7,6},{8,9},{9,8},{10,11... | collective-permute-start | bytes 983048 | tf_op jit(solution)/shard_map/ppermute | solution.py:227
  45.8 1.0 copy-start
